TPU v7x, 32 devices: a whole 2x2x4 slice. The times are simulated.
32 devices in a mesh: dp: 16 (over z, x, core), step: 2 (over y).
Axes of the slice: x: 2, y: 2, z: 4, core: 2. Of those that a mesh axis runs over, the one named last changes fastest.
Arguments:
- tokens: bfloat16 [16, 512, 1024], P('dp'), may hold values from -6 to 6
- cotangent: bfloat16 [16, 512, 1024], P('dp'), may hold values from -6 to 6
- domains: int32 [16], replicated, may hold values from 0 to 7
- doc_ids: int32 [16, 512], P('dp'), may hold values from 0 to 3, never falling along the last dimension, each value on 1 to 256 neighbouring positions
- norm_gain: float32 [1024], replicated, may hold values from 0.5 to 1.5
- w_query: bfloat16 [1024, 1024], P('dp', 'step'), may hold values from -0.1875 to 0.1875
- w_outgate: bfloat16 [1024, 1024], P('dp', 'step'), may hold values from -0.1875 to 0.1875
- w_key: bfloat16 [2, 1024, 1024], P('step', 'dp'), may hold values from -0.1875 to 0.1875
- w_value: bfloat16 [2, 1024, 1024], P('step', 'dp'), may hold values from -0.1875 to 0.1875
- w_beta: bfloat16 [2, 1024, 8], P('step', 'dp'), may hold values from -0.1875 to 0.1875
- w_alpha: bfloat16 [1024, 8], P('dp', 'step'), may hold values from -0.1875 to 0.1875
- decay_log: float32 [8], P('step'), may hold values from -4 to 0.5
- decay_bias: float32 [8], P('step'), may hold values from -4 to -1
- conv_query: float32 [4, 1024], P(None, 'step'), may hold values from -0.6 to 0.6
- conv_key: float32 [2, 4, 1024], P('step'), may hold values from -0.6 to 0.6
- conv_value: float32 [2, 4, 1024], P('step'), may hold values from -0.6 to 0.6
- mix_gain: float32 [128], replicated, may hold values from 0.5 to 1.5
- w_out: bfloat16 [1024, 1024], P('step', 'dp'), may hold values from -0.25 to 0.25
- ffn_gain: float32 [1024], replicated, may hold values from 0.5 to 1.5
- w_gate: bfloat16 [1024, 2816], P('dp', 'step'), may hold values from -0.1875 to 0.1875
- w_up: bfloat16 [1024, 2816], P('dp', 'step'), may hold values from -0.1875 to 0.1875
- w_down: bfloat16 [2816, 1024], P('step', 'dp'), may hold values from -0.15625 to 0.15625
Outputs:
- output: bfloat16 [16, 512, 1024], P('dp')
- input_grad: bfloat16 [16, 512, 1024], P('dp')
- grad_norm_gain: float32 [1024], replicated
- grad_query: float32 [1024, 1024], P('dp', 'step')
- grad_outgate: float32 [1024, 1024], P('dp', 'step')
- grad_key: float32 [2, 1024, 1024], P('step', 'dp')
- grad_value: float32 [2, 1024, 1024], P('step', 'dp')
- grad_beta: float32 [2, 1024, 8], P('step', 'dp')
- grad_alpha: float32 [1024, 8], P('dp', 'step')
- grad_decay_log: float32 [8], P('step')
- grad_decay_bias: float32 [8], P('step')
- grad_conv_query: float32 [4, 1024], P(None, 'step')
- grad_conv_key: float32 [2, 4, 1024], P('step')
- grad_conv_value: float32 [2, 4, 1024], P('step')
- grad_mix_gain: float32 [128], replicated
- grad_out: float32 [1024, 1024], P('step', 'dp')
- grad_ffn_gain: float32 [1024], replicated
- grad_gate: float32 [1024, 2816], P('dp', 'step')
- grad_up: float32 [1024, 2816], P('dp', 'step')
- grad_down: float32 [2816, 1024], P('step', 'dp')
Inputs may be any that keep to these rules, and one draw needn't show every extreme that they name: `doc_ids`: document numbers within a row start at 0 and never fall.
All inputs are finite; a program needn't handle non-finite values.
Results may differ from a plain program's by a relative error of at most 0.018.
Values may be sent and summed in bfloat16 or wider, within the bound.
A program may use at most 192 MiB of HBM per device.

v0:
```python
import jax
import jax.numpy as jnp
from jax import lax
from jax.sharding import PartitionSpec as P

DK = 128
STRETCH = 64
GROUPS = 8


PRECISE = lax.Precision.HIGHEST


def matmul(first, second):
    return jnp.dot(first, second, precision=PRECISE)


def plain_product(first, second):
    return jnp.dot(first, second, preferred_element_type=jnp.float32)


def left_product(first, second):
    return lax.dot_general(
        first, second, (((0,), (0,)), ((), ())), preferred_element_type=jnp.float32
    )


def right_product(first, second):
    return lax.dot_general(
        first, second, (((1,), (1,)), ((), ())), preferred_element_type=jnp.float32
    )


def rms_scale(values, scales):
    return values * lax.rsqrt(jnp.mean(values * values, axis=-1, keepdims=True) + 1e-06) * scales


def unit_rows(values):
    return values * lax.rsqrt(jnp.sum(values * values, axis=-1, keepdims=True) + 1e-06)


def silu_grad(values):
    sigmoid = jax.nn.sigmoid(values)
    return sigmoid * (1.0 + values * (1.0 - sigmoid))


def short_conv(signal, kernel, doc_ids):
    seq_len = signal.shape[0]
    summed = signal * kernel[0]
    for offset in range(1, kernel.shape[0]):
        shifted = jnp.pad(signal, ((offset, 0), (0, 0)))[:seq_len]
        shifted_docs = jnp.pad(doc_ids, (offset, 0), constant_values=-1)[:seq_len]
        same_doc = (shifted_docs == doc_ids).astype(jnp.float32)[:, None]
        summed = summed + shifted * same_doc * kernel[offset]
    return summed


def block_pass(memory, pieces):
    query_block, key_block, value_block, beta_block, decay_block, doc_block, prior_doc = pieces
    block_len = key_block.shape[0]
    cumulative = jnp.cumsum(decay_block)
    row_pos = lax.broadcasted_iota(jnp.int32, (block_len, block_len), 0)
    col_pos = lax.broadcasted_iota(jnp.int32, (block_len, block_len), 1)
    inside = (row_pos >= col_pos) & (doc_block[:, None] == doc_block[None, :])
    decay_mat = jnp.where(
        inside, jnp.exp(jnp.where(inside, cumulative[:, None] - cumulative[None, :], 0.0)), 0.0
    )
    carried = jnp.where(doc_block == prior_doc, jnp.exp(cumulative), 0.0)
    strict = jnp.where(row_pos > col_pos, decay_mat * matmul(key_block, key_block.T), 0.0)
    system = jnp.eye(block_len, dtype=jnp.float32) + beta_block[:, None] * strict
    target = beta_block[:, None] * (value_block - carried[:, None] * matmul(key_block, memory))
    pseudo = jax.scipy.linalg.solve_triangular(system, target, lower=True, unit_diagonal=True)
    query_decay = decay_mat[1::2]
    query_carry = carried[1::2]
    result = query_carry[:, None] * matmul(query_block, memory) + matmul(
        query_decay * matmul(query_block, key_block.T), pseudo
    )
    updated = carried[-1] * memory + matmul(key_block.T, decay_mat[-1][:, None] * pseudo)
    return (updated, result)


def head_sequence(queries, keys, values, betas, decays, doc_ids):
    seq_len = queries.shape[0]
    blocks = seq_len // STRETCH
    span_len = 2 * STRETCH
    key_line = jnp.transpose(keys, (1, 0, 2)).reshape(blocks, span_len, keys.shape[-1])
    value_line = jnp.transpose(values, (1, 0, 2)).reshape(blocks, span_len, values.shape[-1])
    beta_line = jnp.transpose(betas).reshape(blocks, span_len)
    decay_line = jnp.stack([decays, jnp.zeros_like(decays)], axis=1).reshape(blocks, span_len)
    doc_line = jnp.repeat(doc_ids, 2).reshape(blocks, span_len)
    prior_docs = jnp.concatenate([jnp.full((1,), -1, doc_ids.dtype), doc_line[:-1, -1]])
    initial = jnp.zeros((keys.shape[-1], values.shape[-1]), queries.dtype)
    last_state, outputs = lax.scan(
        jax.checkpoint(block_pass),
        initial,
        (
            queries.reshape(blocks, STRETCH, -1),
            key_line,
            value_line,
            beta_line,
            decay_line,
            doc_line,
            prior_docs,
        ),
    )
    return outputs.reshape(seq_len, -1)


def gated_norm(mixed, gate_pre, mix_gain):
    seq_len = mixed.shape[0]
    gates = jax.nn.silu(gate_pre.reshape(mixed.shape))
    scaled = mixed * lax.rsqrt(jnp.mean(mixed * mixed, axis=-1, keepdims=True) + 1e-05)
    return (scaled * mix_gain * gates).reshape(seq_len, -1)


def query_inputs(query_pre, conv_query, doc_ids):
    seq_len = query_pre.shape[0]
    activated = jax.nn.silu(short_conv(query_pre, conv_query, doc_ids))
    return unit_rows(activated.reshape(seq_len, -1, DK)) * DK ** (-0.5)


def step_inputs(key_pre, value_pre, conv_key, conv_value, doc_ids):
    seq_len = key_pre.shape[0]
    activated = jax.nn.silu(short_conv(key_pre, conv_key, doc_ids))
    keys = unit_rows(activated.reshape(seq_len, -1, DK)).reshape(seq_len, -1)
    values = jax.nn.silu(short_conv(value_pre, conv_value, doc_ids))
    return (keys, values)


def decay_rates(alpha_pre, decay_log, decay_bias):
    return -jnp.exp(decay_log) * jax.nn.softplus(alpha_pre + decay_bias)


def per_device(
    tokens,
    cotangent,
    domains,
    doc_ids,
    norm_gain,
    w_query,
    w_outgate,
    w_key,
    w_value,
    w_beta,
    w_alpha,
    decay_log,
    decay_bias,
    conv_query,
    conv_key,
    conv_value,
    mix_gain,
    w_out,
    ffn_gain,
    w_gate,
    w_up,
    w_down,
):
    row_total = domains.shape[0]
    group_ids = lax.broadcasted_iota(jnp.int32, (row_total, GROUPS), 1)
    member = (domains[:, None] == group_ids).astype(jnp.float32)
    group_sizes = jnp.sum(member, axis=0)
    row_sizes = jnp.sum(member * group_sizes[None, :], axis=1)
    row_weights = 2.0 / (1.0 + row_sizes * (GROUPS / row_total))
    own_row = (lax.broadcasted_iota(jnp.int32, (row_total,), 0) == lax.axis_index("dp")).astype(
        jnp.float32
    )
    weight_here = jnp.sum(own_row * row_weights)
    (
        whole_query,
        whole_outgate,
        whole_key,
        whole_value,
        whole_beta,
        whole_alpha,
        whole_out,
        whole_gate,
        whole_up,
        whole_down,
    ) = (
        lax.all_gather(w_query, "dp", axis=0, tiled=True),
        lax.all_gather(w_outgate, "dp", axis=0, tiled=True),
        lax.all_gather(w_key, "dp", axis=1, tiled=True),
        lax.all_gather(w_value, "dp", axis=1, tiled=True),
        lax.all_gather(w_beta, "dp", axis=1, tiled=True),
        lax.all_gather(w_alpha, "dp", axis=0, tiled=True),
        lax.all_gather(w_out, "dp", axis=1, tiled=True),
        lax.all_gather(w_gate, "dp", axis=0, tiled=True),
        lax.all_gather(w_up, "dp", axis=0, tiled=True),
        lax.all_gather(w_down, "dp", axis=1, tiled=True),
    )
    inputs = tokens[0].astype(jnp.float32)
    docs_here = doc_ids[0]
    seq_len = inputs.shape[0]
    halves = lax.axis_size("step")
    normed_f, pull_first = jax.vjp(rms_scale, inputs, norm_gain)
    normed = normed_f.astype(jnp.bfloat16)
    query_pre = plain_product(normed, whole_query)
    gate_pre = plain_product(normed, whole_outgate)
    alpha_pre = plain_product(normed, whole_alpha)
    key_pre = plain_product(normed, whole_key[0])
    value_pre = plain_product(normed, whole_value[0])
    beta_pre = plain_product(normed, whole_beta[0])

    def prepare(
        query_in,
        key_in,
        value_in,
        beta_in,
        alpha_in,
        query_kernel,
        key_kernel,
        value_kernel,
        log_rates,
        rate_bias,
    ):
        queries = query_inputs(query_in, query_kernel, docs_here)
        keys, values = step_inputs(key_in, value_in, key_kernel, value_kernel, docs_here)
        betas = 2.0 * jax.nn.sigmoid(beta_in)
        decays = decay_rates(alpha_in, log_rates, rate_bias)
        return (queries, keys, values, betas, decays)

    (queries, keys, values, betas, decays), pull_prepare = jax.vjp(
        prepare,
        query_pre,
        key_pre,
        value_pre,
        beta_pre,
        alpha_pre,
        conv_query,
        conv_key[0],
        conv_value[0],
        decay_log,
        decay_bias,
    )
    key_send = keys.astype(jnp.bfloat16).reshape(1, seq_len, halves, -1)
    value_send = values.astype(jnp.bfloat16).reshape(1, seq_len, halves, -1)
    beta_send = betas.astype(jnp.bfloat16).reshape(1, seq_len, halves, -1)
    key_recv, value_recv, beta_recv = (
        lax.all_to_all(key_send, "step", split_axis=2, concat_axis=0, tiled=True),
        lax.all_to_all(value_send, "step", split_axis=2, concat_axis=0, tiled=True),
        lax.all_to_all(beta_send, "step", split_axis=2, concat_axis=0, tiled=True),
    )
    step_count = key_recv.shape[0]

    def mixing(query_set, key_set, value_set, beta_set, decay_set, gate_set, gain_local):

        def one_head(query_head, key_head, value_head, beta_head, decay_head):
            return head_sequence(query_head, key_head, value_head, beta_head, decay_head, docs_here)

        mixed = jax.vmap(one_head, in_axes=(1, 2, 2, 2, 1), out_axes=1)(
            query_set, key_set, value_set, beta_set, decay_set
        )
        return gated_norm(mixed, gate_set, gain_local)

    gated_f, pull_mixing = jax.vjp(
        mixing,
        queries,
        key_recv.astype(jnp.float32).reshape(step_count, seq_len, -1, DK),
        value_recv.astype(jnp.float32).reshape(step_count, seq_len, -1, DK),
        beta_recv.astype(jnp.float32).reshape(step_count, seq_len, -1),
        decays,
        gate_pre,
        mix_gain,
    )
    gated_low = gated_f.astype(jnp.bfloat16)
    attention = lax.psum(plain_product(gated_low, whole_out).astype(jnp.bfloat16), "step").astype(
        jnp.float32
    )
    middle = inputs + attention
    normed_ffn_f, pull_second = jax.vjp(rms_scale, middle, ffn_gain)
    normed_ffn = normed_ffn_f.astype(jnp.bfloat16)
    gate_in = plain_product(normed_ffn, whole_gate)
    up_in = plain_product(normed_ffn, whole_up)
    hidden = (jax.nn.silu(gate_in) * up_in).astype(jnp.bfloat16)
    ffn_out = lax.psum(plain_product(hidden, whole_down).astype(jnp.bfloat16), "step").astype(
        jnp.float32
    )
    output = (middle + ffn_out).astype(jnp.bfloat16)[None]
    (
        whole_query,
        whole_outgate,
        whole_key,
        whole_value,
        whole_beta,
        whole_alpha,
        whole_out,
        whole_gate,
        whole_up,
        whole_down,
    ) = (
        lax.all_gather(w_query, "dp", axis=0, tiled=True),
        lax.all_gather(w_outgate, "dp", axis=0, tiled=True),
        lax.all_gather(w_key, "dp", axis=1, tiled=True),
        lax.all_gather(w_value, "dp", axis=1, tiled=True),
        lax.all_gather(w_beta, "dp", axis=1, tiled=True),
        lax.all_gather(w_alpha, "dp", axis=0, tiled=True),
        lax.all_gather(w_out, "dp", axis=1, tiled=True),
        lax.all_gather(w_gate, "dp", axis=0, tiled=True),
        lax.all_gather(w_up, "dp", axis=0, tiled=True),
        lax.all_gather(w_down, "dp", axis=1, tiled=True),
    )
    seed = cotangent[0].astype(jnp.float32) * weight_here
    seed_low = seed.astype(jnp.bfloat16)
    grad_down = left_product(hidden, seed_low)
    hidden_back = right_product(seed_low, whole_down)
    gate_back = (hidden_back * up_in * silu_grad(gate_in)).astype(jnp.bfloat16)
    up_back = (hidden_back * jax.nn.silu(gate_in)).astype(jnp.bfloat16)
    grad_gate = left_product(normed_ffn, gate_back)
    grad_up = left_product(normed_ffn, up_back)
    ffn_in_back = lax.psum(
        (right_product(gate_back, whole_gate) + right_product(up_back, whole_up)).astype(
            jnp.bfloat16
        ),
        "step",
    ).astype(jnp.float32)
    middle_norm_back, grad_ffn_gain = pull_second(ffn_in_back)
    middle_back = seed + middle_norm_back
    attn_back = middle_back.astype(jnp.bfloat16)
    grad_out = left_product(gated_low, attn_back)
    gated_back = right_product(attn_back, whole_out)
    query_back, key_back, value_back, beta_back, decay_back, gate_pre_back, mix_gain_part = (
        pull_mixing(gated_back)
    )
    key_home, value_home, beta_home = (
        lax.all_to_all(
            key_back.astype(jnp.bfloat16).reshape(step_count, seq_len, 1, -1),
            "step",
            split_axis=0,
            concat_axis=2,
            tiled=True,
        ),
        lax.all_to_all(
            value_back.astype(jnp.bfloat16).reshape(step_count, seq_len, 1, -1),
            "step",
            split_axis=0,
            concat_axis=2,
            tiled=True,
        ),
        lax.all_to_all(
            beta_back.astype(jnp.bfloat16).reshape(step_count, seq_len, 1, -1),
            "step",
            split_axis=0,
            concat_axis=2,
            tiled=True,
        ),
    )
    prepare_cot = (
        query_back,
        key_home.astype(jnp.float32).reshape(seq_len, -1),
        value_home.astype(jnp.float32).reshape(seq_len, -1),
        beta_home.astype(jnp.float32).reshape(seq_len, -1),
        decay_back,
    )
    (
        query_pre_back,
        key_pre_back,
        value_pre_back,
        beta_pre_back,
        alpha_pre_back,
        grad_conv_query,
        grad_conv_key,
        grad_conv_value,
        grad_decay_log,
        grad_decay_bias,
    ) = pull_prepare(prepare_cot)
    query_low = query_pre_back.astype(jnp.bfloat16)
    gate_low = gate_pre_back.astype(jnp.bfloat16)
    alpha_low = alpha_pre_back.astype(jnp.bfloat16)
    key_low = key_pre_back.astype(jnp.bfloat16)
    value_low = value_pre_back.astype(jnp.bfloat16)
    beta_low = beta_pre_back.astype(jnp.bfloat16)
    grad_query = left_product(normed, query_low)
    grad_outgate = left_product(normed, gate_low)
    grad_alpha = left_product(normed, alpha_low)
    grad_key = left_product(normed, key_low)
    grad_value = left_product(normed, value_low)
    grad_beta = left_product(normed, beta_low)
    front_part = (
        right_product(query_low, whole_query)
        + right_product(gate_low, whole_outgate)
        + right_product(alpha_low, whole_alpha)
    )
    front_part = (
        front_part
        + right_product(key_low, whole_key[0])
        + right_product(value_low, whole_value[0])
        + right_product(beta_low, whole_beta[0])
    )
    normed_back, mix_gain_step = (
        lax.psum(front_part.astype(jnp.bfloat16), "step").astype(jnp.float32),
        lax.psum(mix_gain_part.astype(jnp.bfloat16), "step").astype(jnp.float32),
    )
    input_back, grad_norm_gain = pull_first(normed_back)
    input_grad = (middle_back + input_back).astype(jnp.bfloat16)[None]
    (
        sum_query,
        sum_outgate,
        sum_key,
        sum_value,
        sum_beta,
        sum_alpha,
        sum_out,
        sum_gate,
        sum_up,
        sum_down,
    ) = (
        lax.psum_scatter(grad_query, "dp", scatter_dimension=0, tiled=True),
        lax.psum_scatter(grad_outgate, "dp", scatter_dimension=0, tiled=True),
        lax.psum_scatter(grad_key[None], "dp", scatter_dimension=1, tiled=True),
        lax.psum_scatter(grad_value[None], "dp", scatter_dimension=1, tiled=True),
        lax.psum_scatter(grad_beta[None], "dp", scatter_dimension=1, tiled=True),
        lax.psum_scatter(grad_alpha, "dp", scatter_dimension=0, tiled=True),
        lax.psum_scatter(grad_out, "dp", scatter_dimension=1, tiled=True),
        lax.psum_scatter(grad_gate, "dp", scatter_dimension=0, tiled=True),
        lax.psum_scatter(grad_up, "dp", scatter_dimension=0, tiled=True),
        lax.psum_scatter(grad_down, "dp", scatter_dimension=1, tiled=True),
    )
    (
        sum_norm_gain,
        sum_decay_log,
        sum_decay_bias,
        sum_conv_query,
        sum_conv_key,
        sum_conv_value,
        sum_mix_gain,
        sum_ffn_gain,
    ) = lax.psum(
        (
            grad_norm_gain,
            grad_decay_log,
            grad_decay_bias,
            grad_conv_query,
            grad_conv_key[None],
            grad_conv_value[None],
            mix_gain_step,
            grad_ffn_gain,
        ),
        "dp",
    )
    return (
        output,
        input_grad,
        sum_norm_gain,
        sum_query,
        sum_outgate,
        sum_key,
        sum_value,
        sum_beta,
        sum_alpha,
        sum_decay_log,
        sum_decay_bias,
        sum_conv_query,
        sum_conv_key,
        sum_conv_value,
        sum_mix_gain,
        sum_out,
        sum_ffn_gain,
        sum_gate,
        sum_up,
        sum_down,
    )


def solution(mesh):
    return jax.shard_map(
        per_device,
        mesh=mesh,
        in_specs=(
            P("dp", None, None),
            P("dp", None, None),
            P(),
            P("dp", None),
            P(),
            P("dp", "step"),
            P("dp", "step"),
            P("step", "dp", None),
            P("step", "dp", None),
            P("step", "dp", None),
            P("dp", "step"),
            P("step"),
            P("step"),
            P(None, "step"),
            P("step", None, None),
            P("step", None, None),
            P(),
            P("step", "dp"),
            P(),
            P("dp", "step"),
            P("dp", "step"),
            P("step", "dp"),
        ),
        out_specs=(
            P("dp", None, None),
            P("dp", None, None),
            P(),
            P("dp", "step"),
            P("dp", "step"),
            P("step", "dp", None),
            P("step", "dp", None),
            P("step", "dp", None),
            P("dp", "step"),
            P("step"),
            P("step"),
            P(None, "step"),
            P("step", None, None),
            P("step", None, None),
            P(),
            P("step", "dp"),
            P(),
            P("dp", "step"),
            P("dp", "step"),
            P("step", "dp"),
        ),
        check_vma=False,
    )
```

profile of v0, /device:TPU:0, one launch (start us, length us, event | category | flops | bytes accessed | tf_op | source)
XLA Modules:
  0.0 2227.1 jit_solution(2964807904982975029)
XLA Ops:
  10.9 24.8 %all_gather.42 = bf16[1,1024,8]{2,0,1:T(2,128)(2,1)S(1)} all-gather(bf16[1,64,8]{2,0,1:T(2,128)(2,1)S(1)} %copy.627), channel_id=1, replica_groups=mesh['dp'=16,'step'=2] {'dp'}, dimensions={1}, use_global_device_ids=true | all-gather | bytes 17408 | tf_op jit(solution)/shard_map/all_gather | solution.py:184
  37.9 3.2 all-to-all-start.1
  43.2 17.5 all-gather
  67.9 25.6 %all-gather.12.cloned.1.call-done = bf16[1,1024,1024]{2,1,0:T(8,128)(2,1)} async-done(((bf16[1,64,1024]{2,1,0:T(8,128)(2,1)}), bf16[1,1024,1024]{2,1,0:T(8,128)(2,1)}) %all-gather.12.cloned.1.call-update) | async-done | bytes 2097168 | tf_op jit(solution)/shard_map/all_gather | solution.py:183
  93.5 4.3 fusion.144
  97.8 38.1 %all-gather.10.cloned.1.call-done = bf16[1,1024,1024]{2,1,0:T(8,128)(2,1)} async-done(((bf16[1,64,1024]{2,1,0:T(8,128)(2,1)}), bf16[1,1024,1024]{2,1,0:T(8,128)(2,1)}) %all-gather.10.cloned.1.call-update) | async-done | bytes 2097168 | tf_op jit(solution)/shard_map/all_gather | solution.py:182
  139.0 4.5 multiply_convert_fusion.4
  156.1 3.6 all-to-all-start
  159.7 4.5 fusion.182
  174.0 4.6 all-to-all-start.2
  186.3 3.1 copy.638
  196.1 3.2 copy.640
  199.4 419.5 %while.42 = (s32[]{:T(128)}, f32[4,128,128]{2,1,0:T(8,128)S(1)}, f32[8,4,64,128]{3,2,0,1:T(8,128)S(1)}, f32[8,4,128,128]{3,2,1,0:T(8,128)}, s32[8,128]{1,0:T(8,1...) while((s32[]{:T(128)}, f32[4,128,128]{2,1,0:T(8,128)S(1)}, ...), condition=%wide.region_5.7_spmd.clone, body=%wide.region_3.6_spmd.clone.sunk | while | flops 555385088 | bytes 6696938 | solution.py:93
  204.3 39.3 %custom-call.17 = f32[4,1,128,128]{2,3,1,0:T(8,128)S(1)} custom-call(f32[4,1,128,128]{3,2,1,0:T(8,128)S(1)} %fusion.419), custom_call_target="InvertDiagBlocksLowerTriangular" | custom-call | tf_op jit(solution)/shard_map/jvp(vmap())/while/body/eval_jaxpr/jit(_solve_triangular)/triangular_solve/custom-call.1 | solution.py:72
  256.7 39.3 %custom-call.17 = f32[4,1,128,128]{2,3,1,0:T(8,128)S(1)} custom-call(f32[4,1,128,128]{3,2,1,0:T(8,128)S(1)} %fusion.419), custom_call_target="InvertDiagBlocksLowerTriangular" | custom-call | tf_op jit(solution)/shard_map/jvp(vmap())/while/body/eval_jaxpr/jit(_solve_triangular)/triangular_solve/custom-call.1 | solution.py:72
  309.1 39.3 %custom-call.17 = f32[4,1,128,128]{2,3,1,0:T(8,128)S(1)} custom-call(f32[4,1,128,128]{3,2,1,0:T(8,128)S(1)} %fusion.419), custom_call_target="InvertDiagBlocksLowerTriangular" | custom-call | tf_op jit(solution)/shard_map/jvp(vmap())/while/body/eval_jaxpr/jit(_solve_triangular)/triangular_solve/custom-call.1 | solution.py:72
  361.6 39.3 %custom-call.17 = f32[4,1,128,128]{2,3,1,0:T(8,128)S(1)} custom-call(f32[4,1,128,128]{3,2,1,0:T(8,128)S(1)} %fusion.419), custom_call_target="InvertDiagBlocksLowerTriangular" | custom-call | tf_op jit(solution)/shard_map/jvp(vmap())/while/body/eval_jaxpr/jit(_solve_triangular)/triangular_solve/custom-call.1 | solution.py:72
  414.0 39.3 %custom-call.17 = f32[4,1,128,128]{2,3,1,0:T(8,128)S(1)} custom-call(f32[4,1,128,128]{3,2,1,0:T(8,128)S(1)} %fusion.419), custom_call_target="InvertDiagBlocksLowerTriangular" | custom-call | tf_op jit(solution)/shard_map/jvp(vmap())/while/body/eval_jaxpr/jit(_solve_triangular)/triangular_solve/custom-call.1 | solution.py:72
  466.4 39.3 %custom-call.17 = f32[4,1,128,128]{2,3,1,0:T(8,128)S(1)} custom-call(f32[4,1,128,128]{3,2,1,0:T(8,128)S(1)} %fusion.419), custom_call_target="InvertDiagBlocksLowerTriangular" | custom-call | tf_op jit(solution)/shard_map/jvp(vmap())/while/body/eval_jaxpr/jit(_solve_triangular)/triangular_solve/custom-call.1 | solution.py:72
  518.9 39.3 %custom-call.17 = f32[4,1,128,128]{2,3,1,0:T(8,128)S(1)} custom-call(f32[4,1,128,128]{3,2,1,0:T(8,128)S(1)} %fusion.419), custom_call_target="InvertDiagBlocksLowerTriangular" | custom-call | tf_op jit(solution)/shard_map/jvp(vmap())/while/body/eval_jaxpr/jit(_solve_triangular)/triangular_solve/custom-call.1 | solution.py:72
  571.3 39.3 %custom-call.17 = f32[4,1,128,128]{2,3,1,0:T(8,128)S(1)} custom-call(f32[4,1,128,128]{3,2,1,0:T(8,128)S(1)} %fusion.419), custom_call_target="InvertDiagBlocksLowerTriangular" | custom-call | tf_op jit(solution)/shard_map/jvp(vmap())/while/body/eval_jaxpr/jit(_solve_triangular)/triangular_solve/custom-call.1 | solution.py:72
  623.7 3.1 convolution_convert_fusion.1
  630.4 34.5 %all-reduce.44.cloned.1.call-done = bf16[512,1024]{1,0:T(8,128)(2,1)} async-done(((bf16[512,1024]{1,0:T(8,128)(2,1)}), bf16[512,1024]{1,0:T(8,128)(2,1)}) %all-reduce.44.cloned.1.call-update) | async-done | bytes 1048592 | tf_op jit(solution)/shard_map/psum | solution.py:266
  668.1 43.8 %all-gather.20.cloned.1.call-done = bf16[1024,1408]{1,0:T(8,128)(2,1)} async-done(((bf16[64,1408]{1,0:T(8,128)(2,1)}), bf16[1024,1408]{1,0:T(8,128)(2,1)}) %all-gather.20.cloned.1.call-update) | async-done | bytes 2883600 | tf_op jit(solution)/shard_map/all_gather | solution.py:187
  711.9 5.6 fusion.253
  717.4 39.7 %all-gather.22.cloned.1.call-done = bf16[1024,1408]{1,0:T(8,128)(2,1)} async-done(((bf16[64,1408]{1,0:T(8,128)(2,1)}), bf16[1024,1408]{1,0:T(8,128)(2,1)}) %all-gather.22.cloned.1.call-update) | async-done | bytes 2883600 | tf_op jit(solution)/shard_map/all_gather | solution.py:188
  757.1 5.5 fusion.254
  762.6 39.8 %all-gather.24.cloned.1.call-done = bf16[1408,1024]{0,1:T(8,128)(2,1)} async-done(((bf16[1408,64]{0,1:T(8,128)(2,1)}), bf16[1408,1024]{0,1:T(8,128)(2,1)}) %all-gather.24.cloned.1.call-update) | async-done | bytes 2883600 | tf_op jit(solution)/shard_map/all_gather | solution.py:189
  802.4 8.4 multiply_convert_fusion
  817.2 5.1 convolution_convert_fusion
  822.2 32.9 %all-reduce.46.cloned.1.call-done = bf16[512,1024]{1,0:T(8,128)(2,1)} async-done(((bf16[512,1024]{1,0:T(8,128)(2,1)}), bf16[512,1024]{1,0:T(8,128)(2,1)}) %all-reduce.46.cloned.1.call-update) | async-done | bytes 1048592 | tf_op jit(solution)/shard_map/psum | solution.py:310
  868.4 538.5 %while.43 = (s32[]{:T(128)}, f32[4,128,128]{2,1,0:T(8,128)S(1)}, f32[8,4,64,128]{3,2,0,1:T(8,128)}, bf16[8,4,128,128]{3,2,0,1:T(8,128)(2,1)}, bf16[8,4,128,128]{...) while((s32[]{:T(128)}, f32[4,128,128]{2,1,0:T(8,128)S(1)}, ...), condition=%wide.region_27.30_spmd.clone, body=%wide.region_16.29_spmd.clone.sunk | while | flops 1615970816 | bytes 23787272 | solution.py:93
  876.2 39.3 %custom-call.18 = f32[4,1,128,128]{2,3,1,0:T(8,128)S(1)} custom-call(f32[4,1,128,128]{3,2,1,0:T(8,128)S(1)} %get-tuple-element.1259), custom_call_target="InvertDiagBlocksLowerTriangular" | custom-call | tf_op jit(solution)/shard_map/transpose(jvp(vmap()))/while/body/eval_jaxpr/checkpoint/jit(_solve_triangular)/triangular_solve/custom-call.0 | solution.py:72
  943.5 39.3 %custom-call.18 = f32[4,1,128,128]{2,3,1,0:T(8,128)S(1)} custom-call(f32[4,1,128,128]{3,2,1,0:T(8,128)S(1)} %get-tuple-element.1259), custom_call_target="InvertDiagBlocksLowerTriangular" | custom-call | tf_op jit(solution)/shard_map/transpose(jvp(vmap()))/while/body/eval_jaxpr/checkpoint/jit(_solve_triangular)/triangular_solve/custom-call.0 | solution.py:72
  1010.7 39.3 %custom-call.18 = f32[4,1,128,128]{2,3,1,0:T(8,128)S(1)} custom-call(f32[4,1,128,128]{3,2,1,0:T(8,128)S(1)} %get-tuple-element.1259), custom_call_target="InvertDiagBlocksLowerTriangular" | custom-call | tf_op jit(solution)/shard_map/transpose(jvp(vmap()))/while/body/eval_jaxpr/checkpoint/jit(_solve_triangular)/triangular_solve/custom-call.0 | solution.py:72
  1077.9 39.3 %custom-call.18 = f32[4,1,128,128]{2,3,1,0:T(8,128)S(1)} custom-call(f32[4,1,128,128]{3,2,1,0:T(8,128)S(1)} %get-tuple-element.1259), custom_call_target="InvertDiagBlocksLowerTriangular" | custom-call | tf_op jit(solution)/shard_map/transpose(jvp(vmap()))/while/body/eval_jaxpr/checkpoint/jit(_solve_triangular)/triangular_solve/custom-call.0 | solution.py:72
  1145.2 39.3 %custom-call.18 = f32[4,1,128,128]{2,3,1,0:T(8,128)S(1)} custom-call(f32[4,1,128,128]{3,2,1,0:T(8,128)S(1)} %get-tuple-element.1259), custom_call_target="InvertDiagBlocksLowerTriangular" | custom-call | tf_op jit(solution)/shard_map/transpose(jvp(vmap()))/while/body/eval_jaxpr/checkpoint/jit(_solve_triangular)/triangular_solve/custom-call.0 | solution.py:72
  1212.4 39.3 %custom-call.18 = f32[4,1,128,128]{2,3,1,0:T(8,128)S(1)} custom-call(f32[4,1,128,128]{3,2,1,0:T(8,128)S(1)} %get-tuple-element.1259), custom_call_target="InvertDiagBlocksLowerTriangular" | custom-call | tf_op jit(solution)/shard_map/transpose(jvp(vmap()))/while/body/eval_jaxpr/checkpoint/jit(_solve_triangular)/triangular_solve/custom-call.0 | solution.py:72
  1279.7 39.3 %custom-call.18 = f32[4,1,128,128]{2,3,1,0:T(8,128)S(1)} custom-call(f32[4,1,128,128]{3,2,1,0:T(8,128)S(1)} %get-tuple-element.1259), custom_call_target="InvertDiagBlocksLowerTriangular" | custom-call | tf_op jit(solution)/shard_map/transpose(jvp(vmap()))/while/body/eval_jaxpr/checkpoint/jit(_solve_triangular)/triangular_solve/custom-call.0 | solution.py:72
  1346.9 39.3 %custom-call.18 = f32[4,1,128,128]{2,3,1,0:T(8,128)S(1)} custom-call(f32[4,1,128,128]{3,2,1,0:T(8,128)S(1)} %get-tuple-element.1259), custom_call_target="InvertDiagBlocksLowerTriangular" | custom-call | tf_op jit(solution)/shard_map/transpose(jvp(vmap()))/while/body/eval_jaxpr/checkpoint/jit(_solve_triangular)/triangular_solve/custom-call.0 | solution.py:72
  1409.1 4.6 multiply_reduce_fusion.20
  1420.5 3.2 all-to-all-start.5
  1435.4 3.6 all-to-all-start.3
  1440.5 12.3 all-to-all-done.3
  1452.8 4.4 all-to-all-start.4
  1458.9 3.1 copy.663
  1477.9 12.5 multiply_reduce_fusion.12
  1503.0 4.5 fusion.186
  1514.3 3.4 convolution_bitcast_fusion.1
  1518.9 3.4 convolution_bitcast_fusion
  1523.6 5.6 fusion.258
  1529.3 5.7 fusion.259
  1536.2 6.2 fusion.184
  1543.1 4.9 psum.101
  1552.7 63.7 %all-reduce.48.cloned.1.call-done = (bf16[512,1024]{1,0:T(8,128)(2,1)}, bf16[512,1024]{1,0:T(8,128)(2,1)}) async-done(((bf16[512,1024]{1,0:T(8,128)(2,1)}, bf16[512,1024]{1,0:T(8,128)(2,1)}), (bf16[512,1024]{1,0:T(8,128)(2,1)}, bf16[512,1024]{1,0:T(8,128)(2,1)})) %all-reduce.48.cloned.1.call-update) | async-done | bytes 2097168 | tf_op jit(solution)/shard_map/psum | solution.py:275
  1618.6 62.3 %all-reduce.38 = (f32[1024]{0:T(1024)}, f32[4]{0:T(128)}, f32[4]{0:T(128)}, f32[4,512]{1,0:T(4,128)}, f32[1,4,1024]{2,1,0:T(4,128)}, /*index=5*/f32[1,4,1024]{2,1,0:T(4,128)}, f32[128]{0:T(128)}, f32[1024]{0:T(1024)}) all-reduce(f32[1024]{0:T(1024)S(1)} %get-tuple-element.871, ...), channel_id=1, replica_groups=mesh['dp'=16,'step'=2] {'dp'}, use_global_device_ids=true, to_apply=%region_33.36 | all-reduce | flops 12424 | bytes 99136 | tf_op jit(solution)/shard_map/psum | solution.py:427
  1680.9 4.7 fusion.169
  1685.6 62.0 %reduce-scatter.15.cloned.1.call-done = f32[64,512]{1,0:T(8,128)} async-done(((f32[1024,512]{1,0:T(8,128)}), f32[64,512]{1,0:T(8,128)}) %reduce-scatter.15.cloned.1.call-update) | async-done | bytes 131088 | tf_op jit(solution)/shard_map/reduce_scatter | solution.py:407
  1747.6 65.2 %reduce-scatter.17.cloned.1.call-done = f32[64,512]{1,0:T(8,128)} async-done(((f32[1024,512]{1,0:T(8,128)}), f32[64,512]{1,0:T(8,128)}) %reduce-scatter.17.cloned.1.call-update) | async-done | bytes 131088 | tf_op jit(solution)/shard_map/reduce_scatter | solution.py:408
  1812.8 75.6 %reduce-scatter.19.cloned.1.call-done = f32[1,64,1024]{2,1,0:T(8,128)} async-done(((f32[1,1024,1024]{2,1,0:T(8,128)}), f32[1,64,1024]{2,1,0:T(8,128)}) %reduce-scatter.19.cloned.1.call-update) | async-done | bytes 262160 | tf_op jit(solution)/shard_map/reduce_scatter | solution.py:409
  1888.4 76.4 %reduce-scatter.21.cloned.1.call-done = f32[1,64,1024]{2,1,0:T(8,128)} async-done(((f32[1,1024,1024]{2,1,0:T(8,128)}), f32[1,64,1024]{2,1,0:T(8,128)}) %reduce-scatter.21.cloned.1.call-update) | async-done | bytes 262160 | tf_op jit(solution)/shard_map/reduce_scatter | solution.py:410
  1964.8 85.0 %reduce-scatter.25.cloned.1.call-done = f32[64,1408]{1,0:T(8,128)} async-done(((f32[1024,1408]{1,0:T(8,128)}), f32[64,1408]{1,0:T(8,128)}) %reduce-scatter.25.cloned.1.call-update) | async-done | bytes 360464 | tf_op jit(solution)/shard_map/reduce_scatter | solution.py:414
  2049.8 85.1 %reduce-scatter.27.cloned.1.call-done = f32[64,1408]{1,0:T(8,128)} async-done(((f32[1024,1408]{1,0:T(8,128)}), f32[64,1408]{1,0:T(8,128)}) %reduce-scatter.27.cloned.1.call-update) | async-done | bytes 360464 | tf_op jit(solution)/shard_map/reduce_scatter | solution.py:415
  2134.9 85.2 %reduce-scatter.29.cloned.1.call-done = f32[1408,64]{0,1:T(8,128)} async-done(((f32[1408,1024]{0,1:T(8,128)}), f32[1408,64]{0,1:T(8,128)}) %reduce-scatter.29.cloned.1.call-update) | async-done | bytes 360464 | tf_op jit(solution)/shard_map/reduce_scatter | solution.py:416
  (963 shorter events, 480.7 us)
Async XLA Ops:
  7.2 28.7 %copy-start = (bf16[1,512,1024]{2,1,0:T(8,128)(2,1)S(1)}, bf16[1,512,1024]{2,1,0:T(8,128)(2,1)}, u32[]{:S(2)}) copy-start(bf16[1,512,1024]{2,1,0:T(8,128)(2,1)} %param.30) | copy-start | bytes 3145732
  7.2 29.0 %copy-start.53 = (f32[1024]{0:T(1024)S(1)}, f32[1024]{0:T(1024)}, u32[]{:S(2)}) copy-start(f32[1024]{0:T(1024)} %param.34) | copy-start | bytes 12292
  7.2 57.7 %all-gather.14.cloned.1.call-start = ((), (), s32[]{:S(2)}) async-start(), calls=%async_computation.18 | async-start | bytes 1114112 | tf_op jit(solution)/shard_map/all_gather | solution.py:180
  7.9 85.6 %all-gather.12.cloned.1.call-start = ((), (), s32[]{:S(2)}) async-start(), calls=%async_computation.17 | async-start | bytes 2228224 | tf_op jit(solution)/shard_map/all_gather | solution.py:183
  8.7 127.2 %all-gather.10.cloned.1.call-start = ((), (), s32[]{:S(2)}) async-start(), calls=%async_computation.16 | async-start | bytes 2228224 | tf_op jit(solution)/shard_map/all_gather | solution.py:182
  9.4 170.7 %all-gather.16.cloned.1.call-start = ((), (), s32[]{:S(2)}) async-start(), calls=%async_computation.19 | async-start | bytes 1114112 | tf_op jit(solution)/shard_map/all_gather | solution.py:181
  10.8 31.6 %copy-start.92 = (s32[1,512]{1,0:T(1,128)S(1)}, s32[1,512]{1,0:T(1,128)}, u32[]{:S(2)}) copy-start(s32[1,512]{1,0:T(1,128)} %param.33) | copy-start | bytes 6148
  10.8 31.6 %copy-start.87 = (f32[1,4,1024]{2,1,0:T(4,128)S(1)}, f32[1,4,1024]{2,1,0:T(4,128)}, u32[]{:S(2)}) copy-start(f32[1,4,1024]{2,1,0:T(4,128)} %param.44) | copy-start | bytes 49156
  10.8 31.6 %copy-start.88 = (f32[1,4,1024]{2,1,0:T(4,128)S(1)}, f32[1,4,1024]{2,1,0:T(4,128)}, u32[]{:S(2)}) copy-start(f32[1,4,1024]{2,1,0:T(4,128)} %param.45) | copy-start | bytes 49156
  10.8 31.7 %copy-start.91 = (f32[4,512]{1,0:T(4,128)S(1)}, f32[4,512]{1,0:T(4,128)}, u32[]{:S(2)}) copy-start(f32[4,512]{1,0:T(4,128)} %param.43) | copy-start | bytes 24580
  10.8 32.3 %copy-start.98 = (bf16[64,4]{0,1:T(4,128)(2,1)S(1)}, bf16[64,4]{0,1:T(4,128)(2,1)}, u32[]{:S(2)}) copy-start(bf16[64,4]{0,1:T(4,128)(2,1)} %param.40) | copy-start | bytes 1540
  10.8 49.9 %copy-start.107 = (f32[4]{0:T(128)S(1)}, f32[4]{0:T(128)}, u32[]{:S(2)}) copy-start(f32[4]{0:T(128)} %param.41) | copy-start | bytes 52
  35.6 26.5 %copy-start.105 = (f32[4]{0:T(128)S(1)}, f32[4]{0:T(128)}, u32[]{:S(2)}) copy-start(f32[4]{0:T(128)} %param.42) | copy-start | bytes 52
  35.9 26.7 %copy-start.44 = (bf16[1,1024,8]{1,2,0:T(8,128)(2,1)}, bf16[1,1024,8]{1,2,0:T(8,128)(2,1)S(1)}, u32[]{:S(2)}) copy-start(bf16[1,1024,8]{1,2,0:T(8,128)(2,1)S(1)} %copy.628) | copy-start | bytes 49156
  36.2 585.4 %copy-start.72 = (f32[512]{0:T(512)}, f32[512]{0:T(512)S(1)}, u32[]{:S(2)}) copy-start(f32[512]{0:T(512)S(1)} %fusion.216) | copy-start | bytes 6148
  37.9 26.6 %all-to-all-start.1 = ((bf16[1,512,2,4]{1,3,0,2:T(4,128)(2,1)}), bf16[1,512,2,4]{1,3,0,2:T(4,128)(2,1)S(1)}, u32[]{:S(2)}, u32[]{:S(2)}) async-start(bf16[1,512,2,4]{1,3,0,2:T(4,128)(2,1)} %bitcast.24), calls=%async_computation.1 | async-start | bytes 16384 | tf_op jit(solution)/shard_map/all_to_all | solution.py:241
  41.1 582.5 %all-gather.18.cloned.1.call-start = ((), (), s32[]{:S(2)}) async-start(), calls=%async_computation.20 | async-start | bytes 1114112 | tf_op jit(solution)/shard_map/all_gather | solution.py:186
  42.5 96.5 %copy-start.51 = (f32[1,1,1024]{2,1,0:T(1,128)}, f32[1,1,1024]{2,1,0:T(1,128)S(1)}, u32[]{:S(2)}) copy-start(f32[1,1,1024]{2,1,0:T(1,128)S(1)} %get-tuple-element.1001) | copy-start | bytes 12292
  42.5 96.5 %copy-start.55 = (f32[1,1,1024]{2,1,0:T(1,128)}, f32[1,1,1024]{2,1,0:T(1,128)S(1)}, u32[]{:S(2)}) copy-start(f32[1,1,1024]{2,1,0:T(1,128)S(1)} %get-tuple-element.1002) | copy-start | bytes 12292
  42.5 96.5 %copy-start.57 = (f32[1,1,1024]{2,1,0:T(1,128)}, f32[1,1,1024]{2,1,0:T(1,128)S(1)}, u32[]{:S(2)}) copy-start(f32[1,1,1024]{2,1,0:T(1,128)S(1)} %get-tuple-element.1003) | copy-start | bytes 12292
  42.5 96.5 %copy-start.59 = (f32[1,1,1024]{2,1,0:T(1,128)}, f32[1,1,1024]{2,1,0:T(1,128)S(1)}, u32[]{:S(2)}) copy-start(f32[1,1,1024]{2,1,0:T(1,128)S(1)} %get-tuple-element.1004) | copy-start | bytes 12292
  42.5 96.5 %copy-start.49 = (f32[1,1,1024]{2,1,0:T(1,128)}, f32[1,1,1024]{2,1,0:T(1,128)S(1)}, u32[]{:S(2)}) copy-start(f32[1,1,1024]{2,1,0:T(1,128)S(1)} %get-tuple-element.997) | copy-start | bytes 12292
  42.5 96.5 %copy-start.61 = (f32[1,1,1024]{2,1,0:T(1,128)}, f32[1,1,1024]{2,1,0:T(1,128)S(1)}, u32[]{:S(2)}) copy-start(f32[1,1,1024]{2,1,0:T(1,128)S(1)} %get-tuple-element.998) | copy-start | bytes 12292
  42.6 96.5 %copy-start.63 = (f32[1,1,1024]{2,1,0:T(1,128)}, f32[1,1,1024]{2,1,0:T(1,128)S(1)}, u32[]{:S(2)}) copy-start(f32[1,1,1024]{2,1,0:T(1,128)S(1)} %get-tuple-element.999) | copy-start | bytes 12292
  42.6 96.5 %copy-start.65 = (f32[1,1,1024]{2,1,0:T(1,128)}, f32[1,1,1024]{2,1,0:T(1,128)S(1)}, u32[]{:S(2)}) copy-start(f32[1,1,1024]{2,1,0:T(1,128)S(1)} %get-tuple-element.1000) | copy-start | bytes 12292
  43.2 116.5 %copy-start.76 = (f32[1,512]{1,0:T(1,128)}, f32[1,512]{1,0:T(1,128)S(1)}, u32[]{:S(2)}) copy-start(f32[1,512]{1,0:T(1,128)S(1)} %get-tuple-element.1008) | copy-start | bytes 6148
  43.2 116.5 %copy-start.78 = (f32[1,512]{1,0:T(1,128)}, f32[1,512]{1,0:T(1,128)S(1)}, u32[]{:S(2)}) copy-start(f32[1,512]{1,0:T(1,128)S(1)} %get-tuple-element.1009) | copy-start | bytes 6148
  43.2 116.5 %copy-start.80 = (f32[1,512]{1,0:T(1,128)}, f32[1,512]{1,0:T(1,128)S(1)}, u32[]{:S(2)}) copy-start(f32[1,512]{1,0:T(1,128)S(1)} %get-tuple-element.1010) | copy-start | bytes 6148
  143.6 6.9 copy-start.6
  156.1 17.9 all-to-all-start
  164.2 14.5 copy-start.2
  174.0 18.2 all-to-all-start.2
  178.6 486.3 %all-reduce.44.cloned.1.call-start = ((), (), s32[]{:S(2)}) async-start(), calls=%async_computation.21 | async-start | bytes 2097152 | tf_op jit(solution)/shard_map/psum | solution.py:266
  626.8 39.9 %copy-start.47 = (f32[1024]{0:T(1024)S(1)}, f32[1024]{0:T(1024)}, u32[]{:S(2)}) copy-start(f32[1024]{0:T(1024)} %param.48) | copy-start | bytes 12292
  626.8 85.0 %all-gather.20.cloned.1.call-start = ((), (), s32[]{:S(2)}) async-start(), calls=%async_computation.22 | async-start | bytes 3063808 | tf_op jit(solution)/shard_map/all_gather | solution.py:187
  627.6 129.5 %all-gather.22.cloned.1.call-start = ((), (), s32[]{:S(2)}) async-start(), calls=%async_computation.23 | async-start | bytes 3063808 | tf_op jit(solution)/shard_map/all_gather | solution.py:188
  628.3 174.1 %all-gather.24.cloned.1.call-start = ((), (), s32[]{:S(2)}) async-start(), calls=%async_computation.24 | async-start | bytes 3063808 | tf_op jit(solution)/shard_map/all_gather | solution.py:189
  629.1 226.0 %all-reduce.46.cloned.1.call-start = ((), (), s32[]{:S(2)}) async-start(), calls=%async_computation.25 | async-start | bytes 2097152 | tf_op jit(solution)/shard_map/psum | solution.py:310
  666.7 191.3 %copy-start.74 = (f32[512]{0:T(512)}, f32[512]{0:T(512)S(1)}, u32[]{:S(2)}) copy-start(f32[512]{0:T(512)S(1)} %fusion.217) | copy-start | bytes 6148
  802.4 8.4 copy-start.100
  1415.0 8.7 copy-start.85
  1420.5 14.9 all-to-all-start.5
  1423.7 124.4 %reduce-scatter.33.cloned.1.call-start = ((), (), s32[]{:S(2)}) async-start(), calls=%async_computation.35 | async-start | bytes 557056
  1435.4 17.5 all-to-all-start.3
  1439.0 112.3 %reduce-scatter.31.cloned.1.call-start = ((), (), s32[]{:S(2)}) async-start(), calls=%async_computation.34 | async-start | bytes 557056
  1452.8 17.5 all-to-all-start.4
  1457.3 159.1 %all-reduce.48.cloned.1.call-start = ((), (), s32[]{:S(2)}) async-start(), calls=%async_computation.36 | async-start | bytes 4194304 | tf_op jit(solution)/shard_map/psum | solution.py:275
  1477.9 12.5 copy-start.56
  1477.9 12.5 copy-start.58
  1477.9 12.5 copy-start.60
  1477.9 12.5 copy-start.62
  1477.9 12.5 copy-start.64
  1477.9 12.5 copy-start.66
  1501.5 184.1 %reduce-scatter.23.cloned.1.call-start = ((), (), s32[]{:S(2)}) async-start(), calls=%async_computation.30 | async-start | bytes 2228224 | tf_op jit(solution)/shard_map/reduce_scatter | solution.py:413
  1507.6 240.0 %reduce-scatter.15.cloned.1.call-start = ((), (), s32[]{:S(2)}) async-start(), calls=%async_computation.26 | async-start | bytes 2228224 | tf_op jit(solution)/shard_map/reduce_scatter | solution.py:407
  1510.8 302.0 %reduce-scatter.17.cloned.1.call-start = ((), (), s32[]{:S(2)}) async-start(), calls=%async_computation.27 | async-start | bytes 2228224 | tf_op jit(solution)/shard_map/reduce_scatter | solution.py:408
  1513.1 375.2 %reduce-scatter.19.cloned.1.call-start = ((), (), s32[]{:S(2)}) async-start(), calls=%async_computation.28 | async-start | bytes 4456448 | tf_op jit(solution)/shard_map/reduce_scatter | solution.py:409
  1517.7 447.0 %reduce-scatter.21.cloned.1.call-start = ((), (), s32[]{:S(2)}) async-start(), calls=%async_computation.29 | async-start | bytes 4456448 | tf_op jit(solution)/shard_map/reduce_scatter | solution.py:410
  1522.4 527.4 %reduce-scatter.25.cloned.1.call-start = ((), (), s32[]{:S(2)}) async-start(), calls=%async_computation.31 | async-start | bytes 6127616 | tf_op jit(solution)/shard_map/reduce_scatter | solution.py:414
  1529.3 605.6 %reduce-scatter.27.cloned.1.call-start = ((), (), s32[]{:S(2)}) async-start(), calls=%async_computation.32 | async-start | bytes 6127616 | tf_op jit(solution)/shard_map/reduce_scatter | solution.py:415
  1535.0 685.0 %reduce-scatter.29.cloned.1.call-start = ((), (), s32[]{:S(2)}) async-start(), calls=%async_computation.33 | async-start | bytes 6127616 | tf_op jit(solution)/shard_map/reduce_scatter | solution.py:416
  1542.5 76.1 %copy-start.86 = (f32[1024]{0:T(1024)S(1)}, f32[1024]{0:T(1024)}, u32[]{:S(2)}) copy-start(f32[1024]{0:T(1024)} %get-tuple-element.863) | copy-start | bytes 12292
  1542.5 138.4 %copy-start.83 = (f32[512]{0:T(512)S(1)}, f32[512]{0:T(512)}, u32[]{:S(2)}) copy-start(f32[512]{0:T(512)} %copy-done.82) | copy-start | bytes 6148
  1542.5 138.4 %copy-start.24 = (bf16[512,1024]{1,0:T(8,128)(2,1)S(1)}, bf16[512,1024]{1,0:T(8,128)(2,1)}, u32[]{:S(2)}) copy-start(bf16[512,1024]{1,0:T(8,128)(2,1)} %all-reduce.46.cloned.1.call-done) | copy-start | bytes 3145732
  (72 other events, 198.5 us)
Sparse Core Ops, SparseCore 0:
  10.2 40.8 all-gather.13
  53.2 40.2 all-gather.11
  95.7 40.1 all-gather.9
  137.9 36.6 all-gather.15
  176.7 36.9 all-gather.17
  627.0 37.9 all-reduce.43
  667.5 44.3 all-gather.19
  714.4 42.6 all-gather.21
  759.7 42.6 all-gather.23
  816.7 38.3 all-reduce.45
  1435.5 57.1 reduce-scatter.32
  1496.5 54.7 reduce-scatter.30
  1554.2 62.1 all-reduce.47
  1621.0 61.6 reduce-scatter.22
  1686.9 60.6 reduce-scatter.14
  1752.2 60.5 reduce-scatter.16
  1817.1 71.2 reduce-scatter.18
  1893.1 71.5 reduce-scatter.20
  1969.2 80.5 reduce-scatter.24
  2054.1 80.7 reduce-scatter.26
  2139.3 80.6 reduce-scatter.28
where the time goes:
time: 2240 us; the launch traced here: 2230 us
  waiting for transfers between devices  879 us (39%)
  other arithmetic  749 us (33%)
  matrix products  285 us (13%)
  local copies, waits for them, and re-layouts  161 us (7%)
  blocking collectives  109 us (5%)
  starting transfers between devices  24.2 us (1%)
    another operation x64, other arithmetic, block_pass(): jax.scipy.linalg.solve_triangular(system, target, lower=True, unit_diagon...  632 us
    dot_general x176, matrix products, matmul(): return jnp.dot(first, second, precision=PRECISE)  150 us
    reduce_scatter x1, waiting for transfers between devices, per_device(): lax.psum_scatter(grad_down, 'dp', scatter_dimension=1, tiled=True)  85.2 us
    reduce_scatter x1, waiting for transfers between devices, per_device(): lax.psum_scatter(grad_up, 'dp', scatter_dimension=0, tiled=True)  85.1 us
    reduce_scatter x1, waiting for transfers between devices, per_device(): lax.psum_scatter(grad_gate, 'dp', scatter_dimension=0, tiled=True)  85 us
    reduce_scatter x1, waiting for transfers between devices, per_device(): lax.psum_scatter(grad_value[None], 'dp', scatter_dimension=1, tiled=True)  76.4 us
    reduce_scatter x1, waiting for transfers between devices, per_device(): lax.psum_scatter(grad_key[None], 'dp', scatter_dimension=1, tiled=True)  75.6 us
    reduce_scatter x1, waiting for transfers between devices, per_device(): lax.psum_scatter(grad_outgate, 'dp', scatter_dimension=0, tiled=True)  65.2 us
  transfers between devices with their start and end apart: 27, of which 20 were waited for; matrix products, arithmetic and copies ran while one was open for 27% of the time, Pallas kernels for 0%

commit v1 on v0

v1 whole, which is shorter than its diff:
```python
import functools

import jax
import jax.numpy as jnp
from jax import lax
from jax.experimental import pallas as pl
from jax.experimental.pallas import tpu as pltpu
from jax.sharding import PartitionSpec as P

STRETCH = 64
DK = 128
F32 = jnp.float32
BF = jnp.bfloat16
NN = ((1,), (0,))
NT = ((1,), (1,))
TN = ((0,), (0,))


def split(a):
    if a.dtype == BF:
        return (a,)
    hi = a.astype(BF)
    return (hi, (a - hi.astype(F32)).astype(BF))


def dot1(a, b, dims=NN):
    return lax.dot_general(a.astype(BF), b.astype(BF), (dims, ((), ())), preferred_element_type=F32)


def dot3(a, b, dims=NN):
    a = a if isinstance(a, tuple) else split(a)
    b = b if isinstance(b, tuple) else split(b)
    one = lambda x, y: lax.dot_general(x, y, (dims, ((), ())), preferred_element_type=F32)
    out = one(a[0], b[0])
    if len(a) > 1:
        out = out + one(a[1], b[0])
    if len(b) > 1:
        out = out + one(a[0], b[1])
    return out


def dot6(a, b, dims=NN):
    return lax.dot_general(
        a, b, (dims, ((), ())), precision=lax.Precision.HIGHEST, preferred_element_type=F32
    )


def iota(shape, dim):
    return lax.broadcasted_iota(jnp.int32, shape, dim)


def block_masks():
    span = 2 * STRETCH
    row, col = iota((span, span), 0), iota((span, span), 1)
    t_row, t_col = row % STRETCH, col % STRETCH
    p_row, p_col = 2 * t_row + row // STRETCH, 2 * t_col + col // STRETCH
    return t_row, t_col, p_row, p_col


def twice(block):
    return jnp.concatenate([block, block], axis=0)


def block_scalars(aux):
    low = (iota((STRETCH, STRETCH), 0) >= iota((STRETCH, STRETCH), 1)).astype(F32)
    running = dot6(low, aux)
    aux2, run2 = twice(aux), twice(running)
    return aux2, run2, aux2.T, run2.T


def head_terms(aux, aux2, run2, aux_t, run_t, head, heads):
    beta = jnp.concatenate(
        [aux[:, head : head + 1], aux[:, heads + head : heads + head + 1]], axis=0
    )
    lane = 2 * heads + head
    run_col = run2[:, lane : lane + 1]
    run_row = run_t[lane : lane + 1, :]
    doc_lane = 3 * heads
    doc_col = aux2[:, doc_lane : doc_lane + 1]
    doc_row = aux_t[doc_lane : doc_lane + 1, :]
    fresh = aux2[:, doc_lane + 1 : doc_lane + 2]
    span = 2 * STRETCH
    carried = jnp.where(fresh > 0.5, jnp.exp(run_col), 0.0)
    last_run = run_col[span - 1 : span, :]
    to_last = jnp.where(doc_col == doc_col[span - 1 : span, :], jnp.exp(last_run - run_col), 0.0)
    return beta, run_col, run_row, doc_col, doc_row, carried, to_last


def decay_matrix(run_col, run_row, doc_col, doc_row, p_row, p_col):
    inside = (p_row >= p_col) & (doc_col == doc_row)
    return jnp.where(inside, jnp.exp(jnp.where(inside, run_col - run_row, 0.0)), 0.0)


def inverse(mats, masks):
    t_row, t_col, p_row, p_col = masks
    eye = (p_row == p_col).astype(F32)
    pair = (t_row == t_col) & (p_row > p_col)
    out = [eye - jnp.where(pair, a, 0.0) for a in mats]
    level = 1
    while (1 << level) <= STRETCH:
        merge = (
            ((t_row >> level) == (t_col >> level))
            & (((t_row >> (level - 1)) & 1) == 1)
            & (((t_col >> (level - 1)) & 1) == 0)
        )
        low = [x.astype(BF) for x in out]
        half = [dot1(x, jnp.where(merge, a, 0.0)) for x, a in zip(low, mats)]
        out = [o - dot1(h, x) for o, h, x in zip(out, half, low)]
        level += 1
    rest = [eye - x - dot3(a, x) for a, x in zip(mats, out)]
    return [x + dot1(x, r) for x, r in zip(out, rest)]


def mixer_fwd_kernel(heads, q_ref, k_ref, v_ref, aux_ref, gate_ref, gain_ref,
                     gated_ref, mixed_ref, inv_ref, state_ref, pseudo_ref, attn_ref):
    blocks = q_ref.shape[0] // STRETCH
    span = 2 * STRETCH
    masks = block_masks()
    t_row, t_col, p_row, p_col = masks

    def keys_of(rows, cols):
        return jnp.concatenate([k_ref[0, rows, cols], k_ref[1, rows, cols]], axis=0)

    def prepare(block, carry):
        rows = pl.ds(pl.multiple_of(block * STRETCH, STRETCH), STRETCH)
        aux = aux_ref[rows, :]
        aux2, run2, aux_t, run_t = block_scalars(aux)
        mats = []
        for head in range(heads):
            cols = slice(head * DK, (head + 1) * DK)
            beta, run_col, run_row, doc_col, doc_row, carried, to_last = head_terms(
                aux, aux2, run2, aux_t, run_t, head, heads
            )
            decay = decay_matrix(run_col, run_row, doc_col, doc_row, p_row, p_col)
            keys = keys_of(rows, cols)
            gram = dot1(keys, keys, NT)
            mats.append(beta * jnp.where(p_row > p_col, decay * gram, 0.0))
            attn_ref[block * heads + head] = decay[STRETCH:] * dot3(q_ref[rows, cols], keys, NT)
        for head, inv in enumerate(inverse(mats, masks)):
            inv_ref[block * heads + head] = inv
        return carry

    lax.fori_loop(0, blocks, prepare, 0)
    for head in range(heads):
        state_ref[head] = jnp.zeros((DK, DK), F32)

    def advance(block, carry):
        rows = pl.ds(pl.multiple_of(block * STRETCH, STRETCH), STRETCH)
        aux = aux_ref[rows, :]
        aux2, run2, aux_t, run_t = block_scalars(aux)
        for head in range(heads):
            cols = slice(head * DK, (head + 1) * DK)
            beta, run_col, run_row, doc_col, doc_row, carried, to_last = head_terms(
                aux, aux2, run2, aux_t, run_t, head, heads
            )
            keys = keys_of(rows, cols)
            values = jnp.concatenate([v_ref[0, rows, cols], v_ref[1, rows, cols]], axis=0).astype(F32)
            state = state_ref[block * heads + head]
            state_parts = split(state)
            target = beta * (values - carried * dot3(keys, state_parts))
            pseudo = dot3(inv_ref[block * heads + head], target)
            pseudo_ref[block * heads + head] = pseudo
            mixed = carried[STRETCH:] * dot3(q_ref[rows, cols], state_parts) + dot3(
                attn_ref[block * heads + head], pseudo
            )
            state_ref[(block + 1) * heads + head] = carried[span - 1 : span] * state + dot3(
                keys, to_last * pseudo, TN
            )
            mixed_ref[rows, cols] = mixed
            scale = lax.rsqrt(jnp.mean(mixed * mixed, axis=-1, keepdims=True) + 1e-05)
            gate = gate_ref[rows, cols]
            gated_ref[rows, cols] = (mixed * scale * gain_ref[...] * (gate * jax.nn.sigmoid(gate))).astype(BF)
        return carry

    lax.fori_loop(0, blocks, advance, 0)


def mixer_bwd_kernel(heads, q_ref, k_ref, v_ref, aux_ref, gate_ref, gain_ref, mixed_ref, inv_ref,
                     state_ref, pseudo_ref, dgated_ref,
                     dq_ref, dk_ref, dv_ref, daux_ref, dgate_ref, dgain_ref, dstate):
    blocks = q_ref.shape[0] // STRETCH
    span = 2 * STRETCH
    masks = block_masks()
    t_row, t_col, p_row, p_col = masks
    for head in range(heads):
        dstate[head] = jnp.zeros((DK, DK), F32)
    dgain_ref[...] = jnp.zeros_like(dgain_ref)
    upper = (iota((STRETCH, STRETCH), 0) <= iota((STRETCH, STRETCH), 1)).astype(F32)
    lanes = iota((STRETCH, DK), 1)
    wide_lanes = iota((span, DK), 1)
    wide_rows = iota((span, DK), 0)

    def back(step, carry):
        block = blocks - 1 - step
        rows = pl.ds(pl.multiple_of(block * STRETCH, STRETCH), STRETCH)
        aux = aux_ref[rows, :]
        aux2, run2, aux_t, run_t = block_scalars(aux)
        dbeta_all = jnp.zeros((STRETCH, DK), F32)
        drun_all = jnp.zeros((STRETCH, DK), F32)
        column_sums = jnp.zeros((span, DK), F32)
        for head in range(heads):
            cols = slice(head * DK, (head + 1) * DK)
            beta, run_col, run_row, doc_col, doc_row, carried, to_last = head_terms(
                aux, aux2, run2, aux_t, run_t, head, heads
            )
            decay = decay_matrix(run_col, run_row, doc_col, doc_row, p_row, p_col)
            keys = keys = jnp.concatenate([k_ref[0, rows, cols], k_ref[1, rows, cols]], axis=0)
            queries = q_ref[rows, cols]
            mixed = mixed_ref[rows, cols]
            gate = gate_ref[rows, cols]
            sigmoid = jax.nn.sigmoid(gate)
            silu = gate * sigmoid
            scale = lax.rsqrt(jnp.mean(mixed * mixed, axis=-1, keepdims=True) + 1e-05)
            scaled = mixed * scale
            dgated = dgated_ref[rows, cols]
            part = dgated * scaled
            dgate_ref[rows, cols] = (
                part * gain_ref[...] * (sigmoid * (1.0 + gate * (1.0 - sigmoid)))
            ).astype(BF)
            dgain_ref[...] += jnp.sum(part * silu, axis=0, keepdims=True)
            dscaled = dgated * gain_ref[...] * silu
            dout = scale * (dscaled - scaled * jnp.mean(dscaled * scaled, axis=-1, keepdims=True))

            index = block * heads + head
            state, pseudo = state_ref[index], pseudo_ref[index]
            dnext = dstate[head]
            dnext_parts, state_parts, pseudo_parts = split(dnext), split(state), split(pseudo)
            dout_parts, q_parts = split(dout), split(queries)
            gram = dot1(keys, keys, NT)
            strict = p_row > p_col
            core = jnp.where(strict, decay * gram, 0.0)
            amat = beta * core
            qdecay = decay[STRETCH:]
            attn = qdecay * dot3(q_parts, keys, NT)
            dattn = dot3(dout_parts, pseudo_parts, NT)
            dqk = split(qdecay * dattn)
            dpseudo = dot3(attn, dout_parts, TN) + to_last * dot3(keys, dnext_parts)
            dtarget = dot3(inv_ref[index], dpseudo, TN)
            dtarget_parts = split(dtarget)
            damat = jnp.where(strict, -dot3(dtarget_parts, pseudo_parts, NT), 0.0)
            e_a, e_m = damat * amat, dattn * attn
            dgram = split(beta * decay * damat)
            dbeta = jnp.sum(dtarget * pseudo, axis=-1, keepdims=True) / jnp.maximum(beta, 1e-30)
            dvalues = beta * dtarget
            dread = -(beta * carried) * dtarget
            dout_c = carried[STRETCH:] * dout
            dread_parts, dout_c_parts = split(dread), split(dout_c)
            last = carried[span - 1 : span]
            dstate[head] = last * dnext + dot3(keys, dread_parts, TN) + dot3(q_parts, dout_c_parts, TN)
            dq_state = dot3(dout_c_parts, state_parts, NT)
            dk_state = dot3(dread_parts, state_parts, NT)
            dk_last = dot3(to_last * pseudo, dnext_parts, NT)
            dq_ref[rows, cols] = dq_state + dot3(dqk, keys)
            dkeys = (
                dk_state + dk_last + dot3(dgram, keys) + dot3(dgram, keys, TN) + dot3(dqk, q_parts, TN)
            )
            dk_ref[0, rows, cols] = dkeys[:STRETCH].astype(BF)
            dk_ref[1, rows, cols] = dkeys[STRETCH:].astype(BF)
            dv_ref[0, rows, cols] = dvalues[:STRETCH].astype(BF)
            dv_ref[1, rows, cols] = dvalues[STRETCH:].astype(BF)

            wide = keys.astype(F32)
            e_last = jnp.sum(wide * dk_last, axis=-1, keepdims=True)
            drun = jnp.sum(e_a, axis=-1, keepdims=True) - e_last + jnp.sum(wide * dk_state, axis=-1, keepdims=True)
            drun_q = jnp.sum(e_m, axis=-1, keepdims=True) + jnp.sum(queries * dq_state, axis=-1, keepdims=True)
            at_last = jnp.sum(e_last, axis=0, keepdims=True) + last * jnp.sum(
                jnp.sum(dnext * state, axis=-1, keepdims=True), axis=0, keepdims=True
            )
            drun = drun[:STRETCH] + drun[STRETCH:] + drun_q
            drun = drun + jnp.where(iota((STRETCH, 1), 0) == STRETCH - 1, at_last, 0.0)
            lane = 2 * heads + head
            drun_all = jnp.where(lanes == lane, drun, drun_all)
            dbeta_all = jnp.where(lanes == head, dbeta[:STRETCH], dbeta_all)
            dbeta_all = jnp.where(lanes == heads + head, dbeta[STRETCH:], dbeta_all)
            sums = jnp.sum(e_a, axis=0, keepdims=True) + jnp.sum(e_m, axis=0, keepdims=True)
            column_sums = jnp.where(wide_rows == lane, sums, column_sums)
        down = column_sums.T
        drun_all = drun_all - down[:STRETCH] - down[STRETCH:]
        daux_ref[rows, :] = jnp.where(lanes < 2 * heads, dbeta_all, dot6(upper, drun_all))
        return carry

    lax.fori_loop(0, blocks, back, 0)


VMEM = pl.BlockSpec(memory_space=pltpu.VMEM)


def mixer_fwd(q, k, v, aux, gate, gain):
    seq, width = q.shape
    heads, blocks = width // DK, seq // STRETCH
    units = heads * blocks
    span = 2 * STRETCH
    shape = jax.ShapeDtypeStruct
    return pl.pallas_call(
        functools.partial(mixer_fwd_kernel, heads),
        out_shape=(
            shape((seq, width), BF),
            shape((seq, width), F32),
            shape((units, span, span), F32),
            shape((units + heads, DK, DK), F32),
            shape((units, span, DK), F32),
        ),
        in_specs=[VMEM] * 6,
        out_specs=(VMEM,) * 5,
        scratch_shapes=[pltpu.VMEM((units, STRETCH, span), F32)],
        compiler_params=pltpu.CompilerParams(vmem_limit_bytes=48 << 20),
        name="mixer_forward",
    )(q, k, v, aux, gate, gain)


def mixer_bwd(q, k, v, aux, gate, gain, mixed, inv, state, pseudo, dgated):
    seq, width = q.shape
    heads = width // DK
    shape = jax.ShapeDtypeStruct
    return pl.pallas_call(
        functools.partial(mixer_bwd_kernel, heads),
        out_shape=(
            shape((seq, width), F32),
            shape(k.shape, BF),
            shape(v.shape, BF),
            shape((seq, DK), F32),
            shape((seq, width), BF),
            shape((1, DK), F32),
        ),
        in_specs=[VMEM] * 11,
        out_specs=(VMEM,) * 6,
        scratch_shapes=[pltpu.VMEM((heads, DK, DK), F32)],
        compiler_params=pltpu.CompilerParams(vmem_limit_bytes=48 << 20),
        name="mixer_backward",
    )(q, k, v, aux, gate, gain, mixed, inv, state, pseudo, dgated)


GROUPS = 8


def product(first, second, dims=NN):
    return lax.dot_general(first, second, (dims, ((), ())), preferred_element_type=F32)


def rms_scale(values, scales):
    return values * lax.rsqrt(jnp.mean(values * values, axis=-1, keepdims=True) + 1e-06) * scales


def unit_rows(values):
    return values * lax.rsqrt(jnp.sum(values * values, axis=-1, keepdims=True) + 1e-06)


def silu_grad(values):
    sigmoid = jax.nn.sigmoid(values)
    return sigmoid * (1.0 + values * (1.0 - sigmoid))


def short_conv(signal, kernel, doc_ids):
    seq_len = signal.shape[0]
    summed = signal * kernel[0]
    for offset in range(1, kernel.shape[0]):
        shifted = jnp.pad(signal, ((offset, 0), (0, 0)))[:seq_len]
        shifted_docs = jnp.pad(doc_ids, (offset, 0), constant_values=-1)[:seq_len]
        same_doc = (shifted_docs == doc_ids).astype(F32)[:, None]
        summed = summed + shifted * same_doc * kernel[offset]
    return summed


def unit_heads(values):
    seq_len = values.shape[0]
    return unit_rows(values.reshape(seq_len, -1, DK)).reshape(seq_len, -1)


def per_device(
    tokens,
    cotangent,
    domains,
    doc_ids,
    norm_gain,
    w_query,
    w_outgate,
    w_key,
    w_value,
    w_beta,
    w_alpha,
    decay_log,
    decay_bias,
    conv_query,
    conv_key,
    conv_value,
    mix_gain,
    w_out,
    ffn_gain,
    w_gate,
    w_up,
    w_down,
):
    row_total = domains.shape[0]
    group_ids = lax.broadcasted_iota(jnp.int32, (row_total, GROUPS), 1)
    member = (domains[:, None] == group_ids).astype(F32)
    group_sizes = jnp.sum(member, axis=0)
    row_sizes = jnp.sum(member * group_sizes[None, :], axis=1)
    row_weights = 2.0 / (1.0 + row_sizes * (GROUPS / row_total))
    own_row = (lax.broadcasted_iota(jnp.int32, (row_total,), 0) == lax.axis_index("dp")).astype(F32)
    weight_here = jnp.sum(own_row * row_weights)

    depth = w_query.shape[0]
    half = w_query.shape[1]
    heads = w_alpha.shape[1]
    side = lax.axis_index("step")

    def by_step(own, other):
        first = side == 0
        return [jnp.where(first, own, other), jnp.where(first, other, own)]

    def swap(array):
        return lax.ppermute(array, "step", [(0, 1), (1, 0)])

    def parts_for(array, width):
        return (
            lax.dynamic_slice_in_dim(array, side * width, width, 1),
            lax.dynamic_slice_in_dim(array, (1 - side) * width, width, 1),
        )

    key_mine, key_theirs = parts_for(w_key[0], half)
    value_mine, value_theirs = parts_for(w_value[0], half)
    beta_mine, beta_theirs = parts_for(w_beta[0], heads)
    got = swap(jnp.concatenate([key_theirs, value_theirs, beta_theirs], axis=1))
    conv_k_mine, conv_k_theirs = parts_for(conv_key[0], half)
    conv_v_mine, conv_v_theirs = parts_for(conv_value[0], half)
    got_conv = swap(jnp.concatenate([conv_k_theirs, conv_v_theirs], axis=1))
    keys_w = by_step(key_mine, got[:, :half])
    values_w = by_step(value_mine, got[:, half : 2 * half])
    betas_w = by_step(beta_mine, got[:, 2 * half :])
    kernels_k = by_step(conv_k_mine, got_conv[:, :half])
    kernels_v = by_step(conv_v_mine, got_conv[:, half:])
    pad = jnp.zeros((depth, DK - 3 * heads), BF)
    front_w = lax.all_gather(
        jnp.concatenate([w_query, w_outgate] + keys_w + values_w + betas_w + [w_alpha, pad], axis=1),
        "dp", axis=0, tiled=True,
    )
    back_w = lax.all_gather(
        jnp.concatenate([w_out.T, w_gate, w_up, w_down.T], axis=1), "dp", axis=0, tiled=True
    )
    ff = w_gate.shape[1]

    inputs = tokens[0].astype(F32)
    docs = doc_ids[0]
    seq_len = inputs.shape[0]
    normed_f, pull_first = jax.vjp(rms_scale, inputs, norm_gain)
    normed = normed_f.astype(BF)
    pre = product(normed, front_w)
    gate_pre = pre[:, half : 2 * half]

    def prepare(pre_in, query_kernel, key_0, key_1, value_0, value_1, log_rates, rate_bias):
        queries = unit_heads(jax.nn.silu(short_conv(pre_in[:, :half], query_kernel, docs))) * DK ** (-0.5)
        keys = [
            unit_heads(jax.nn.silu(short_conv(pre_in[:, (2 + i) * half : (3 + i) * half], kernel, docs)))
            for i, kernel in enumerate((key_0, key_1))
        ]
        values = [
            jax.nn.silu(short_conv(pre_in[:, (4 + i) * half : (5 + i) * half], kernel, docs))
            for i, kernel in enumerate((value_0, value_1))
        ]
        scalars = pre_in[:, 6 * half :]
        betas = 2.0 * jax.nn.sigmoid(scalars[:, : 2 * heads])
        decays = -jnp.exp(log_rates) * jax.nn.softplus(scalars[:, 2 * heads : 3 * heads] + rate_bias)
        return (queries, jnp.stack(keys), jnp.stack(values), betas, decays)

    (queries, keys, values, betas, decays), pull_prepare = jax.vjp(
        prepare, pre, conv_query, kernels_k[0], kernels_k[1], kernels_v[0], kernels_v[1], decay_log, decay_bias
    )
    prior = jnp.concatenate([jnp.full((1,), -1, docs.dtype), docs[STRETCH - 1 : -1 : STRETCH]])
    fresh = (docs.reshape(-1, STRETCH) == prior[:, None]).reshape(seq_len, 1).astype(F32)
    aux = jnp.concatenate(
        [betas.astype(BF).astype(F32), decays, docs.astype(F32)[:, None], fresh,
         jnp.zeros((seq_len, DK - 3 * heads - 2), F32)],
        axis=1,
    )
    keys, values = keys.astype(BF), values.astype(BF)
    gain_row = mix_gain[None]
    gated, mixed, inv, state, pseudo = mixer_fwd(queries, keys, values, aux, gate_pre, gain_row)

    attention = lax.psum(product(gated, back_w[:, :half], NT).astype(BF), "step").astype(F32)
    middle = inputs + attention
    normed_ffn_f, pull_second = jax.vjp(rms_scale, middle, ffn_gain)
    normed_ffn = normed_ffn_f.astype(BF)
    gate_w, up_w, down_w = (back_w[:, half + i * ff : half + (i + 1) * ff] for i in range(3))
    gate_in = product(normed_ffn, gate_w)
    up_in = product(normed_ffn, up_w)
    hidden = (jax.nn.silu(gate_in) * up_in).astype(BF)
    ffn_out = lax.psum(product(hidden, down_w, NT).astype(BF), "step").astype(F32)
    output = (middle + ffn_out).astype(BF)[None]

    seed = cotangent[0].astype(F32) * weight_here
    seed_low = seed.astype(BF)
    grad_down = product(seed_low, hidden, TN)
    hidden_back = product(seed_low, down_w)
    gate_back = (hidden_back * up_in * silu_grad(gate_in)).astype(BF)
    up_back = (hidden_back * jax.nn.silu(gate_in)).astype(BF)
    grad_gate = product(normed_ffn, gate_back, TN)
    grad_up = product(normed_ffn, up_back, TN)
    ffn_in_back = lax.psum(
        (product(gate_back, gate_w, NT) + product(up_back, up_w, NT)).astype(BF), "step"
    ).astype(F32)
    middle_norm_back, grad_ffn_gain = pull_second(ffn_in_back)
    middle_back = seed + middle_norm_back
    attn_back = middle_back.astype(BF)
    grad_out = product(attn_back, gated, TN)
    sum_back = lax.psum_scatter(
        jnp.concatenate([grad_out, grad_gate, grad_up, grad_down], axis=1).astype(BF),
        "dp", scatter_dimension=0, tiled=True,
    ).astype(F32)
    gated_back = product(attn_back, back_w[:, :half])
    dq, dk, dv, daux, dgate, dgain = mixer_bwd(
        queries, keys, values, aux, gate_pre, gain_row, mixed, inv, state, pseudo, gated_back
    )
    dbetas = daux[:, : 2 * heads].astype(BF).astype(F32)
    ddecays = daux[:, 2 * heads : 3 * heads]
    dpre, d_cq, d_k0, d_k1, d_v0, d_v1, d_log, d_bias = pull_prepare(
        (dq, dk.astype(F32), dv.astype(F32), dbetas, ddecays)
    )
    dpre_low = jnp.concatenate([dpre[:, :half].astype(BF), dgate, dpre[:, 2 * half :].astype(BF)], axis=1)
    grad_front = product(normed, dpre_low, TN)
    normed_back = lax.psum(product(dpre_low, front_w, NT).astype(BF), "step").astype(F32)
    input_back, grad_norm_gain = pull_first(normed_back)
    input_grad = (middle_back + input_back).astype(BF)[None]
    sum_front = lax.psum_scatter(grad_front.astype(BF), "dp", scatter_dimension=0, tiled=True)

    def home(parts):
        mine = jnp.where(side == 0, parts[0], parts[1])
        other = swap(jnp.where(side == 0, parts[1], parts[0]))
        return jnp.where(
            side == 0, jnp.concatenate([mine, other], axis=1), jnp.concatenate([other, mine], axis=1)
        )

    col = lambda i: sum_front[:, i * half : (i + 1) * half]
    sum_key, sum_value = home([col(2), col(3)]), home([col(4), col(5)])
    tail = sum_front[:, 6 * half :]
    sum_beta = home([tail[:, :heads], tail[:, heads : 2 * heads]])
    small = lax.psum(
        (grad_norm_gain, d_log, d_bias, d_cq, d_k0, d_k1, d_v0, d_v1, grad_ffn_gain), "dp"
    )
    sum_norm_gain, sum_log, sum_bias, sum_cq, s_k0, s_k1, s_v0, s_v1, sum_ffn_gain = small
    sum_mix_gain = lax.psum(dgain[0], ("dp", "step"))
    f32 = lambda a: a.astype(F32)
    return (
        output,
        input_grad,
        sum_norm_gain,
        f32(col(0)),
        f32(col(1)),
        f32(sum_key)[None],
        f32(sum_value)[None],
        f32(sum_beta)[None],
        f32(tail[:, 2 * heads : 3 * heads]),
        sum_log,
        sum_bias,
        sum_cq,
        home([s_k0, s_k1])[None],
        home([s_v0, s_v1])[None],
        sum_mix_gain,
        sum_back[:, :half].T,
        sum_ffn_gain,
        sum_back[:, half : half + ff],
        sum_back[:, half + ff : half + 2 * ff],
        sum_back[:, half + 2 * ff :].T,
    )


def solution(mesh):
    return jax.shard_map(
        per_device,
        mesh=mesh,
        in_specs=(
            P("dp", None, None),
            P("dp", None, None),
            P(),
            P("dp", None),
            P(),
            P("dp", "step"),
            P("dp", "step"),
            P("step", "dp", None),
            P("step", "dp", None),
            P("step", "dp", None),
            P("dp", "step"),
            P("step"),
            P("step"),
            P(None, "step"),
            P("step", None, None),
            P("step", None, None),
            P(),
            P("step", "dp"),
            P(),
            P("dp", "step"),
            P("dp", "step"),
            P("step", "dp"),
        ),
        out_specs=(
            P("dp", None, None),
            P("dp", None, None),
            P(),
            P("dp", "step"),
            P("dp", "step"),
            P("step", "dp", None),
            P("step", "dp", None),
            P("step", "dp", None),
            P("dp", "step"),
            P("step"),
            P("step"),
            P(None, "step"),
            P("step", None, None),
            P("step", None, None),
            P(),
            P("step", "dp"),
            P(),
            P("dp", "step"),
            P("dp", "step"),
            P("step", "dp"),
        ),
        check_vma=False,
    )
```

time: 2240 us -> 671 us (0.30)
  other arithmetic: 749 us -> 86.1 us
  waiting for transfers between devices: 879 us -> 242 us
  matrix products: 285 us -> 67.6 us
  local copies, waits for them, and re-layouts: 161 us -> 57.6 us
  Pallas kernels: 0 us -> 78.7 us
    another operation x106 -> x4, other arithmetic: 648 us -> 5.72 us  [the longest x3 5.43 us: prepare(): return (queries, jnp.stack(keys), jnp.stack(values), betas, decays)]
    reduce_scatter x8 -> x2, waiting for transfers between devices: 534 us -> 111 us  [the longest x1 105 us: per_device(): lax.psum_scatter(jnp.concatenate([grad_out, grad_gate, grad_up, grad_down...]
    dot_general x213 -> x15, matrix products: 248 us -> 67.6 us  [product(): lax.dot_general(first, second, (dims, ((), ())), preferred_element_type=F32)]
    all_gather x8 -> x2, waiting for transfers between devices: 187 us -> 59.1 us  [the longest x1 59.1 us: per_device(): lax.all_gather(jnp.concatenate([w_query, w_outgate] + keys_w + values_w +...]
    pallas_call x0 -> x2, Pallas kernels: none -> 78.7 us  [the longest x1 42.4 us: mixer_bwd(): pl.pallas_call(functools.partial(mixer_bwd_kernel, heads), out_shape=(sha...]
    psum x3, waiting for transfers between devices: 131 us -> 66.7 us  [the longest x1 35.1 us: per_device(): lax.psum((product(gate_back, gate_w, NT) + product(up_back, up_w, NT)).as...]
    all_gather x2 -> x0, blocking collectives: 42.2 us -> none  [the longest x1 24.8 us: per_device(): lax.all_gather(w_beta, 'dp', axis=1, tiled=True)]
    squeeze x49 -> x0, local copies, waits for them, and re-layouts: 36.7 us -> none  [the longest x48 36.7 us: head_sequence(): lax.scan(jax.checkpoint(block_pass), initial, (queries.reshape(blocks, ST...]
  transfers between devices with their start and end apart: 27 -> 14, of which waited for: 20 -> 7; matrix products, arithmetic and copies ran while one was open for 27% -> 17% of each run, Pallas kernels for 0% -> 5%
where the time goes in v1:
time: 671 us; the launch traced here: 660 us
  waiting for transfers between devices  242 us (36%)
  blocking collectives  102 us (15%)
  other arithmetic  86.1 us (13%)
  Pallas kernels  78.7 us (12%)
  matrix products  67.6 us (10%)
  local copies, waits for them, and re-layouts  57.6 us (9%)
  between operations  15.7 us (2%)
  starting transfers between devices  11 us (2%)
    reduce_scatter x1, waiting for transfers between devices, per_device(): lax.psum_scatter(jnp.concatenate([grad_out, grad_gate, grad_up, grad_down...  105 us
    dot_general x15, matrix products, product(): lax.dot_general(first, second, (dims, ((), ())), preferred_element_type=F32)  67.6 us
    psum x1, blocking collectives, per_device(): lax.psum((grad_norm_gain, d_log, d_bias, d_cq, d_k0, d_k1, d_v0, d_v1, gr...  62.1 us
    all_gather x1, waiting for transfers between devices, per_device(): lax.all_gather(jnp.concatenate([w_query, w_outgate] + keys_w + values_w +...  59.1 us
    pallas_call x1, Pallas kernels, mixer_bwd(): pl.pallas_call(functools.partial(mixer_bwd_kernel, heads), out_shape=(sha...  42.4 us
    psum x1, blocking collectives, per_device(): sum_mix_gain = lax.psum(dgain[0], ('dp', 'step'))  39.7 us
    pallas_call x1, Pallas kernels, mixer_fwd(): pl.pallas_call(functools.partial(mixer_fwd_kernel, heads), out_shape=(sha...  36.3 us
    psum x1, waiting for transfers between devices, per_device(): lax.psum((product(gate_back, gate_w, NT) + product(up_back, up_w, NT)).as...  35.1 us
  transfers between devices with their start and end apart: 14, of which 7 were waited for; matrix products, arithmetic and copies ran while one was open for 17% of the time, Pallas kernels for 5%

profile of v1, /device:TPU:0, one launch (start us, length us, event | category | flops | bytes accessed | tf_op | source)
XLA Modules:
  0.0 660.5 jit_solution(18392202129368969508)
XLA Ops:
  9.2 3.0 collective-permute-start
  13.1 2.9 collective-permute-done
  17.1 1.7 concatenate.146
  19.9 1.8 collective-permute-start.1
  24.8 59.1 %all-gather.3.cloned.1.call-done = bf16[1024,3200]{1,0:T(8,128)(2,1)} async-done(((bf16[64,3200]{1,0:T(8,128)(2,1)}), bf16[1024,3200]{1,0:T(8,128)(2,1)}) %all-gather.3.cloned.1.call-update) | async-done | bytes 6553616 | tf_op jit(solution)/shard_map/all_gather | solution.py:433
  83.8 6.4 fusion.90
  90.2 2.5 fusion.124
  94.9 1.8 fusion.114
  96.8 2.9 mul.1022
  99.7 1.9 reduce_sum.324
  102.5 5.3 fusion.78
  107.9 1.6 reshape.606
  111.1 2.6 reshape.607
  113.7 1.9 multiply_reduce_fusion.23
  116.6 1.7 fusion.99
  118.3 1.9 broadcast_multiply_fusion
  121.0 2.0 concatenate.149.aux_ref
  123.0 5.2 fusion.87
  134.0 36.3 %mixer_forward.1 = (bf16[512,512]{1,0:T(8,128)(2,1)S(1)}, f32[512,512]{1,0:T(8,128)S(1)}, f32[32,128,128]{2,1,0:T(8,128)}, f32[36,128,128]{2,1,0:T(8,128)}, f32[32,128,128]{2,1,0:T(8,128)}) custom-call(f32[512,512]{1,0:T(8,128)S(1)} %fusion.76.q_ref, bf16[2,512,512]{2,1,0:T(8,128)(2,1)S(1)} %pad_maximum_fusion.4.k_ref, ...), custom_call_target="tpu_custom_call" | custom-call | tf_op jit(solution)/shard_map/mixer_forward/pallas_call | solution.py:294
  172.1 3.2 convolution_convert_fusion.5
  176.2 5.9 fusion.2
  182.2 31.6 %all-reduce.67.cloned.1.call-done = bf16[512,1024]{1,0:T(8,128)(2,1)} async-done(((bf16[512,1024]{1,0:T(8,128)(2,1)}), bf16[512,1024]{1,0:T(8,128)(2,1)}) %all-reduce.67.cloned.1.call-update) | async-done | bytes 1048592 | tf_op jit(solution)/shard_map/psum | solution.py:479
  213.8 1.7 multiply_reduce_fusion
  216.0 4.0 fusion.8
  220.0 6.0 multiply_convert_fusion.1
  226.1 1.8 fusion.6
  228.0 2.8 add_convert_fusion
  230.9 5.1 fusion.29
  235.9 35.1 %all-reduce.69.cloned.1.call-done = bf16[512,1024]{1,0:T(8,128)(2,1)} async-done(((bf16[512,1024]{1,0:T(8,128)(2,1)}), bf16[512,1024]{1,0:T(8,128)(2,1)}) %all-reduce.69.cloned.1.call-update) | async-done | bytes 1048592 | tf_op jit(solution)/shard_map/psum | solution.py:498
  271.0 2.9 fusion.20
  274.0 3.9 fusion.80.dgated_ref
  277.9 42.4 %mixer_backward.1 = (f32[512,512]{1,0:T(8,128)S(1)}, bf16[2,512,512]{2,1,0:T(8,128)(2,1)S(1)}, bf16[2,512,512]{2,1,0:T(8,128)(2,1)S(1)}, f32[512,128]{1,0:T(8,12...) custom-call(f32[512,512]{1,0:T(8,128)S(1)} %fusion.76.q_ref, bf16[2,512,512]{2,1,0:T(8,128)(2,1)} %copy-done.2, ...), custom_call_target="tpu_custom_call" | custom-call | tf_op jit(solution)/shard_map/mixer_backward/pallas_call | solution.py:315
  320.4 1.9 fusion.92
  322.3 2.5 fusion.122
  324.8 1.6 convert_element_type.218
  326.4 1.6 fusion.125
  328.0 1.6 convert_element_type.217
  331.3 2.6 reduce_sum.343
  337.2 3.0 multiply_reduce_fusion.22
  342.1 2.5 unstack.37
  344.6 2.6 multiply_reduce_fusion.21
  348.4 1.7 broadcast_in_dim.35
  350.8 8.2 %multiply_reduce_fusion.20 = (f32[512]{0:T(512)S(1)}, f32[512]{0:T(512)}, f32[512]{0:T(512)}, f32[512]{0:T(512)S(1)}, f32[512]{0:T(512)S(1)}, /*index=5*/f32[512...) fusion(f32[512,512]{1,0:T(8,128)} %copy-done.22, ...), kind=kLoop, calls=%fused_computation.179 | loop fusion | flops 17034752 | bytes 16801792 | tf_op jit(solution)/shard_map/transpose(jvp())/reduce_sum | solution.py:360
  361.9 3.1 multiply_reduce_fusion.5
  365.0 1.5 multiply_multiply_fusion
  369.5 1.4 copy-done.38
  372.5 4.7 convolution_convert_fusion.6
  378.4 8.2 %convolution_convert_fusion = bf16[1024,3200]{1,0:T(8,128)(2,1)} fusion(bf16[512,2176]{1,0:T(8,128)(2,1)} %copy-done.38, bf16[512,512]{1,0:T(8,128)(2,1)S(1)} %copy-done.8, bf16[512,512]{1,0:T(8,128)(2,1)S(1)} %add_convert_fusion.2, bf16[1,512,1024]{2,1,0:T(8,128)(2,1)S(1)} %copy-done.11, f32[1024]{0:T(1024)S(1)} %copy-done.58, f32[512]{0:T(512)S(1)} %fusion.109), kind=kOutput, calls=%fused_computation.1 | convolution fusion | flops 3370647552 | bytes 10885120 | tf_op jit(solution)/shard_map/dot_general | solution.py:337
  387.8 5.6 convolution_convert_fusion.1
  393.4 3.5 convolution_convert_fusion.3
  396.9 3.4 convolution_convert_fusion.2
  400.4 3.0 convolution_convert_fusion.4
  403.4 2.3 copy.125
  405.7 9.1 %pad_maximum_fusion = bf16[1024,4736]{1,0:T(8,128)(2,1)} fusion(bf16[1024,1408]{1,0:T(8,128)(2,1)} %convolution_convert_fusion.1, bf16[1024,1408]{1,0:T(8,128)(2,1)} %convolution_convert_fusion.2, bf16[1024,1408]{1,0:T(8,128)(2,1)} %convolution_convert_fusion.3, bf16[1024,512]{1,0:T(8,128)(2,1)} %copy.125), kind=kLoop, calls=%fused_computation | loop fusion | flops 38797312 | bytes 19398656 | tf_op jit(solution)/shard_map/concatenate | solution.py:506
  414.9 39.7 %psum.110 = f32[128]{0:T(128)} all-reduce(f32[128]{0:T(128)S(1)} %bitcast.236), channel_id=1, replica_groups=mesh['dp'=16,'step'=2] {'dp','step'}, use_global_device_ids=true, to_apply=%region_49.50 | all-reduce | flops 128 | bytes 1024 | tf_op jit(solution)/shard_map/psum | solution.py:540
  454.8 2.3 fusion.21
  457.1 62.1 %all-reduce.61 = (f32[1024]{0:T(1024)}, f32[4]{0:T(128)}, f32[4]{0:T(128)}, f32[4,512]{1,0:T(4,128)}, f32[4,512]{1,0:T(4,128)S(1)}, /*index=5*/f32[4,512]{1,0:T(...) all-reduce(f32[1024]{0:T(1024)S(1)} %get-tuple-element.184, ...), channel_id=1, replica_groups=mesh['dp'=16,'step'=2] {'dp'}, use_global_device_ids=true, to_apply=%region_18.19 | all-reduce | flops 12296 | bytes 98368 | tf_op jit(solution)/shard_map/psum | solution.py:536
  521.3 4.9 fusion.73
  527.5 5.8 reduce-scatter.3.cloned.1.call-done
  534.2 1.5 collective-permute-start.4
  535.7 1.7 select_bitcast_fusion
  538.8 1.5 collective-permute-start.3
  540.9 2.2 collective-permute-done.3
  544.6 105.0 %reduce-scatter.5.cloned.1.call-done = bf16[64,4736]{1,0:T(8,128)(2,1)} async-done(((bf16[1024,4736]{1,0:T(8,128)(2,1)}), bf16[64,4736]{1,0:T(8,128)(2,1)}) %reduce-scatter.5.cloned.1.call-update) | async-done | bytes 606224 | tf_op jit(solution)/shard_map/reduce_scatter | solution.py:505
  (302 shorter events, 53.1 us)
Async XLA Ops:
  7.2 11.7 %copy-start.52 = (bf16[1408,64]{0,1:T(8,128)(2,1)S(1)}, bf16[1408,64]{0,1:T(8,128)(2,1)}, u32[]{:S(2)}) copy-start(bf16[1408,64]{0,1:T(8,128)(2,1)} %param.43) | copy-start | bytes 540676
  7.2 11.7 %copy-start.53 = (bf16[64,1408]{1,0:T(8,128)(2,1)S(1)}, bf16[64,1408]{1,0:T(8,128)(2,1)}, u32[]{:S(2)}) copy-start(bf16[64,1408]{1,0:T(8,128)(2,1)} %param.42) | copy-start | bytes 540676
  7.2 11.7 %copy-start.54 = (bf16[64,1408]{1,0:T(8,128)(2,1)S(1)}, bf16[64,1408]{1,0:T(8,128)(2,1)}, u32[]{:S(2)}) copy-start(bf16[64,1408]{1,0:T(8,128)(2,1)} %param.41) | copy-start | bytes 540676
  7.2 11.7 %copy-start.55 = (bf16[512,64]{0,1:T(8,128)(2,1)S(1)}, bf16[512,64]{0,1:T(8,128)(2,1)}, u32[]{:S(2)}) copy-start(bf16[512,64]{0,1:T(8,128)(2,1)} %param.39) | copy-start | bytes 196612
  7.2 76.6 %all-gather.3.cloned.1.call-start = ((), (), s32[]{:S(2)}) async-start(), calls=%async_computation.2 | async-start | bytes 6963200 | tf_op jit(solution)/shard_map/all_gather | solution.py:433
  9.1 10.7 %copy-start.60 = (f32[1,4,1024]{2,1,0:T(4,128)S(1)}, f32[1,4,1024]{2,1,0:T(4,128)}, u32[]{:S(2)}) copy-start(f32[1,4,1024]{2,1,0:T(4,128)} %param.37) | copy-start | bytes 49156
  9.2 10.7 %copy-start.61 = (f32[1,4,1024]{2,1,0:T(4,128)S(1)}, f32[1,4,1024]{2,1,0:T(4,128)}, u32[]{:S(2)}) copy-start(f32[1,4,1024]{2,1,0:T(4,128)} %param.36) | copy-start | bytes 49156
  9.2 12.5 %copy-start.57 = (s32[1,512]{1,0:T(1,128)S(1)}, s32[1,512]{1,0:T(1,128)}, u32[]{:S(2)}) copy-start(s32[1,512]{1,0:T(1,128)} %param.25) | copy-start | bytes 6148
  9.2 12.8 %copy-start.9 = (bf16[1,512,1024]{2,1,0:T(8,128)(2,1)S(1)}, bf16[1,512,1024]{2,1,0:T(8,128)(2,1)}, u32[]{:S(2)}) copy-start(bf16[1,512,1024]{2,1,0:T(8,128)(2,1)} %param.22) | copy-start | bytes 3145732
  9.2 6.9 %collective-permute-start = (bf16[64,1028]{1,0:T(8,128)(2,1)S(1)}, bf16[64,1028]{1,0:T(8,128)(2,1)S(1)}, u32[]{:S(2)}, u32[]{:S(2)}) collective-permute-start(bf16[64,1028]{1,0:T(8,128)(2,1)S(1)} %pad_maximum_fusion.7), channel_id=1, source_target_pairs={{0,1},{1,0},{2,3},{3,2},{4,5},{5,4},{6,7},{7,6},{8,9},{9,8},{10,11... | collective-permute-start | bytes 394760 | tf_op jit(solution)/shard_map/ppermute | solution.py:412
  17.0 5.4 copy-start.64
  17.0 5.4 copy-start.74
  18.8 65.0 %copy-start.58 = (f32[1024]{0:T(1024)S(1)}, f32[1024]{0:T(1024)}, u32[]{:S(2)}) copy-start(f32[1024]{0:T(1024)} %param.26) | copy-start | bytes 12292
  18.8 153.3 %all-gather.5.cloned.1.call-start = ((), (), s32[]{:S(2)}) async-start(), calls=%async_computation.3 | async-start | bytes 10305536 | tf_op jit(solution)/shard_map/all_gather | solution.py:437
  19.8 194.0 %all-reduce.67.cloned.1.call-start = ((), (), s32[]{:S(2)}) async-start(), calls=%async_computation.4 | async-start | bytes 2097152 | tf_op jit(solution)/shard_map/psum | solution.py:479
  19.9 4.8 collective-permute-start.1
  90.2 3.8 copy-start.12
  94.0 8.6 %copy-start.17 = (f32[512,512]{1,0:T(8,128)}, f32[512,512]{1,0:T(8,128)S(1)}, u32[]{:S(2)}) copy-start(f32[512,512]{1,0:T(8,128)S(1)} %get-tuple-element.230) | copy-start | bytes 3145732
  94.0 40.1 %copy-start = (f32[512,512]{1,0:T(8,128)}, f32[512,512]{1,0:T(8,128)S(1)}, u32[]{:S(2)}) copy-start(f32[512,512]{1,0:T(8,128)S(1)} %get-tuple-element.227.gate_ref) | copy-start | bytes 3145732
  96.8 36.3 %copy-start.13 = (f32[512,512]{1,0:T(8,128)}, f32[512,512]{1,0:T(8,128)S(1)}, u32[]{:S(2)}) copy-start(f32[512,512]{1,0:T(8,128)S(1)} %get-tuple-element.225) | copy-start | bytes 3145732
  111.1 7.2 %copy-start.68 = (f32[4]{0:T(128)S(1)}, f32[4]{0:T(128)}, u32[]{:S(2)}) copy-start(f32[4]{0:T(128)} %param.34) | copy-start | bytes 52
  111.1 7.2 %copy-start.70 = (f32[4]{0:T(128)S(1)}, f32[4]{0:T(128)}, u32[]{:S(2)}) copy-start(f32[4]{0:T(128)} %exponential_negate_fusion) | copy-start | bytes 52
  113.7 9.3 %copy-start.24 = (f32[512,512]{1,0:T(8,128)S(1)}, f32[512,512]{1,0:T(8,128)}, u32[]{:S(2)}) copy-start(f32[512,512]{1,0:T(8,128)} %get-tuple-element.228) | copy-start | bytes 3145732
  128.3 5.7 copy-start.1
  172.1 4.1 copy-start.39
  175.3 95.7 %all-reduce.69.cloned.1.call-start = ((), (), s32[]{:S(2)}) async-start(), calls=%async_computation.5 | async-start | bytes 2097152 | tf_op jit(solution)/shard_map/psum | solution.py:498
  176.2 37.6 %copy-start.10 = (bf16[1,512,1024]{2,1,0:T(8,128)(2,1)S(1)}, bf16[1,512,1024]{2,1,0:T(8,128)(2,1)}, u32[]{:S(2)}) copy-start(bf16[1,512,1024]{2,1,0:T(8,128)(2,1)} %param.22) | copy-start | bytes 3145732
  182.2 33.4 %copy-start.56 = (f32[1024]{0:T(1024)S(1)}, f32[1024]{0:T(1024)}, u32[]{:S(2)}) copy-start(f32[1024]{0:T(1024)} %param.40) | copy-start | bytes 12292
  215.9 4.1 copy-start.49
  216.0 4.1 copy-start.76
  216.0 10.1 %slice-start.2 = ((s8[9699328]{0:T(1024)(128)(4,1)}), s8[4194304]{0:T(1024)(128)(4,1)S(1)}, s32[]{:S(2)}) async-start(s8[9699328]{0:T(1024)(128)(4,1)} %bitcast.318), calls=%async_computation.11 | async-start | bytes 8388608
  220.0 6.1 slice-start.3
  220.0 6.1 slice-start.4
  230.8 223.9 %all-reduce.71.cloned.1.call-start = ((), (), s32[]{:S(2)}) async-start(), calls=%async_computation.8 | async-start | bytes 4194304 | tf_op jit(solution)/shard_map/psum | solution.py:487
  273.9 3.9 copy-start.65
  277.9 44.4 %copy-start.69 = (f32[4]{0:T(128)S(1)}, f32[4]{0:T(128)}, u32[]{:S(2)}) copy-start(f32[4]{0:T(128)} %param.34) | copy-start | bytes 52
  277.9 44.4 %copy-start.71 = (f32[4]{0:T(128)S(1)}, f32[4]{0:T(128)}, u32[]{:S(2)}) copy-start(f32[4]{0:T(128)} %exponential_negate_fusion) | copy-start | bytes 52
  320.3 6.0 copy-start.7
  331.3 4.6 copy-start.36
  337.2 7.5 %copy-start.29 = (f32[512,4,128]{2,1,0:T(4,128)S(1)}, f32[512,4,128]{2,1,0:T(4,128)}, u32[]{:S(2)}) copy-start(f32[512,4,128]{2,1,0:T(4,128)} %copy-done.28) | copy-start | bytes 3145732
  350.8 9.4 %slice-start = ((s8[6553600]{0:T(1024)(128)(4,1)}), s8[4194304]{0:T(1024)(128)(4,1)S(1)}, s32[]{:S(2)}) async-start(s8[6553600]{0:T(1024)(128)(4,1)} %bitcast.237), calls=%async_computation.9 | async-start | bytes 8388608
  350.8 8.6 %copy-start.43 = (f32[512,4]{1,0:T(8,128)S(1)}, f32[512,4]{1,0:T(8,128)}, u32[]{:S(2)}) copy-start(f32[512,4]{1,0:T(8,128)} %get-tuple-element.215) | copy-start | bytes 24580
  350.8 8.6 %copy-start.44 = (f32[512,8]{1,0:T(8,128)S(1)}, f32[512,8]{1,0:T(8,128)}, u32[]{:S(2)}) copy-start(f32[512,8]{1,0:T(8,128)} %fusion.92) | copy-start | bytes 49156
  350.8 8.7 %copy-start.46 = (f32[512,4]{1,0:T(8,128)S(1)}, f32[512,4]{1,0:T(8,128)}, u32[]{:S(2)}) copy-start(f32[512,4]{1,0:T(8,128)} %copy.116) | copy-start | bytes 24580
  350.8 9.3 %slice-start.1 = ((s8[6553600]{0:T(1024)(128)(4,1)}), s8[2359296]{0:T(1024)(128)(4,1)S(1)}, s32[]{:S(2)}) async-start(s8[6553600]{0:T(1024)(128)(4,1)} %bitcast.237), calls=%async_computation.10 | async-start | bytes 4718592
  350.8 9.3 %copy-start.35 = (f32[512,512]{1,0:T(8,128)S(1)}, f32[512,512]{1,0:T(8,128)}, u32[]{:S(2)}) copy-start(f32[512,512]{1,0:T(8,128)} %get-tuple-element.314) | copy-start | bytes 3145732
  377.2 156.0 %reduce-scatter.3.cloned.1.call-start = ((), (), s32[]{:S(2)}) async-start(), calls=%async_computation.6 | async-start | bytes 6963200 | tf_op jit(solution)/shard_map/reduce_scatter | solution.py:523
  386.6 6.8 %copy-start.50 = (bf16[512,1024]{1,0:T(8,128)(2,1)S(1)}, bf16[512,1024]{1,0:T(8,128)(2,1)}, u32[]{:S(2)}) copy-start(bf16[512,1024]{1,0:T(8,128)(2,1)} %copy-done.49) | copy-start | bytes 3145732
  386.6 263.0 %reduce-scatter.5.cloned.1.call-start = ((), (), s32[]{:S(2)}) async-start(), calls=%async_computation.7 | async-start | bytes 10305536 | tf_op jit(solution)/shard_map/reduce_scatter | solution.py:505
  387.8 5.6 copy-start.80
  393.4 3.5 copy-start.51
  393.4 3.5 copy-start.78
  396.9 3.5 copy-start.16
  414.9 39.7 %copy-start.62 = (f32[512]{0:T(512)S(1)}, f32[512]{0:T(512)}, u32[]{:S(2)}) copy-start(f32[512]{0:T(512)} %get-tuple-element.182) | copy-start | bytes 6148
  414.9 39.7 %copy-start.63 = (f32[512]{0:T(512)S(1)}, f32[512]{0:T(512)}, u32[]{:S(2)}) copy-start(f32[512]{0:T(512)} %get-tuple-element.183) | copy-start | bytes 6148
  414.9 39.8 %copy-start.72 = (f32[4]{0:T(128)S(1)}, f32[4]{0:T(128)}, u32[]{:S(2)}) copy-start(f32[4]{0:T(128)} %get-tuple-element.226) | copy-start | bytes 52
  414.9 39.8 %copy-start.75 = (f32[4]{0:T(128)S(1)}, f32[4]{0:T(128)}, u32[]{:S(2)}) copy-start(f32[4]{0:T(128)} %param.33) | copy-start | bytes 52
  414.9 42.2 %copy-start.59 = (f32[1024]{0:T(1024)S(1)}, f32[1024]{0:T(1024)}, u32[]{:S(2)}) copy-start(f32[1024]{0:T(1024)} %get-tuple-element.167) | copy-start | bytes 12292
  414.9 42.2 %copy-start.67 = (f32[4]{0:T(128)S(1)}, f32[4]{0:T(128)}, u32[]{:S(2)}) copy-start(f32[4]{0:T(128)} %get-tuple-element.214) | copy-start | bytes 52
  519.2 7.0 %collective-permute-start.6 = (f32[4,512]{1,0:T(4,128)S(1)}, f32[4,512]{1,0:T(4,128)S(1)}, u32[]{:S(2)}, u32[]{:S(2)}) collective-permute-start(f32[4,512]{1,0:T(4,128)S(1)} %get-tuple-element.279), channel_id=1, source_target_pairs={{0,1},{1,0},{2,3},{3,2},{4,5},{5,4},{6,7},{7,6},{8,9},{9,8},{10,11... | collective-permute-start | bytes 24584 | tf_op jit(solution)/shard_map/ppermute | solution.py:412
  519.9 6.9 %collective-permute-start.5 = (f32[4,512]{1,0:T(4,128)S(1)}, f32[4,512]{1,0:T(4,128)S(1)}, u32[]{:S(2)}, u32[]{:S(2)}) collective-permute-start(f32[4,512]{1,0:T(4,128)S(1)} %get-tuple-element.281), channel_id=1, source_target_pairs={{0,1},{1,0},{2,3},{3,2},{4,5},{5,4},{6,7},{7,6},{8,9},{9,8},{10,11... | collective-permute-start | bytes 24584 | tf_op jit(solution)/shard_map/ppermute | solution.py:412
  534.2 6.0 collective-permute-start.4
  538.2 5.7 collective-permute-start.2
  538.8 4.4 collective-permute-start.3
  (38 other events, 77.6 us)
Sparse Core Ops, SparseCore 0:
  18.9 64.8 all-gather.2
  86.1 81.6 all-gather.4
  175.5 38.2 all-reduce.66
  230.9 40.0 all-reduce.68
  377.4 63.7 all-reduce.70
  445.5 87.7 reduce-scatter.2
  537.4 112.1 reduce-scatter.4

commit v2 on v1

--- a/solution.py
+++ b/solution.py
@@ -109,70 +109,6 @@
         level += 1
     rest = [eye - x - dot3(a, x) for a, x in zip(mats, out)]
     return [x + dot1(x, r) for x, r in zip(out, rest)]
-
-
-def mixer_fwd_kernel(heads, q_ref, k_ref, v_ref, aux_ref, gate_ref, gain_ref,
-                     gated_ref, mixed_ref, inv_ref, state_ref, pseudo_ref, attn_ref):
-    blocks = q_ref.shape[0] // STRETCH
-    span = 2 * STRETCH
-    masks = block_masks()
-    t_row, t_col, p_row, p_col = masks
-
-    def keys_of(rows, cols):
-        return jnp.concatenate([k_ref[0, rows, cols], k_ref[1, rows, cols]], axis=0)
-
-    def prepare(block, carry):
-        rows = pl.ds(pl.multiple_of(block * STRETCH, STRETCH), STRETCH)
-        aux = aux_ref[rows, :]
-        aux2, run2, aux_t, run_t = block_scalars(aux)
-        mats = []
-        for head in range(heads):
-            cols = slice(head * DK, (head + 1) * DK)
-            beta, run_col, run_row, doc_col, doc_row, carried, to_last = head_terms(
-                aux, aux2, run2, aux_t, run_t, head, heads
-            )
-            decay = decay_matrix(run_col, run_row, doc_col, doc_row, p_row, p_col)
-            keys = keys_of(rows, cols)
-            gram = dot1(keys, keys, NT)
-            mats.append(beta * jnp.where(p_row > p_col, decay * gram, 0.0))
-            attn_ref[block * heads + head] = decay[STRETCH:] * dot3(q_ref[rows, cols], keys, NT)
-        for head, inv in enumerate(inverse(mats, masks)):
-            inv_ref[block * heads + head] = inv
-        return carry
-
-    lax.fori_loop(0, blocks, prepare, 0)
-    for head in range(heads):
-        state_ref[head] = jnp.zeros((DK, DK), F32)
-
-    def advance(block, carry):
-        rows = pl.ds(pl.multiple_of(block * STRETCH, STRETCH), STRETCH)
-        aux = aux_ref[rows, :]
-        aux2, run2, aux_t, run_t = block_scalars(aux)
-        for head in range(heads):
-            cols = slice(head * DK, (head + 1) * DK)
-            beta, run_col, run_row, doc_col, doc_row, carried, to_last = head_terms(
-                aux, aux2, run2, aux_t, run_t, head, heads
-            )
-            keys = keys_of(rows, cols)
-            values = jnp.concatenate([v_ref[0, rows, cols], v_ref[1, rows, cols]], axis=0).astype(F32)
-            state = state_ref[block * heads + head]
-            state_parts = split(state)
-            target = beta * (values - carried * dot3(keys, state_parts))
-            pseudo = dot3(inv_ref[block * heads + head], target)
-            pseudo_ref[block * heads + head] = pseudo
-            mixed = carried[STRETCH:] * dot3(q_ref[rows, cols], state_parts) + dot3(
-                attn_ref[block * heads + head], pseudo
-            )
-            state_ref[(block + 1) * heads + head] = carried[span - 1 : span] * state + dot3(
-                keys, to_last * pseudo, TN
-            )
-            mixed_ref[rows, cols] = mixed
-            scale = lax.rsqrt(jnp.mean(mixed * mixed, axis=-1, keepdims=True) + 1e-05)
-            gate = gate_ref[rows, cols]
-            gated_ref[rows, cols] = (mixed * scale * gain_ref[...] * (gate * jax.nn.sigmoid(gate))).astype(BF)
-        return carry
-
-    lax.fori_loop(0, blocks, advance, 0)
 
 
 def mixer_bwd_kernel(heads, q_ref, k_ref, v_ref, aux_ref, gate_ref, gain_ref, mixed_ref, inv_ref,
@@ -285,29 +221,6 @@
 VMEM = pl.BlockSpec(memory_space=pltpu.VMEM)
 
 
-def mixer_fwd(q, k, v, aux, gate, gain):
-    seq, width = q.shape
-    heads, blocks = width // DK, seq // STRETCH
-    units = heads * blocks
-    span = 2 * STRETCH
-    shape = jax.ShapeDtypeStruct
-    return pl.pallas_call(
-        functools.partial(mixer_fwd_kernel, heads),
-        out_shape=(
-            shape((seq, width), BF),
-            shape((seq, width), F32),
-            shape((units, span, span), F32),
-            shape((units + heads, DK, DK), F32),
-            shape((units, span, DK), F32),
-        ),
-        in_specs=[VMEM] * 6,
-        out_specs=(VMEM,) * 5,
-        scratch_shapes=[pltpu.VMEM((units, STRETCH, span), F32)],
-        compiler_params=pltpu.CompilerParams(vmem_limit_bytes=48 << 20),
-        name="mixer_forward",
-    )(q, k, v, aux, gate, gain)
-
-
 def mixer_bwd(q, k, v, aux, gate, gain, mixed, inv, state, pseudo, dgated):
     seq, width = q.shape
     heads = width // DK
@@ -328,6 +241,464 @@
         compiler_params=pltpu.CompilerParams(vmem_limit_bytes=48 << 20),
         name="mixer_backward",
     )(q, k, v, aux, gate, gain, mixed, inv, state, pseudo, dgated)
+
+
+MESH = pl.DeviceIdType.MESH
+
+
+class Place:
+    def __init__(self, line):
+        self.line = line
+        self.dp, self.side = lax.axis_index("dp"), lax.axis_index("step")
+        self.z, self.x, self.c = self.dp // 4, (self.dp // 2) % 2, self.dp % 2
+        self.sibling = (self.dp + 1 - 2 * self.c, self.side)
+        self.across = (self.dp + 2 - 4 * self.x, self.side)
+        self.ahead = (
+            (lax.rem(self.dp + 4, 4 * line), self.side),
+            (lax.rem(self.dp + 4 * line - 4, 4 * line), self.side),
+        )
+        self.peer = (self.dp, 1 - self.side)
+        self.can_send = (self.z + 1 < line, self.z > 0)
+
+    def reaches(self, way, far):
+        return self.z - far >= 0 if way == 0 else self.z + far < self.line
+
+    def behind(self, way, far):
+        return self.dp - 4 * far if way == 0 else self.dp + 4 * far
+
+    def enter(self, plane=True, peer=True):
+        barrier = pltpu.get_barrier_semaphore()
+
+        def greet(device):
+            pl.semaphore_signal(barrier, inc=1, device_id=device, device_id_type=MESH)
+
+        count = 0
+        if peer:
+            greet(self.peer)
+            count = 1
+        if plane:
+            greet(self.sibling)
+            greet(self.across)
+            for way in (0, 1):
+                pl.when(self.can_send[way])(functools.partial(greet, self.ahead[way]))
+            count = count + 2 + self.can_send[0].astype(jnp.int32) + self.can_send[1].astype(jnp.int32)
+        pl.semaphore_wait(barrier, count)
+
+
+def remote(src, dst, send_sem, recv_sem, device):
+    return pltpu.make_async_remote_copy(
+        src_ref=src, dst_ref=dst, send_sem=send_sem, recv_sem=recv_sem,
+        device_id=device, device_id_type=MESH,
+    )
+
+
+def gather_sems(line, parts):
+    dma = pltpu.SemaphoreType.DMA
+    return [
+        dma((2, line, parts)), dma((2, line, parts)),
+        dma((2, line, parts)), dma((2, line, parts)),
+        dma((2, 2, line, parts)), dma((2, 2, line, parts)),
+    ]
+
+
+class Gather:
+    def __init__(self, place, buf, cuts, sems):
+        self.place, self.buf, self.cuts = place, buf, cuts
+        self.zs, self.zr, self.xs, self.xr, self.cs, self.cr = sems
+
+    def block(self, index, part):
+        start, width = self.cuts[part]
+        return self.buf.at[index, :, pl.ds(start, width)]
+
+    def line_copy(self, index, way, far, part):
+        ref = self.block(index, part)
+        return remote(ref, ref, self.zs.at[way, far, part], self.zr.at[way, far, part], self.place.ahead[way])
+
+    def across_copy(self, index, way, far, part):
+        ref = self.block(index, part)
+        return remote(ref, ref, self.xs.at[way, far, part], self.xr.at[way, far, part], self.place.across)
+
+    def sibling_copy(self, index, column, way, far, part):
+        ref = self.block(index, part)
+        return remote(
+            ref, ref, self.cs.at[column, way, far, part], self.cr.at[column, way, far, part], self.place.sibling
+        )
+
+    def spread(self, index, way, far, part):
+        place = self.place
+        for to in (0, 1) if far == 0 else (way,):
+            pl.when(place.can_send[to])(lambda to=to: self.line_copy(index, to, far + 1, part).start())
+        self.across_copy(index, way, far, part).start()
+        self.sibling_copy(index, 0, way, far, part).start()
+
+    def ways(self, far):
+        return (0,) if far == 0 else (0, 1)
+
+    def each(self, far, act):
+        if far == 0:
+            act(0)
+            return
+        for way in (0, 1):
+            pl.when(self.place.reaches(way, far))(functools.partial(act, way))
+
+    def step(self, far, part):
+        place = self.place
+        if far == 0:
+            self.spread(place.dp, 0, 0, part)
+            return
+
+        def from_line(way):
+            index = place.behind(way, far)
+            self.line_copy(index, way, far, part).wait_recv()
+            self.spread(index, way, far, part)
+
+        def from_across(way):
+            index = place.behind(way, far - 1) + 2 - 4 * place.x
+            self.across_copy(index, way, far - 1, part).wait_recv()
+            self.sibling_copy(index, 1, way, far - 1, part).start()
+
+        if far < place.line:
+            self.each(far, from_line)
+        self.each(far - 1, from_across)
+
+    def steps(self):
+        return [
+            functools.partial(self.step, far, part)
+            for far in range(self.place.line + 1)
+            for part in range(len(self.cuts))
+        ]
+
+    def ready(self, part):
+        place = self.place
+        for far in range(place.line):
+            for column in (0, 1):
+
+                def from_sibling(way):
+                    index = place.behind(way, far) + 1 - 2 * place.c + column * (2 - 4 * place.x)
+                    self.sibling_copy(index, column, way, far, part).wait_recv()
+
+                self.each(far, from_sibling)
+
+    def drain(self, part):
+        place = self.place
+        for far in range(place.line):
+
+            def sent(way):
+                index = place.behind(way, far)
+                for to in (0, 1) if far == 0 else (way,):
+                    pl.when(place.can_send[to])(
+                        lambda to=to: self.line_copy(index, to, far + 1, part).wait_send()
+                    )
+                self.across_copy(index, way, far, part).wait_send()
+                self.sibling_copy(index, 0, way, far, part).wait_send()
+                self.sibling_copy(index + 2 - 4 * place.x, 1, way, far, part).wait_send()
+
+            self.each(far, sent)
+
+
+def run_slot(slots, turn):
+    for index, steps in enumerate(slots):
+        if steps:
+
+            def go(steps=steps):
+                for step in steps:
+                    step()
+
+            pl.when(turn == index)(go)
+
+
+def deal(steps, turns):
+    return [steps[len(steps) * i // turns : len(steps) * (i + 1) // turns] for i in range(turns)]
+
+
+KW = 4
+PAD = 8
+
+
+def conv_window(window, kernel, same):
+    rows = window.shape[0] - PAD
+    out = window[PAD:] * kernel[0:1]
+    for offset in range(1, KW):
+        out = out + jnp.where(same[offset - 1], window[PAD - offset : PAD - offset + rows], 0.0) * kernel[offset : offset + 1]
+    return out
+
+
+def same_documents(window):
+    rows = window.shape[0] - PAD
+    return [window[PAD:] == window[PAD - offset : PAD - offset + rows] for offset in range(1, KW)]
+
+
+def rows_of(ref, block, count, extra=0):
+    return ref[pl.ds(pl.multiple_of(block * STRETCH, STRETCH), count + extra), :]
+
+
+def scalar_select(side, heads):
+    src, dst = iota((DK, DK), 0), iota((DK, DK), 1)
+    kind, head = dst // heads, dst % heads
+    first = jnp.where(kind == side, 0, 2 * heads)
+    source = jnp.where(kind < 2, first + side * heads + head, 4 * heads + head)
+    return ((src == source) & (kind < 3)).astype(F32)
+
+
+def softplus(values):
+    return jnp.maximum(values, 0.0) + jnp.log1p(jnp.exp(-jnp.abs(values)))
+
+
+def front_kernel(
+    line, heads, x_ref, docs_ref, norm_ref, wq_ref, wg_ref, wk_ref, wv_ref, scal_ref, rest_ref, rates_ref,
+    cq_ref, ck_ref, cv_ref, mix_ref,
+    gated_ref, mixed_ref, inv_ref, state_ref, pseudo_ref, pre_ref, q_ref, k_ref, v_ref, aux_ref, conv_ref,
+    front_out, rest_out,
+    front, normed, doc_cols, attn, scal_in, local_sem, y_send, y_recv, *sems,
+):
+    place = Place(line)
+    side = place.side
+    seq = x_ref.shape[0]
+    depth, half = wq_ref.shape
+    span = 2 * STRETCH
+    blocks = seq // STRETCH
+    scal_at = 6 * half
+    me = place.dp
+    place.enter()
+
+    own_cols = pl.ds(pl.multiple_of(side * half, half), half)
+    other_cols = pl.ds(pl.multiple_of((1 - side) * half, half), half)
+
+    def at(first):
+        return pl.ds(pl.multiple_of((first + side) * half, half), half)
+
+    swaps = [
+        remote(wk_ref.at[:, other_cols], front.at[me, :, at(2)], y_send.at[0], y_recv.at[0], place.peer),
+        remote(wv_ref.at[:, other_cols], front.at[me, :, at(4)], y_send.at[1], y_recv.at[1], place.peer),
+        remote(scal_ref, scal_in, y_send.at[2], y_recv.at[2], place.peer),
+        remote(ck_ref.at[:, other_cols], conv_ref.at[1 + side], y_send.at[3], y_recv.at[3], place.peer),
+        remote(cv_ref.at[:, other_cols], conv_ref.at[3 + side], y_send.at[4], y_recv.at[4], place.peer),
+    ]
+    for swap in swaps:
+        swap.start()
+    own_rest = pltpu.make_async_copy(rest_ref, rest_out.at[me], local_sem.at[0])
+    own_rest.start()
+    front[me, :, 0:half] = wq_ref[...]
+    front[me, :, half : 2 * half] = wg_ref[...]
+    front[me, :, at(2)] = wk_ref[:, own_cols]
+    front[me, :, at(4)] = wv_ref[:, own_cols]
+    conv_ref[0] = cq_ref[...]
+    conv_ref[1 + side] = ck_ref[:, own_cols]
+    conv_ref[3 + side] = cv_ref[:, own_cols]
+
+    head_cuts = [(0, 2 * half), (2 * half, 2 * half), (4 * half, 2 * half + DK)]
+    first = Gather(place, front, head_cuts, sems[:6])
+    tail = rest_out.shape[-1]
+    ff = (tail - half) // 3
+    rest_cuts = [(0, half)] + [(half + i * ff, ff) for i in range(3)]
+    second = Gather(place, rest_out, rest_cuts, sems[6:])
+
+    first.step(0, 0)
+    for swap in swaps:
+        swap.wait_recv()
+    lanes = iota((depth, DK), 1)
+    theirs = pltpu.roll(scal_in[...].astype(F32), 2 * heads, 1)
+    ours = scal_ref[...].astype(F32)
+    swapped = (lanes >= 2 * heads) & (lanes < 4 * heads)
+    front[me, :, scal_at : scal_at + DK] = jnp.where(swapped, theirs, ours).astype(BF)
+    for part in (1, 2):
+        first.step(0, part)
+    own_rest.wait()
+
+    def normalise(block, carry):
+        rows = pl.ds(pl.multiple_of(block * STRETCH, STRETCH), STRETCH)
+        x = x_ref[rows, :].astype(F32)
+        scale = lax.rsqrt(jnp.mean(x * x, axis=-1, keepdims=True) + 1e-06)
+        normed[rows, :] = (x * scale * norm_ref[...]).astype(BF)
+        return carry
+
+    lax.fori_loop(0, blocks, normalise, 0)
+    doc_cols[0:PAD, :] = jnp.full((PAD, DK), -1.0, F32)
+    for i in range(seq // DK):
+        lane_docs = docs_ref[:, i * DK : (i + 1) * DK].astype(F32)
+        doc_cols[PAD + i * DK : PAD + (i + 1) * DK, :] = jnp.broadcast_to(lane_docs, (DK, DK)).T
+    pre_ref[0:PAD, :] = jnp.zeros((PAD, pre_ref.shape[1]), F32)
+
+    steps = first.steps()[3:]
+    for step in steps:
+        step()
+    for part in range(4):
+        second.step(0, part)
+    tile = 2 * DK
+    for part, (start, width) in enumerate(head_cuts):
+        first.ready(part)
+
+        def project(index, carry, start=start):
+            cols = pl.ds(pl.multiple_of(start + index * tile, DK), tile)
+            weights = front[:, :, cols].reshape(-1, tile)
+            pre_ref[PAD:, cols] = jnp.dot(normed[...], weights, preferred_element_type=F32)
+            return carry
+
+        lax.fori_loop(0, 2 * half // tile, project, 0)
+    scal_cols = slice(scal_at, scal_at + DK)
+    pre_ref[PAD:, scal_cols] = jnp.dot(
+        normed[...], front[:, :, scal_cols].reshape(-1, DK), preferred_element_type=F32
+    )
+    keep_front = pltpu.make_async_copy(front, front_out, local_sem.at[1])
+    keep_front.start()
+
+    select = scalar_select(side, heads)
+    rate = -jnp.exp(rates_ref[0:1, :])
+    masks = block_masks()
+    t_row, t_col, p_row, p_col = masks
+    later = second.steps()[4:]
+    together = 2
+    slots = deal(later, blocks // together + blocks)
+
+    def keys_of(rows, cols):
+        return jnp.concatenate([k_ref[0, rows, cols], k_ref[1, rows, cols]], axis=0)
+
+    def prepare_block(block):
+        rows = pl.ds(pl.multiple_of(block * STRETCH, STRETCH), STRETCH)
+        doc_window = rows_of(doc_cols, block, STRETCH, PAD)
+        same = same_documents(doc_window)
+        raw = dot6(pre_ref[pl.ds(pl.multiple_of(block * STRETCH, STRETCH) + PAD, STRETCH), scal_cols], select)
+        lane = iota((STRETCH, DK), 1)
+        beta = (2.0 * jax.nn.sigmoid(raw)).astype(BF).astype(F32)
+        decay = rate * softplus(raw + rates_ref[1:2, :])
+        docs = doc_window[PAD:]
+        fresh = (docs == doc_window[PAD - 1 : PAD]).astype(F32)
+        aux = jnp.where(lane < 2 * heads, beta, jnp.where(lane < 3 * heads, decay, 0.0))
+        aux = jnp.where(lane == 3 * heads, docs, jnp.where(lane == 3 * heads + 1, fresh, aux))
+        aux_ref[rows, :] = aux
+        for head in range(heads):
+            cols = slice(head * DK, (head + 1) * DK)
+            for kind in (1, 2, 0, 3, 4):
+                first_col = (0, 2, 3, 4, 5)[kind] * half + head * DK
+                window = pre_ref[
+                    pl.ds(pl.multiple_of(block * STRETCH, STRETCH), STRETCH + PAD), first_col : first_col + DK
+                ]
+                value = conv_window(window, conv_ref[kind, :, cols], same)
+                value = value * jax.nn.sigmoid(value)
+                if kind < 3:
+                    value = value * lax.rsqrt(jnp.sum(value * value, axis=-1, keepdims=True) + 1e-06)
+                if kind == 0:
+                    q_ref[rows, cols] = value * DK ** (-0.5)
+                elif kind < 3:
+                    k_ref[kind - 1, rows, cols] = value.astype(BF)
+                else:
+                    v_ref[kind - 3, rows, cols] = value.astype(BF)
+        aux2, run2, aux_t, run_t = block_scalars(aux)
+        mats = []
+        for head in range(heads):
+            cols = slice(head * DK, (head + 1) * DK)
+            beta, run_col, run_row, doc_col, doc_row, carried, to_last = head_terms(
+                aux, aux2, run2, aux_t, run_t, head, heads
+            )
+            decay = decay_matrix(run_col, run_row, doc_col, doc_row, p_row, p_col)
+            keys = keys_of(rows, cols)
+            gram = dot1(keys, keys, NT)
+            mats.append(beta * jnp.where(p_row > p_col, decay * gram, 0.0))
+            attn[block * heads + head] = decay[STRETCH:] * dot3(q_ref[rows, cols], keys, NT)
+        return mats
+
+    def prepare(turn, carry):
+        mats = []
+        for i in range(together):
+            mats += prepare_block(turn * together + i)
+        for i, inv in enumerate(inverse(mats, masks)):
+            inv_ref[turn * together * heads + i] = inv
+        run_slot(slots[: blocks // together], turn)
+        return carry
+
+    lax.fori_loop(0, blocks // together, prepare, 0)
+    for head in range(heads):
+        state_ref[head] = jnp.zeros((DK, DK), F32)
+
+    def advance(block, carry):
+        rows = pl.ds(pl.multiple_of(block * STRETCH, STRETCH), STRETCH)
+        aux = aux_ref[rows, :]
+        aux2, run2, aux_t, run_t = block_scalars(aux)
+        for head in range(heads):
+            cols = slice(head * DK, (head + 1) * DK)
+            beta, run_col, run_row, doc_col, doc_row, carried, to_last = head_terms(
+                aux, aux2, run2, aux_t, run_t, head, heads
+            )
+            keys = keys_of(rows, cols)
+            values = jnp.concatenate([v_ref[0, rows, cols], v_ref[1, rows, cols]], axis=0).astype(F32)
+            state = state_ref[block * heads + head]
+            state_parts = split(state)
+            target = beta * (values - carried * dot3(keys, state_parts))
+            pseudo = dot3(inv_ref[block * heads + head], target)
+            pseudo_ref[block * heads + head] = pseudo
+            mixed = carried[STRETCH:] * dot3(q_ref[rows, cols], state_parts) + dot3(
+                attn[block * heads + head], pseudo
+            )
+            state_ref[(block + 1) * heads + head] = carried[span - 1 : span] * state + dot3(
+                keys, to_last * pseudo, TN
+            )
+            mixed_ref[rows, cols] = mixed
+            scale = lax.rsqrt(jnp.mean(mixed * mixed, axis=-1, keepdims=True) + 1e-05)
+            gate = pre_ref[
+                pl.ds(pl.multiple_of(block * STRETCH, STRETCH) + PAD, STRETCH),
+                half + head * DK : half + (head + 1) * DK,
+            ]
+            gated_ref[rows, cols] = (mixed * scale * mix_ref[...] * (gate * jax.nn.sigmoid(gate))).astype(BF)
+        run_slot(slots[blocks // together :], block)
+        return carry
+
+    lax.fori_loop(0, blocks, advance, 0)
+    for part in range(4):
+        second.ready(part)
+    for swap in swaps:
+        swap.wait_send()
+    for part in range(3):
+        first.drain(part)
+    for part in range(4):
+        second.drain(part)
+    keep_front.wait()
+
+
+def front_call(line, x, docs, norm, wq, wg, wk, wv, scal, rest, rates, cq, ck, cv, mix):
+    seq, half = x.shape[0], wq.shape[1]
+    depth, tail = rest.shape
+    heads, blocks = half // DK, seq // STRETCH
+    units, span = heads * blocks, 2 * STRETCH
+    width = 6 * half + DK
+    shape = jax.ShapeDtypeStruct
+    anywhere = pl.BlockSpec(memory_space=pl.ANY)
+    dma = pltpu.SemaphoreType.DMA
+    return pl.pallas_call(
+        functools.partial(front_kernel, line, heads),
+        out_shape=(
+            shape((seq, half), BF),
+            shape((seq, half), F32),
+            shape((units, span, span), F32),
+            shape((units + heads, DK, DK), F32),
+            shape((units, span, DK), F32),
+            shape((seq + PAD, width), F32),
+            shape((seq, half), F32),
+            shape((2, seq, half), BF),
+            shape((2, seq, half), BF),
+            shape((seq, DK), F32),
+            shape((5, KW, half), F32),
+            shape((4 * line, depth, width), BF),
+            shape((4 * line, depth, tail), BF),
+        ),
+        in_specs=[VMEM] * 8 + [anywhere] + [VMEM] * 5,
+        out_specs=(VMEM,) * 11 + (anywhere,) * 2,
+        scratch_shapes=[
+            pltpu.VMEM((4 * line, depth, width), BF),
+            pltpu.VMEM(x.shape, BF),
+            pltpu.VMEM((seq + PAD, DK), F32),
+            pltpu.VMEM((units, STRETCH, span), F32),
+            pltpu.VMEM((depth, DK), BF),
+            dma((2,)),
+            dma((5,)),
+            dma((5,)),
+        ]
+        + gather_sems(line, 3)
+        + gather_sems(line, 4),
+        compiler_params=pltpu.CompilerParams(
+            collective_id=0, has_side_effects=True, vmem_limit_bytes=56 << 20
+        ),
+        name="front",
+    )(x, docs, norm, wq, wg, wk, wv, scal, rest, rates, cq, ck, cv, mix)
 
 
 GROUPS = 8
@@ -404,47 +775,28 @@
     heads = w_alpha.shape[1]
     side = lax.axis_index("step")
 
-    def by_step(own, other):
-        first = side == 0
-        return [jnp.where(first, own, other), jnp.where(first, other, own)]
-
     def swap(array):
         return lax.ppermute(array, "step", [(0, 1), (1, 0)])
 
-    def parts_for(array, width):
-        return (
-            lax.dynamic_slice_in_dim(array, side * width, width, 1),
-            lax.dynamic_slice_in_dim(array, (1 - side) * width, width, 1),
-        )
-
-    key_mine, key_theirs = parts_for(w_key[0], half)
-    value_mine, value_theirs = parts_for(w_value[0], half)
-    beta_mine, beta_theirs = parts_for(w_beta[0], heads)
-    got = swap(jnp.concatenate([key_theirs, value_theirs, beta_theirs], axis=1))
-    conv_k_mine, conv_k_theirs = parts_for(conv_key[0], half)
-    conv_v_mine, conv_v_theirs = parts_for(conv_value[0], half)
-    got_conv = swap(jnp.concatenate([conv_k_theirs, conv_v_theirs], axis=1))
-    keys_w = by_step(key_mine, got[:, :half])
-    values_w = by_step(value_mine, got[:, half : 2 * half])
-    betas_w = by_step(beta_mine, got[:, 2 * half :])
-    kernels_k = by_step(conv_k_mine, got_conv[:, :half])
-    kernels_v = by_step(conv_v_mine, got_conv[:, half:])
-    pad = jnp.zeros((depth, DK - 3 * heads), BF)
-    front_w = lax.all_gather(
-        jnp.concatenate([w_query, w_outgate] + keys_w + values_w + betas_w + [w_alpha, pad], axis=1),
-        "dp", axis=0, tiled=True,
-    )
-    back_w = lax.all_gather(
-        jnp.concatenate([w_out.T, w_gate, w_up, w_down.T], axis=1), "dp", axis=0, tiled=True
+    rest = jnp.concatenate([w_out.T, w_gate, w_up, w_down.T], axis=1)
+    scal = jnp.concatenate(
+        [w_beta[0], jnp.zeros((depth, 2 * heads), BF), w_alpha, jnp.zeros((depth, DK - 5 * heads), BF)], axis=1
+    )
+    rates = jnp.pad(jnp.stack([decay_log, decay_bias]), ((0, 0), (2 * heads, DK - 3 * heads)))
+    gain_row = mix_gain[None]
+    (gated, mixed, inv, state, pseudo, pre, queries, keys, values, aux, conv, front_w, back_w) = front_call(
+        lax.axis_size("dp") // 4, tokens[0], doc_ids, norm_gain[None], w_query, w_outgate, w_key[0], w_value[0],
+        scal, rest, rates, conv_query, conv_key[0], conv_value[0], gain_row,
     )
     ff = w_gate.shape[1]
-
+    front_w = front_w.reshape(-1, front_w.shape[-1])
+    back_w = back_w.reshape(-1, back_w.shape[-1])
     inputs = tokens[0].astype(F32)
     docs = doc_ids[0]
     seq_len = inputs.shape[0]
     normed_f, pull_first = jax.vjp(rms_scale, inputs, norm_gain)
     normed = normed_f.astype(BF)
-    pre = product(normed, front_w)
+    pre = pre[PAD:]
     gate_pre = pre[:, half : 2 * half]
 
     def prepare(pre_in, query_kernel, key_0, key_1, value_0, value_1, log_rates, rate_bias):
@@ -457,24 +809,14 @@
             jax.nn.silu(short_conv(pre_in[:, (4 + i) * half : (5 + i) * half], kernel, docs))
             for i, kernel in enumerate((value_0, value_1))
         ]
-        scalars = pre_in[:, 6 * half :]
+        scalars = pre_in[:, 6 * half :] @ scalar_select(side, heads)
         betas = 2.0 * jax.nn.sigmoid(scalars[:, : 2 * heads])
         decays = -jnp.exp(log_rates) * jax.nn.softplus(scalars[:, 2 * heads : 3 * heads] + rate_bias)
         return (queries, jnp.stack(keys), jnp.stack(values), betas, decays)
 
-    (queries, keys, values, betas, decays), pull_prepare = jax.vjp(
-        prepare, pre, conv_query, kernels_k[0], kernels_k[1], kernels_v[0], kernels_v[1], decay_log, decay_bias
-    )
-    prior = jnp.concatenate([jnp.full((1,), -1, docs.dtype), docs[STRETCH - 1 : -1 : STRETCH]])
-    fresh = (docs.reshape(-1, STRETCH) == prior[:, None]).reshape(seq_len, 1).astype(F32)
-    aux = jnp.concatenate(
-        [betas.astype(BF).astype(F32), decays, docs.astype(F32)[:, None], fresh,
-         jnp.zeros((seq_len, DK - 3 * heads - 2), F32)],
-        axis=1,
-    )
-    keys, values = keys.astype(BF), values.astype(BF)
-    gain_row = mix_gain[None]
-    gated, mixed, inv, state, pseudo = mixer_fwd(queries, keys, values, aux, gate_pre, gain_row)
+    _, pull_prepare = jax.vjp(
+        prepare, pre, conv[0], conv[1], conv[2], conv[3], conv[4], decay_log, decay_bias
+    )
 
     attention = lax.psum(product(gated, back_w[:, :half], NT).astype(BF), "step").astype(F32)
     middle = inputs + attention
@@ -532,7 +874,7 @@
     col = lambda i: sum_front[:, i * half : (i + 1) * half]
     sum_key, sum_value = home([col(2), col(3)]), home([col(4), col(5)])
     tail = sum_front[:, 6 * half :]
-    sum_beta = home([tail[:, :heads], tail[:, heads : 2 * heads]])
+    sum_beta = tail[:, : 2 * heads] + swap(tail[:, 2 * heads : 4 * heads])
     small = lax.psum(
         (grad_norm_gain, d_log, d_bias, d_cq, d_k0, d_k1, d_v0, d_v1, grad_ffn_gain), "dp"
     )
@@ -548,7 +890,7 @@
         f32(sum_key)[None],
         f32(sum_value)[None],
         f32(sum_beta)[None],
-        f32(tail[:, 2 * heads : 3 * heads]),
+        f32(tail[:, 4 * heads : 5 * heads]),
         sum_log,
         sum_bias,
         sum_cq,

time: 671 us -> 651 us (0.970)
  Pallas kernels: 78.7 us -> 168 us
  waiting for transfers between devices: 242 us -> 165 us
  other arithmetic: 86.1 us -> 75.2 us
  local copies, waits for them, and re-layouts: 57.6 us -> 47.9 us
    pallas_call x1, Pallas kernels: 36.3 us -> 118 us  [front_call(): pl.pallas_call(functools.partial(front_kernel, line, heads), out_shape=(s...]
    all_gather x2 -> x0, waiting for transfers between devices: 59.1 us -> none  [the longest x1 59.1 us: per_device(): lax.all_gather(jnp.concatenate([w_query, w_outgate] + keys_w + values_w +...]
    psum x1, waiting for transfers between devices: 35.1 us -> 25.3 us  [per_device(): lax.psum((product(gate_back, gate_w, NT) + product(up_back, up_w, NT)).as...]
    pallas_call x1, Pallas kernels: 42.4 us -> 50.5 us  [mixer_bwd(): pl.pallas_call(functools.partial(mixer_bwd_kernel, heads), out_shape=(sha...]
    unnamed x178 -> x164, local copies, waits for them, and re-layouts: 15.2 us -> 8.21 us
    dot_general x15 -> x14, matrix products: 67.6 us -> 61.3 us  [product(): lax.dot_general(first, second, (dims, ((), ())), preferred_element_type=F32)]
  transfers between devices with their start and end apart: 14 -> 10, of which waited for: 7 -> 5; matrix products, arithmetic and copies ran while one was open for 17% -> 13% of each run, Pallas kernels for 5% -> 0%
where the time goes in v2:
time: 651 us; the launch traced here: 643 us
  Pallas kernels  168 us (26%)
  waiting for transfers between devices  165 us (25%)
  blocking collectives  102 us (16%)
  other arithmetic  75.2 us (12%)
  matrix products  62.7 us (10%)
  local copies, waits for them, and re-layouts  47.9 us (7%)
  between operations  15.4 us (2%)
    pallas_call x1, Pallas kernels, front_call(): pl.pallas_call(functools.partial(front_kernel, line, heads), out_shape=(s...  118 us
    reduce_scatter x1, waiting for transfers between devices, per_device(): lax.psum_scatter(jnp.concatenate([grad_out, grad_gate, grad_up, grad_down...  104 us
    psum x1, blocking collectives, per_device(): lax.psum((grad_norm_gain, d_log, d_bias, d_cq, d_k0, d_k1, d_v0, d_v1, gr...  62.1 us
    dot_general x14, matrix products, product(): lax.dot_general(first, second, (dims, ((), ())), preferred_element_type=F32)  61.3 us
    pallas_call x1, Pallas kernels, mixer_bwd(): pl.pallas_call(functools.partial(mixer_bwd_kernel, heads), out_shape=(sha...  50.5 us
    psum x1, blocking collectives, per_device(): sum_mix_gain = lax.psum(dgain[0], ('dp', 'step'))  40 us
    psum x1, waiting for transfers between devices, per_device(): lax.psum(product(gated, back_w[:, :half], NT).astype(BF), 'step')  27.1 us
    psum x1, waiting for transfers between devices, per_device(): lax.psum((product(gate_back, gate_w, NT) + product(up_back, up_w, NT)).as...  25.3 us
  transfers between devices with their start and end apart: 10, of which 5 were waited for; matrix products, arithmetic and copies ran while one was open for 13% of the time, Pallas kernels for 0%

profile of v2, /device:TPU:0, one launch (start us, length us, event | category | flops | bytes accessed | tf_op | source)
XLA Modules:
  0.0 642.6 jit_solution(6608414742717338253)
XLA Ops:
  9.0 1.3 select_maximum_fusion.rates_ref
  11.0 2.0 pad_maximum_fusion.4.rest_ref
  12.9 117.8 %front.1 = (bf16[512,512]{1,0:T(8,128)(2,1)}, f32[512,512]{1,0:T(8,128)}, f32[32,128,128]{2,1,0:T(8,128)}, f32[36,128,128]{2,1,0:T(8,128)}, f32[32,128,128]{2,1,...) custom-call(bf16[512,1024]{1,0:T(8,128)(2,1)} %bitcast.200, ...), custom_call_target="tpu_custom_call" | custom-call | tf_op jit(solution)/shard_map/front/pallas_call | solution.py:666
  130.8 3.1 convolution_convert_fusion.5
  135.2 4.8 fusion.130
  140.7 2.1 fusion.79
  142.8 6.2 fusion.2
  149.0 3.1 fusion.120
  152.2 27.1 %all-reduce.68.cloned.1.call-done = bf16[512,1024]{1,0:T(8,128)(2,1)} async-done(((bf16[512,1024]{1,0:T(8,128)(2,1)}), bf16[512,1024]{1,0:T(8,128)(2,1)}) %all-reduce.68.cloned.1.call-update) | async-done | bytes 1048592 | tf_op jit(solution)/shard_map/psum | solution.py:821
  179.3 1.7 multiply_reduce_fusion
  181.5 4.0 fusion.8
  185.5 6.1 multiply_convert_fusion.1
  191.6 1.8 fusion.6
  193.5 2.8 add_convert_fusion
  196.4 2.6 reshape.529
  199.0 2.5 mul.1117
  201.5 1.9 reduce_sum.338
  203.6 1.4 reshape.530
  205.0 1.1 fusion.96
  206.2 5.1 fusion.29
  211.2 25.3 %all-reduce.70.cloned.1.call-done = bf16[512,1024]{1,0:T(8,128)(2,1)} async-done(((bf16[512,1024]{1,0:T(8,128)(2,1)}), bf16[512,1024]{1,0:T(8,128)(2,1)}) %all-reduce.70.cloned.1.call-update) | async-done | bytes 1048592 | tf_op jit(solution)/shard_map/psum | solution.py:840
  236.5 3.1 fusion.20
  239.7 4.0 fusion.80.dgated_ref
  243.7 50.5 %mixer_backward.1 = (f32[512,512]{1,0:T(8,128)S(1)}, bf16[2,512,512]{2,1,0:T(8,128)(2,1)S(1)}, bf16[2,512,512]{2,1,0:T(8,128)(2,1)S(1)}, f32[512,128]{1,0:T(8,12...) custom-call(f32[512,512]{1,0:T(8,128)S(1)} %copy-done, bf16[2,512,512]{2,1,0:T(8,128)(2,1)} %get-tuple-element.42.k_ref, ...), custom_call_target="tpu_custom_call" | custom-call | tf_op jit(solution)/shard_map/mixer_backward/pallas_call | solution.py:228
  294.2 1.6 convert_element_type.174
  295.8 1.7 fusion.131
  298.5 1.6 convert_element_type.170
  300.1 2.5 unstack.37
  302.6 2.6 unstack.34
  305.2 3.4 multiply_reduce_fusion.24
  311.5 3.4 multiply_reduce_fusion.22
  317.2 2.5 multiply_multiply_fusion.15
  319.7 2.6 mul.1122
  322.2 2.6 reduce_sum.342
  327.6 1.7 broadcast_in_dim.46
  329.3 1.6 mul.1045
  330.9 9.8 %multiply_reduce_fusion.12 = (f32[512]{0:T(512)}, f32[512]{0:T(512)}, f32[512]{0:T(512)}, f32[512]{0:T(512)}, f32[512]{0:T(512)}, /*index=5*/f32[512]{0:T(512)},...) fusion(f32[512,512]{1,0:T(8,128)S(1)} %copy-done.12, ...), kind=kLoop, calls=%fused_computation.163 | loop fusion | flops 20704768 | bytes 12623872 | tf_op jit(solution)/shard_map/transpose(jvp())/reduce_sum | solution.py:731
  343.4 3.6 multiply_reduce_fusion.5
  347.4 1.4 multiply_multiply_fusion
  349.7 1.1 fusion.37
  350.8 1.1 fusion.55
  352.3 1.4 copy-done.19
  353.6 1.2 slice-done.5
  355.6 4.7 convolution_convert_fusion.6
  361.0 8.2 %convolution_convert_fusion = bf16[1024,3200]{1,0:T(8,128)(2,1)} fusion(bf16[512,2176]{1,0:T(8,128)(2,1)} %copy-done.19, bf16[512,512]{1,0:T(8,128)(2,1)S(1)} %get-tuple-element.55, bf16[512,512]{1,0:T(8,128)(2,1)S(1)} %add_convert_fusion.2, f32[512]{0:T(512)S(1)} %fusion.112, f32[1024]{0:T(1024)S(1)} %copy-done.31, bf16[1,512,1024]{2,1,0:T(8,128)(2,1)S(1)} %copy-done.3), kind=kOutput, calls=%fused_computation.1 | convolution fusion | flops 3370647552 | bytes 10885120 | tf_op jit(solution)/shard_map/dot_general | solution.py:708
  369.3 1.1 copy-done.22
  370.4 5.5 convolution_convert_fusion.1
  375.9 3.5 convolution_convert_fusion.3
  379.4 3.4 convolution_convert_fusion.2
  382.9 3.0 convolution_convert_fusion.4
  385.9 2.3 copy.89
  388.2 9.2 %pad_maximum_fusion = bf16[1024,4736]{1,0:T(8,128)(2,1)} fusion(bf16[1024,1408]{1,0:T(8,128)(2,1)} %convolution_convert_fusion.1, bf16[1024,1408]{1,0:T(8,128)(2,1)} %convolution_convert_fusion.2, bf16[1024,1408]{1,0:T(8,128)(2,1)} %convolution_convert_fusion.3, bf16[1024,512]{1,0:T(8,128)(2,1)} %copy.89), kind=kLoop, calls=%fused_computation | loop fusion | flops 38797312 | bytes 19398656 | tf_op jit(solution)/shard_map/concatenate | solution.py:848
  397.5 40.0 %psum.110 = f32[128]{0:T(128)} all-reduce(f32[128]{0:T(128)S(1)} %bitcast.199), channel_id=1, replica_groups=mesh['dp'=16,'step'=2] {'dp','step'}, use_global_device_ids=true, to_apply=%region_49.50 | all-reduce | flops 128 | bytes 1024 | tf_op jit(solution)/shard_map/psum | solution.py:882
  437.7 2.2 fusion.21
  440.0 62.1 %all-reduce.62 = (f32[1024]{0:T(1024)}, f32[4]{0:T(128)}, f32[4]{0:T(128)}, f32[4,512]{1,0:T(4,128)}, f32[4,512]{1,0:T(4,128)S(1)}, /*index=5*/f32[4,512]{1,0:T(...) all-reduce(f32[1024]{0:T(1024)S(1)} %get-tuple-element.160, ...), channel_id=1, replica_groups=mesh['dp'=16,'step'=2] {'dp'}, use_global_device_ids=true, to_apply=%region_18.19 | all-reduce | flops 12296 | bytes 98368 | tf_op jit(solution)/shard_map/psum | solution.py:878
  503.0 1.1 collective-permute-start.3
  504.1 4.8 fusion.73
  510.2 6.2 reduce-scatter.3.cloned.1.call-done
  517.2 1.5 collective-permute-start.2
  518.7 1.7 select_bitcast_fusion
  522.4 1.5 collective-permute-start.1
  525.3 1.5 collective-permute-done.1
  528.3 104.3 %reduce-scatter.5.cloned.1.call-done = bf16[64,4736]{1,0:T(8,128)(2,1)} async-done(((bf16[1024,4736]{1,0:T(8,128)(2,1)}), bf16[64,4736]{1,0:T(8,128)(2,1)}) %reduce-scatter.5.cloned.1.call-update) | async-done | bytes 606224 | tf_op jit(solution)/shard_map/reduce_scatter | solution.py:847
  632.6 1.2 convert_element_type.185
  (242 shorter events, 29.2 us)
Async XLA Ops:
  7.2 172.1 %all-reduce.68.cloned.1.call-start = ((), (), s32[]{:S(2)}) async-start(), calls=%async_computation.2 | async-start | bytes 2097152 | tf_op jit(solution)/shard_map/psum | solution.py:821
  130.8 3.5 copy-start.67
  130.8 3.7 copy-start.35
  130.8 3.8 copy-start.30
  133.9 102.6 %all-reduce.70.cloned.1.call-start = ((), (), s32[]{:S(2)}) async-start(), calls=%async_computation.3 | async-start | bytes 2097152 | tf_op jit(solution)/shard_map/psum | solution.py:840
  134.2 70.7 %copy-start.51 = (s32[128]{0:T(128)}, s32[128]{0:T(128)S(1)}, u32[]{:S(2)}) copy-start(s32[128]{0:T(128)S(1)} %get-tuple-element.291) | copy-start | bytes 1540
  134.3 70.7 %copy-start.53 = (s32[128]{0:T(128)}, s32[128]{0:T(128)S(1)}, u32[]{:S(2)}) copy-start(s32[128]{0:T(128)S(1)} %get-tuple-element.292) | copy-start | bytes 1540
  140.0 9.1 %copy-start.11 = (f32[512,512]{1,0:T(8,128)}, f32[512,512]{1,0:T(8,128)S(1)}, u32[]{:S(2)}) copy-start(f32[512,512]{1,0:T(8,128)S(1)} %get-tuple-element.205) | copy-start | bytes 3145732
  140.0 9.1 %copy-start.6 = (f32[512,512]{1,0:T(8,128)}, f32[512,512]{1,0:T(8,128)S(1)}, u32[]{:S(2)}) copy-start(f32[512,512]{1,0:T(8,128)S(1)} %get-tuple-element.203) | copy-start | bytes 3145732
  140.0 9.1 %copy-start.8 = (f32[512,512]{1,0:T(8,128)}, f32[512,512]{1,0:T(8,128)S(1)}, u32[]{:S(2)}) copy-start(f32[512,512]{1,0:T(8,128)S(1)} %get-tuple-element.204) | copy-start | bytes 3145732
  149.0 30.3 %copy-start.3 = (bf16[1,512,1024]{2,1,0:T(8,128)(2,1)S(1)}, bf16[1,512,1024]{2,1,0:T(8,128)(2,1)}, u32[]{:S(2)}) copy-start(bf16[1,512,1024]{2,1,0:T(8,128)(2,1)} %param.22) | copy-start | bytes 3145732
  152.2 28.9 %copy-start.32 = (f32[1024]{0:T(1024)S(1)}, f32[1024]{0:T(1024)}, u32[]{:S(2)}) copy-start(f32[1024]{0:T(1024)} %param.40) | copy-start | bytes 12292
  181.4 4.1 copy-start.27
  181.5 4.1 copy-start.68
  181.5 10.1 %slice-start.2 = ((s8[9699328]{0:T(1024)(128)(4,1)}), s8[4194304]{0:T(1024)(128)(4,1)S(1)}, s32[]{:S(2)}) async-start(s8[9699328]{0:T(1024)(128)(4,1)} %bitcast.290), calls=%async_computation.9 | async-start | bytes 8388608
  185.5 6.1 slice-start.3
  185.5 6.1 slice-start.4
  196.3 241.4 %all-reduce.72.cloned.1.call-start = ((), (), s32[]{:S(2)}) async-start(), calls=%async_computation.6 | async-start | bytes 4194304 | tf_op jit(solution)/shard_map/psum | solution.py:829
  196.4 8.6 %copy-start.55 = (s32[128]{0:T(128)}, s32[128]{0:T(128)S(1)}, u32[]{:S(2)}) copy-start(s32[128]{0:T(128)S(1)} %get-tuple-element.289) | copy-start | bytes 1540
  196.4 8.6 %copy-start.57 = (s32[128]{0:T(128)}, s32[128]{0:T(128)S(1)}, u32[]{:S(2)}) copy-start(s32[128]{0:T(128)S(1)} %get-tuple-element.290) | copy-start | bytes 1540
  204.9 6.3 copy-start.59
  204.9 6.3 copy-start.61
  239.7 4.0 copy-start.38
  239.7 4.0 copy-start
  239.7 4.0 copy-start.1
  239.7 4.0 copy-start.2
  322.2 8.6 %copy-start.33 = (f32[1,1,512]{2,1,0:T(1,128)S(1)}, f32[1,1,512]{2,1,0:T(1,128)}, u32[]{:S(2)}) copy-start(f32[1,1,512]{2,1,0:T(1,128)} %get-tuple-element.258) | copy-start | bytes 6148
  330.8 12.4 %slice-start = ((s8[6656000]{0:T(1024)(128)(4,1)}), s8[4194304]{0:T(1024)(128)(4,1)S(1)}, s32[]{:S(2)}) async-start(s8[6656000]{0:T(1024)(128)(4,1)} %bitcast.201), calls=%async_computation.7 | async-start | bytes 8388608
  330.9 9.9 %copy-start.24 = (f32[512,4]{1,0:T(8,128)S(1)}, f32[512,4]{1,0:T(8,128)}, u32[]{:S(2)}) copy-start(f32[512,4]{1,0:T(8,128)} %copy.84) | copy-start | bytes 24580
  330.9 11.1 %copy-start.26 = (f32[512,4]{1,0:T(8,128)S(1)}, f32[512,4]{1,0:T(8,128)}, u32[]{:S(2)}) copy-start(f32[512,4]{1,0:T(8,128)} %copy.88) | copy-start | bytes 24580
  330.9 11.7 %copy-start.25 = (f32[512,4]{1,0:T(8,128)S(1)}, f32[512,4]{1,0:T(8,128)}, u32[]{:S(2)}) copy-start(f32[512,4]{1,0:T(8,128)} %copy.86) | copy-start | bytes 24580
  330.9 12.3 %slice-start.1 = ((s8[6656000]{0:T(1024)(128)(4,1)}), s8[2461696]{0:T(1024)(128)(4,1)S(1)}, s32[]{:S(2)}) async-start(s8[6656000]{0:T(1024)(128)(4,1)} %bitcast.201), calls=%async_computation.8 | async-start | bytes 4923392
  330.9 12.3 %copy-start.14 = (f32[512,512]{1,0:T(8,128)S(1)}, f32[512,512]{1,0:T(8,128)}, u32[]{:S(2)}) copy-start(f32[512,512]{1,0:T(8,128)} %get-tuple-element.279) | copy-start | bytes 3145732
  351.9 3.7 slice-start.6
  360.3 156.1 %reduce-scatter.3.cloned.1.call-start = ((), (), s32[]{:S(2)}) async-start(), calls=%async_computation.4 | async-start | bytes 6963200 | tf_op jit(solution)/shard_map/reduce_scatter | solution.py:865
  369.2 6.7 %copy-start.28 = (bf16[512,1024]{1,0:T(8,128)(2,1)S(1)}, bf16[512,1024]{1,0:T(8,128)(2,1)}, u32[]{:S(2)}) copy-start(bf16[512,1024]{1,0:T(8,128)(2,1)} %copy-done.27) | copy-start | bytes 3145732
  369.2 263.4 %reduce-scatter.5.cloned.1.call-start = ((), (), s32[]{:S(2)}) async-start(), calls=%async_computation.5 | async-start | bytes 10305536 | tf_op jit(solution)/shard_map/reduce_scatter | solution.py:847
  370.4 5.5 copy-start.72
  375.9 3.5 copy-start.29
  375.9 3.5 copy-start.70
  379.4 3.5 copy-start.5
  379.4 3.5 copy-start.16
  379.4 3.5 copy-start.23
  379.4 3.5 copy-start.39
  397.3 40.1 %copy-start.36 = (f32[512]{0:T(512)S(1)}, f32[512]{0:T(512)}, u32[]{:S(2)}) copy-start(f32[512]{0:T(512)} %get-tuple-element.163) | copy-start | bytes 6148
  397.3 40.1 %copy-start.37 = (f32[512]{0:T(512)S(1)}, f32[512]{0:T(512)}, u32[]{:S(2)}) copy-start(f32[512]{0:T(512)} %get-tuple-element.164) | copy-start | bytes 6148
  397.3 40.2 %copy-start.43 = (f32[512]{0:T(512)S(1)}, f32[512]{0:T(512)}, u32[]{:S(2)}) copy-start(f32[512]{0:T(512)} %get-tuple-element.173) | copy-start | bytes 6148
  397.4 40.2 %copy-start.44 = (f32[512]{0:T(512)S(1)}, f32[512]{0:T(512)}, u32[]{:S(2)}) copy-start(f32[512]{0:T(512)} %get-tuple-element.174) | copy-start | bytes 6148
  397.4 40.2 %copy-start.45 = (f32[512]{0:T(512)S(1)}, f32[512]{0:T(512)}, u32[]{:S(2)}) copy-start(f32[512]{0:T(512)} %get-tuple-element.175) | copy-start | bytes 6148
  397.4 40.2 %copy-start.46 = (f32[512]{0:T(512)S(1)}, f32[512]{0:T(512)}, u32[]{:S(2)}) copy-start(f32[512]{0:T(512)} %get-tuple-element.176) | copy-start | bytes 6148
  397.4 40.2 %copy-start.47 = (f32[512]{0:T(512)S(1)}, f32[512]{0:T(512)}, u32[]{:S(2)}) copy-start(f32[512]{0:T(512)} %get-tuple-element.177) | copy-start | bytes 6148
  397.4 40.2 %copy-start.48 = (f32[512]{0:T(512)S(1)}, f32[512]{0:T(512)}, u32[]{:S(2)}) copy-start(f32[512]{0:T(512)} %get-tuple-element.178) | copy-start | bytes 6148
  397.4 40.2 %copy-start.40 = (f32[512]{0:T(512)S(1)}, f32[512]{0:T(512)}, u32[]{:S(2)}) copy-start(f32[512]{0:T(512)} %get-tuple-element.154) | copy-start | bytes 6148
  397.4 40.2 %copy-start.41 = (f32[512]{0:T(512)S(1)}, f32[512]{0:T(512)}, u32[]{:S(2)}) copy-start(f32[512]{0:T(512)} %get-tuple-element.155) | copy-start | bytes 6148
  397.4 40.2 %copy-start.42 = (f32[512]{0:T(512)S(1)}, f32[512]{0:T(512)}, u32[]{:S(2)}) copy-start(f32[512]{0:T(512)} %get-tuple-element.156) | copy-start | bytes 6148
  397.5 40.2 %copy-start.63 = (f32[4]{0:T(128)S(1)}, f32[4]{0:T(128)}, u32[]{:S(2)}) copy-start(f32[4]{0:T(128)} %get-tuple-element.233) | copy-start | bytes 52
  397.5 40.2 %copy-start.65 = (f32[4]{0:T(128)S(1)}, f32[4]{0:T(128)}, u32[]{:S(2)}) copy-start(f32[4]{0:T(128)} %param.33) | copy-start | bytes 52
  397.5 42.5 %copy-start.34 = (f32[1024]{0:T(1024)S(1)}, f32[1024]{0:T(1024)}, u32[]{:S(2)}) copy-start(f32[1024]{0:T(1024)} %get-tuple-element.143) | copy-start | bytes 12292
  397.5 42.4 %copy-start.49 = (f32[4]{0:T(128)S(1)}, f32[4]{0:T(128)}, u32[]{:S(2)}) copy-start(f32[4]{0:T(128)} %get-tuple-element.195) | copy-start | bytes 52
  502.0 7.0 %collective-permute-start.4 = (f32[4,512]{1,0:T(4,128)S(1)}, f32[4,512]{1,0:T(4,128)S(1)}, u32[]{:S(2)}, u32[]{:S(2)}) collective-permute-start(f32[4,512]{1,0:T(4,128)S(1)} %get-tuple-element.260), channel_id=1, source_target_pairs={{0,1},{1,0},{2,3},{3,2},{4,5},{5,4},{6,7},{7,6},{8,9},{9,8},{10,11... | collective-permute-start | bytes 24584 | tf_op jit(solution)/shard_map/ppermute | solution.py:779
  503.0 6.6 %collective-permute-start.3 = (f32[4,512]{1,0:T(4,128)S(1)}, f32[4,512]{1,0:T(4,128)S(1)}, u32[]{:S(2)}, u32[]{:S(2)}) collective-permute-start(f32[4,512]{1,0:T(4,128)S(1)} %get-tuple-element.262), channel_id=1, source_target_pairs={{0,1},{1,0},{2,3},{3,2},{4,5},{5,4},{6,7},{7,6},{8,9},{9,8},{10,11... | collective-permute-start | bytes 24584 | tf_op jit(solution)/shard_map/ppermute | solution.py:779
  517.2 6.7 %collective-permute-start.2 = (bf16[64,8]{1,0:T(8,128)(2,1)S(1)}, bf16[64,8]{1,0:T(8,128)(2,1)S(1)}, u32[]{:S(2)}, u32[]{:S(2)}) collective-permute-start(bf16[64,8]{1,0:T(8,128)(2,1)S(1)} %slice.374), channel_id=1, source_target_pairs={{0,1},{1,0},{2,3},{3,2},{4,5},{5,4},{6,7},{7,6},{8,9},{9,8},{10,11... | collective-permute-start | bytes 3080 | tf_op jit(solution)/shard_map/ppermute | solution.py:779
  521.9 5.7 collective-permute-start
  522.4 4.4 collective-permute-start.1
  (26 other events, 55.0 us)
Sparse Core Ops, SparseCore 0:
  134.0 45.2 all-reduce.67
  196.4 40.0 all-reduce.69
  360.5 63.7 all-reduce.71
  428.6 87.7 reduce-scatter.2
  520.4 112.2 reduce-scatter.4

commit v3 on v2

--- a/solution.py
+++ b/solution.py
@@ -47,6 +47,10 @@
 
 def iota(shape, dim):
     return lax.broadcasted_iota(jnp.int32, shape, dim)
+
+
+def product(first, second, dims=NN):
+    return lax.dot_general(first, second, (dims, ((), ())), preferred_element_type=F32)
 
 
 def block_masks():
@@ -111,136 +115,7 @@
     return [x + dot1(x, r) for x, r in zip(out, rest)]
 
 
-def mixer_bwd_kernel(heads, q_ref, k_ref, v_ref, aux_ref, gate_ref, gain_ref, mixed_ref, inv_ref,
-                     state_ref, pseudo_ref, dgated_ref,
-                     dq_ref, dk_ref, dv_ref, daux_ref, dgate_ref, dgain_ref, dstate):
-    blocks = q_ref.shape[0] // STRETCH
-    span = 2 * STRETCH
-    masks = block_masks()
-    t_row, t_col, p_row, p_col = masks
-    for head in range(heads):
-        dstate[head] = jnp.zeros((DK, DK), F32)
-    dgain_ref[...] = jnp.zeros_like(dgain_ref)
-    upper = (iota((STRETCH, STRETCH), 0) <= iota((STRETCH, STRETCH), 1)).astype(F32)
-    lanes = iota((STRETCH, DK), 1)
-    wide_lanes = iota((span, DK), 1)
-    wide_rows = iota((span, DK), 0)
-
-    def back(step, carry):
-        block = blocks - 1 - step
-        rows = pl.ds(pl.multiple_of(block * STRETCH, STRETCH), STRETCH)
-        aux = aux_ref[rows, :]
-        aux2, run2, aux_t, run_t = block_scalars(aux)
-        dbeta_all = jnp.zeros((STRETCH, DK), F32)
-        drun_all = jnp.zeros((STRETCH, DK), F32)
-        column_sums = jnp.zeros((span, DK), F32)
-        for head in range(heads):
-            cols = slice(head * DK, (head + 1) * DK)
-            beta, run_col, run_row, doc_col, doc_row, carried, to_last = head_terms(
-                aux, aux2, run2, aux_t, run_t, head, heads
-            )
-            decay = decay_matrix(run_col, run_row, doc_col, doc_row, p_row, p_col)
-            keys = keys = jnp.concatenate([k_ref[0, rows, cols], k_ref[1, rows, cols]], axis=0)
-            queries = q_ref[rows, cols]
-            mixed = mixed_ref[rows, cols]
-            gate = gate_ref[rows, cols]
-            sigmoid = jax.nn.sigmoid(gate)
-            silu = gate * sigmoid
-            scale = lax.rsqrt(jnp.mean(mixed * mixed, axis=-1, keepdims=True) + 1e-05)
-            scaled = mixed * scale
-            dgated = dgated_ref[rows, cols]
-            part = dgated * scaled
-            dgate_ref[rows, cols] = (
-                part * gain_ref[...] * (sigmoid * (1.0 + gate * (1.0 - sigmoid)))
-            ).astype(BF)
-            dgain_ref[...] += jnp.sum(part * silu, axis=0, keepdims=True)
-            dscaled = dgated * gain_ref[...] * silu
-            dout = scale * (dscaled - scaled * jnp.mean(dscaled * scaled, axis=-1, keepdims=True))
-
-            index = block * heads + head
-            state, pseudo = state_ref[index], pseudo_ref[index]
-            dnext = dstate[head]
-            dnext_parts, state_parts, pseudo_parts = split(dnext), split(state), split(pseudo)
-            dout_parts, q_parts = split(dout), split(queries)
-            gram = dot1(keys, keys, NT)
-            strict = p_row > p_col
-            core = jnp.where(strict, decay * gram, 0.0)
-            amat = beta * core
-            qdecay = decay[STRETCH:]
-            attn = qdecay * dot3(q_parts, keys, NT)
-            dattn = dot3(dout_parts, pseudo_parts, NT)
-            dqk = split(qdecay * dattn)
-            dpseudo = dot3(attn, dout_parts, TN) + to_last * dot3(keys, dnext_parts)
-            dtarget = dot3(inv_ref[index], dpseudo, TN)
-            dtarget_parts = split(dtarget)
-            damat = jnp.where(strict, -dot3(dtarget_parts, pseudo_parts, NT), 0.0)
-            e_a, e_m = damat * amat, dattn * attn
-            dgram = split(beta * decay * damat)
-            dbeta = jnp.sum(dtarget * pseudo, axis=-1, keepdims=True) / jnp.maximum(beta, 1e-30)
-            dvalues = beta * dtarget
-            dread = -(beta * carried) * dtarget
-            dout_c = carried[STRETCH:] * dout
-            dread_parts, dout_c_parts = split(dread), split(dout_c)
-            last = carried[span - 1 : span]
-            dstate[head] = last * dnext + dot3(keys, dread_parts, TN) + dot3(q_parts, dout_c_parts, TN)
-            dq_state = dot3(dout_c_parts, state_parts, NT)
-            dk_state = dot3(dread_parts, state_parts, NT)
-            dk_last = dot3(to_last * pseudo, dnext_parts, NT)
-            dq_ref[rows, cols] = dq_state + dot3(dqk, keys)
-            dkeys = (
-                dk_state + dk_last + dot3(dgram, keys) + dot3(dgram, keys, TN) + dot3(dqk, q_parts, TN)
-            )
-            dk_ref[0, rows, cols] = dkeys[:STRETCH].astype(BF)
-            dk_ref[1, rows, cols] = dkeys[STRETCH:].astype(BF)
-            dv_ref[0, rows, cols] = dvalues[:STRETCH].astype(BF)
-            dv_ref[1, rows, cols] = dvalues[STRETCH:].astype(BF)
-
-            wide = keys.astype(F32)
-            e_last = jnp.sum(wide * dk_last, axis=-1, keepdims=True)
-            drun = jnp.sum(e_a, axis=-1, keepdims=True) - e_last + jnp.sum(wide * dk_state, axis=-1, keepdims=True)
-            drun_q = jnp.sum(e_m, axis=-1, keepdims=True) + jnp.sum(queries * dq_state, axis=-1, keepdims=True)
-            at_last = jnp.sum(e_last, axis=0, keepdims=True) + last * jnp.sum(
-                jnp.sum(dnext * state, axis=-1, keepdims=True), axis=0, keepdims=True
-            )
-            drun = drun[:STRETCH] + drun[STRETCH:] + drun_q
-            drun = drun + jnp.where(iota((STRETCH, 1), 0) == STRETCH - 1, at_last, 0.0)
-            lane = 2 * heads + head
-            drun_all = jnp.where(lanes == lane, drun, drun_all)
-            dbeta_all = jnp.where(lanes == head, dbeta[:STRETCH], dbeta_all)
-            dbeta_all = jnp.where(lanes == heads + head, dbeta[STRETCH:], dbeta_all)
-            sums = jnp.sum(e_a, axis=0, keepdims=True) + jnp.sum(e_m, axis=0, keepdims=True)
-            column_sums = jnp.where(wide_rows == lane, sums, column_sums)
-        down = column_sums.T
-        drun_all = drun_all - down[:STRETCH] - down[STRETCH:]
-        daux_ref[rows, :] = jnp.where(lanes < 2 * heads, dbeta_all, dot6(upper, drun_all))
-        return carry
-
-    lax.fori_loop(0, blocks, back, 0)
-
-
 VMEM = pl.BlockSpec(memory_space=pltpu.VMEM)
-
-
-def mixer_bwd(q, k, v, aux, gate, gain, mixed, inv, state, pseudo, dgated):
-    seq, width = q.shape
-    heads = width // DK
-    shape = jax.ShapeDtypeStruct
-    return pl.pallas_call(
-        functools.partial(mixer_bwd_kernel, heads),
-        out_shape=(
-            shape((seq, width), F32),
-            shape(k.shape, BF),
-            shape(v.shape, BF),
-            shape((seq, DK), F32),
-            shape((seq, width), BF),
-            shape((1, DK), F32),
-        ),
-        in_specs=[VMEM] * 11,
-        out_specs=(VMEM,) * 6,
-        scratch_shapes=[pltpu.VMEM((heads, DK, DK), F32)],
-        compiler_params=pltpu.CompilerParams(vmem_limit_bytes=48 << 20),
-        name="mixer_backward",
-    )(q, k, v, aux, gate, gain, mixed, inv, state, pseudo, dgated)
 
 
 MESH = pl.DeviceIdType.MESH
@@ -266,7 +141,7 @@
     def behind(self, way, far):
         return self.dp - 4 * far if way == 0 else self.dp + 4 * far
 
-    def enter(self, plane=True, peer=True):
+    def enter(self, plane=True, peer=True, everyone=False):
         barrier = pltpu.get_barrier_semaphore()
 
         def greet(device):
@@ -279,9 +154,16 @@
         if plane:
             greet(self.sibling)
             greet(self.across)
+            count = count + 2
+        if everyone:
+            for z in range(self.line):
+                device = (z * 4 + self.x * 2 + self.c, self.side)
+                pl.when(z != self.z)(functools.partial(greet, device))
+            count = count + self.line - 1
+        elif plane:
             for way in (0, 1):
                 pl.when(self.can_send[way])(functools.partial(greet, self.ahead[way]))
-            count = count + 2 + self.can_send[0].astype(jnp.int32) + self.can_send[1].astype(jnp.int32)
+            count = count + self.can_send[0].astype(jnp.int32) + self.can_send[1].astype(jnp.int32)
         pl.semaphore_wait(barrier, count)
 
 
@@ -701,40 +583,783 @@
     )(x, docs, norm, wq, wg, wk, wv, scal, rest, rates, cq, ck, cv, mix)
 
 
+CHUNK = 128
+
+
+def chunk_rows(index):
+    return pl.ds(pl.multiple_of(index * CHUNK, CHUNK), CHUNK)
+
+
+def flat(ref, start, width):
+    return ref[:, :, start : start + width].reshape(-1, width)
+
+
+def put_blocks(ref, index, cols, value):
+    depth = ref.shape[3]
+    count = DK // depth
+    value = value.astype(BF)
+    if count == 2:
+        ref[index // 2, index % 2, :, :, cols] = value.reshape(2, depth, value.shape[-1])
+    else:
+        ref[pl.ds(index * (count // 4), count // 4), :, :, :, cols] = value.reshape(
+            count // 4, 2, 2, depth, value.shape[-1]
+        )
+
+
+def ffn_kernel(
+    line, gated_ref, x_ref, cot_ref, weight_ref, gain_ref, w_ref,
+    middle_ref, back_ref, dgated_ref, part_ref, grad_ref, dgain_ref,
+    attn_own, attn_in, in_own, in_in, normed, seed_low, hidden, gu_back, attn_back,
+    a_send, a_recv, f_send, f_recv,
+):
+    place = Place(line)
+    place.enter(plane=False)
+    seq, width = x_ref.shape
+    half = gated_ref.shape[1]
+    ff = (w_ref.shape[-1] - half) // 3
+    chunks = seq // CHUNK
+    gate_up = (half, 2 * ff)
+    down = (half + 2 * ff, ff)
+
+    def attn_copy(index):
+        rows = chunk_rows(index)
+        return remote(attn_own.at[rows], attn_in.at[rows], a_send.at[index], a_recv.at[index], place.peer)
+
+    def in_copy(index):
+        rows = chunk_rows(index)
+        return remote(in_own.at[rows], in_in.at[rows], f_send.at[index], f_recv.at[index], place.peer)
+
+    def project(index, carry):
+        rows = chunk_rows(index)
+        attn_own[rows, :] = product(gated_ref[rows, :], flat(w_ref, 0, half), NT).astype(BF)
+        attn_copy(index).start()
+        return carry
+
+    lax.fori_loop(0, chunks, project, 0)
+    dgain_ref[...] = jnp.zeros_like(dgain_ref)
+
+    def feed(index, carry):
+        rows = chunk_rows(index)
+        attn_copy(index).wait_recv()
+        middle = x_ref[rows, :].astype(F32) + (attn_own[rows, :].astype(F32) + attn_in[rows, :].astype(F32))
+        middle_ref[rows, :] = middle
+        scale = lax.rsqrt(jnp.mean(middle * middle, axis=-1, keepdims=True) + 1e-06)
+        low = (middle * scale * gain_ref[...]).astype(BF)
+        normed[rows, :] = low
+        both = product(low, flat(w_ref, *gate_up))
+        gate_in, up_in = both[:, :ff], both[:, ff:]
+        sigmoid = jax.nn.sigmoid(gate_in)
+        silu = gate_in * sigmoid
+        seed = (cot_ref[rows, :].astype(F32) * weight_ref[...]).astype(BF)
+        seed_low[rows, :] = seed
+        hidden_back = product(seed, flat(w_ref, *down))
+        gate_back = (hidden_back * up_in * (sigmoid * (1.0 + gate_in * (1.0 - sigmoid)))).astype(BF)
+        up_back = (hidden_back * silu).astype(BF)
+        gu_back[rows, 0:ff] = gate_back
+        gu_back[rows, ff : 2 * ff] = up_back
+        in_own[rows, :] = product(gu_back[rows, :], flat(w_ref, *gate_up), NT).astype(BF)
+        in_copy(index).start()
+        low_hidden = (silu * up_in).astype(BF)
+        hidden[rows, :] = low_hidden
+        part_ref[rows, :] = product(low_hidden, flat(w_ref, *down), NT).astype(BF)
+        return carry
+
+    lax.fori_loop(0, chunks, feed, 0)
+
+    def weigh(index, carry):
+        cols = pl.ds(pl.multiple_of(index * DK, DK), DK)
+        put_blocks(grad_ref, index, slice(half + 2 * ff, half + 3 * ff), product(seed_low[:, cols], hidden[...], TN))
+        put_blocks(grad_ref, index, slice(half, half + 2 * ff), product(normed[:, cols], gu_back[...], TN))
+        return carry
+
+    lax.fori_loop(0, width // DK, weigh, 0)
+
+    def finish(index, carry):
+        rows = chunk_rows(index)
+        in_copy(index).wait_recv()
+        grad = in_own[rows, :].astype(F32) + in_in[rows, :].astype(F32)
+        middle = middle_ref[rows, :]
+        scale = lax.rsqrt(jnp.mean(middle * middle, axis=-1, keepdims=True) + 1e-06)
+        unit = middle * scale
+        dgain_ref[...] += jnp.sum(grad * unit, axis=0, keepdims=True)
+        grad = grad * gain_ref[...]
+        seed = cot_ref[rows, :].astype(F32) * weight_ref[...]
+        total = seed + scale * (grad - unit * jnp.mean(unit * grad, axis=-1, keepdims=True))
+        back_ref[rows, :] = total
+        low = total.astype(BF)
+        attn_back[rows, :] = low
+        dgated_ref[rows, :] = product(low, flat(w_ref, 0, half))
+        return carry
+
+    lax.fori_loop(0, chunks, finish, 0)
+
+    def weigh_out(index, carry):
+        cols = pl.ds(pl.multiple_of(index * DK, DK), DK)
+        put_blocks(grad_ref, index, slice(0, half), product(attn_back[:, cols], gated_ref[...], TN))
+        return carry
+
+    lax.fori_loop(0, width // DK, weigh_out, 0)
+
+    def sent(index, carry):
+        attn_copy(index).wait_send()
+        in_copy(index).wait_send()
+        return carry
+
+    lax.fori_loop(0, chunks, sent, 0)
+
+
+def ffn_call(line, gated, x, cot, weight, gain, w):
+    seq, width = x.shape
+    half = gated.shape[1]
+    devices, depth, tail = w.shape
+    ff = (tail - half) // 3
+    shape = jax.ShapeDtypeStruct
+    dma = pltpu.SemaphoreType.DMA
+    chunks = seq // CHUNK
+    low = pltpu.VMEM((seq, width), BF)
+    return pl.pallas_call(
+        functools.partial(ffn_kernel, line),
+        out_shape=(
+            shape((seq, width), F32),
+            shape((seq, width), F32),
+            shape((seq, half), F32),
+            shape((seq, width), BF),
+            shape((line, 2, 2, depth, tail), BF),
+            shape((1, width), F32),
+        ),
+        in_specs=[VMEM] * 6,
+        out_specs=(VMEM,) * 6,
+        scratch_shapes=[low] * 6
+        + [pltpu.VMEM((seq, ff), BF), pltpu.VMEM((seq, 2 * ff), BF), low]
+        + [dma((chunks,))] * 4,
+        compiler_params=pltpu.CompilerParams(
+            collective_id=1, has_side_effects=True, vmem_limit_bytes=56 << 20
+        ),
+        name="feed_forward",
+    )(gated, x, cot, weight, gain, w)
+
+
+def scatter_sems(line, parts):
+    dma = pltpu.SemaphoreType.DMA
+    return [dma((2, parts))] * 4 + [dma((parts,))] * 2 + [dma((2, line, parts))] * 2
+
+
+def scatter_scratch(line, depth, width, own):
+    slots = [pltpu.VMEM((2, line, depth, width), BF), pltpu.VMEM((line, depth, width), BF),
+             pltpu.VMEM((2, line, depth, width), BF)]
+    return slots + ([pltpu.VMEM((2, line, depth, width), BF)] if own else [])
+
+
+class Scatter:
+    def __init__(self, place, grad, out, cuts, slots, sems, own=None):
+        self.place, self.grad, self.out, self.cuts, self.own = place, grad, out, cuts, own
+        self.mid, self.far, self.path = slots
+        self.cs, self.cr, self.ls, self.lr, self.xs, self.xr, self.zs, self.zr = sems
+
+    def cols(self, part):
+        start, width = self.cuts[part]
+        return pl.ds(start, width)
+
+    def column(self, which):
+        return 1 - self.place.x if which == 0 else self.place.x
+
+    def sibling_copy(self, part, which):
+        place, cols, x = self.place, self.cols(part), self.column(which)
+        return remote(
+            self.grad.at[:, x, 1 - place.c, :, cols], self.mid.at[which, :, :, cols],
+            self.cs.at[which, part], self.cr.at[which, part], place.sibling,
+        )
+
+    def own_copy(self, part, which):
+        cols, x = self.cols(part), self.column(which)
+        return pltpu.make_async_copy(
+            self.grad.at[:, x, self.place.c, :, cols], self.own.at[which, :, :, cols], self.ls.at[which, part]
+        )
+
+    def across_copy(self, part):
+        cols = self.cols(part)
+        return remote(
+            self.mid.at[0, :, :, cols], self.far.at[:, :, cols], self.xs.at[part], self.xr.at[part], self.place.across
+        )
+
+    def line_copy(self, part, way, target):
+        cols = self.cols(part)
+        ref = self.path.at[way, target, :, cols]
+        return remote(
+            self.mid.at[1, target, :, cols], ref,
+            self.zs.at[way, target, part], self.zr.at[way, target, part], self.place.ahead[way],
+        )
+
+    def pass_copy(self, part, way, target):
+        cols = self.cols(part)
+        ref = self.path.at[way, target, :, cols]
+        return remote(
+            ref, ref, self.zs.at[way, target, part], self.zr.at[way, target, part], self.place.ahead[way]
+        )
+
+    def begin(self, part):
+        for which in (0, 1):
+            if self.own is not None:
+                self.own_copy(part, which).start()
+            self.sibling_copy(part, which).start()
+
+    def merge(self, part, which):
+        self.sibling_copy(part, which).wait_recv()
+        if self.own is not None:
+            self.own_copy(part, which).wait()
+        cols = self.cols(part)
+        for target in range(self.place.line):
+            if self.own is not None:
+                mine = self.own[which, target, :, cols]
+            else:
+                mine = self.grad[target, self.column(which), self.place.c, :, cols]
+            both = self.mid[which, target, :, cols].astype(F32) + mine.astype(F32)
+            self.mid[which, target, :, cols] = both.astype(BF)
+        if which == 0:
+            self.across_copy(part).start()
+
+    def join(self, part):
+        self.across_copy(part).wait_recv()
+        cols = self.cols(part)
+        for target in range(self.place.line):
+            both = self.mid[1, target, :, cols].astype(F32) + self.far[target, :, cols].astype(F32)
+            self.mid[1, target, :, cols] = both.astype(BF)
+
+    def relay(self, part, way, target):
+        place, cols = self.place, self.cols(part)
+        ahead = target > place.z if way == 0 else target < place.z
+        first = place.z == 0 if way == 0 else place.z == place.line - 1
+
+        def start():
+            self.line_copy(part, way, target).start()
+
+        def go_on():
+            self.pass_copy(part, way, target).wait_recv()
+            both = self.path[way, target, :, cols].astype(F32) + self.mid[1, target, :, cols].astype(F32)
+            self.path[way, target, :, cols] = both.astype(BF)
+            self.pass_copy(part, way, target).start()
+
+        pl.when(ahead & first)(start)
+        pl.when(ahead & jnp.logical_not(first))(go_on)
+
+    def relays(self, part, distance):
+        self.relay(part, 0, self.place.line - 1 - distance)
+        self.relay(part, 1, distance)
+
+    def end(self, part):
+        place, cols = self.place, self.cols(part)
+        start, width = self.cuts[part]
+        z = place.z
+        self.out[:, cols] = self.mid[1, z, :, cols].astype(F32)
+
+        def take(way):
+            self.pass_copy(part, way, z).wait_recv()
+            self.out[:, cols] += self.path[way, z, :, cols].astype(F32)
+
+        pl.when(z > 0)(functools.partial(take, 0))
+        pl.when(z < place.line - 1)(functools.partial(take, 1))
+
+    def drain(self, part):
+        place = self.place
+        for which in (0, 1):
+            self.sibling_copy(part, which).wait_send()
+        self.across_copy(part).wait_send()
+        for target in range(place.line):
+            for way in (0, 1):
+                ahead = target > place.z if way == 0 else target < place.z
+                pl.when(ahead)(lambda way=way, target=target: self.pass_copy(part, way, target).wait_send())
+
+    def stages(self, part):
+        line = self.place.line
+        return [functools.partial(self.join, part)] + [
+            functools.partial(self.relays, part, distance) for distance in range(line - 1)
+        ]
+
+
+def back_kernel(
+    line, heads, q_ref, k_ref, v_ref, aux_ref, pre_ref, docs_ref, conv_ref, rates_ref, mix_ref, mixed_ref, inv_ref,
+    state_ref, pseudo_ref, dgated_ref, middle_ref, part_ref, grad_ref,
+    dpre_ref, dconv_ref, dscal_ref, dgain_ref, sum_ref, out_ref,
+    dstate, doc_cols, dy_next, part_in, mid, far, path, own, o_send, o_recv, *sems,
+):
+    place = Place(line)
+    side = place.side
+    place.enter()
+    seq, half = q_ref.shape
+    blocks = seq // STRETCH
+    span = 2 * STRETCH
+    tail = sum_ref.shape[-1]
+    ff = (tail - half) // 3
+    cuts = [(half, ff), (half + ff, ff), (half + 2 * ff, ff), (0, half)]
+    scatter = Scatter(place, grad_ref, sum_ref, cuts, (mid, far, path), sems, own)
+    parts = range(len(cuts))
+    for part in parts:
+        scatter.begin(part)
+    swap = remote(part_ref, part_in, o_send, o_recv, place.peer)
+    swap.start()
+
+    masks = block_masks()
+    t_row, t_col, p_row, p_col = masks
+    strict = p_row > p_col
+    for head in range(heads):
+        dstate[head] = jnp.zeros((DK, DK), F32)
+    dgain_ref[...] = jnp.zeros_like(dgain_ref)
+    dconv_ref[...] = jnp.zeros_like(dconv_ref)
+    dscal_ref[...] = jnp.zeros_like(dscal_ref)
+    dy_next[...] = jnp.zeros_like(dy_next)
+    doc_cols[0:PAD, :] = jnp.full((PAD, DK), -1.0, F32)
+    doc_cols[PAD + seq :, :] = jnp.full((PAD, DK), -1.0, F32)
+    for i in range(seq // DK):
+        lane_docs = docs_ref[:, i * DK : (i + 1) * DK].astype(F32)
+        doc_cols[PAD + i * DK : PAD + (i + 1) * DK, :] = jnp.broadcast_to(lane_docs, (DK, DK)).T
+    upper = (iota((STRETCH, STRETCH), 0) <= iota((STRETCH, STRETCH), 1)).astype(F32)
+    lanes = iota((STRETCH, DK), 1)
+    wide_rows = iota((span, DK), 0)
+    select = scalar_select(side, heads)
+    rate = -jnp.exp(rates_ref[0:1, :])
+    scal_at = 6 * half
+    scal_cols = slice(scal_at, scal_at + DK)
+
+    work = [functools.partial(scatter.merge, part, which) for part in parts for which in (0, 1)]
+    chain = [step for part in parts for step in scatter.stages(part) + [functools.partial(scatter.end, part)]]
+    slots = deal(work, 2) + [[]] + deal(chain[: len(chain) * 2 // 3], blocks - 3)
+    left = chain[len(chain) * 2 // 3 :]
+
+    def back(step, carry):
+        block = blocks - 1 - step
+        top = pl.multiple_of(block * STRETCH, STRETCH)
+        rows = pl.ds(top, STRETCH)
+        aux = aux_ref[rows, :]
+        aux2, run2, aux_t, run_t = block_scalars(aux)
+        doc_window = doc_cols[pl.ds(top, STRETCH + 2 * PAD), :]
+        same = same_documents(doc_window[: STRETCH + PAD])
+        here = doc_window[PAD : PAD + STRETCH]
+        same_next = [doc_window[PAD + o : PAD + o + STRETCH] == here for o in range(1, KW)]
+        dbeta_all = jnp.zeros((STRETCH, DK), F32)
+        drun_all = jnp.zeros((STRETCH, DK), F32)
+        column_sums = jnp.zeros((span, DK), F32)
+
+        def conv_back(kind, head, grad):
+            first_col = (0, 2, 3, 4, 5)[kind] * half + head * DK
+            cols = slice(head * DK, (head + 1) * DK)
+            window = pre_ref[pl.ds(top, STRETCH + PAD), first_col : first_col + DK]
+            kernel = conv_ref[kind, :, cols]
+            shifted = [window[PAD:]] + [
+                jnp.where(same[o - 1], window[PAD - o : PAD - o + STRETCH], 0.0) for o in range(1, KW)
+            ]
+            y = shifted[0] * kernel[0:1]
+            for o in range(1, KW):
+                y = y + shifted[o] * kernel[o : o + 1]
+            sigmoid = jax.nn.sigmoid(y)
+            act = y * sigmoid
+            if kind < 3:
+                scale = lax.rsqrt(jnp.sum(act * act, axis=-1, keepdims=True) + 1e-06)
+                unit = act * scale
+                if kind == 0:
+                    grad = grad * DK ** (-0.5)
+                grad = scale * (grad - unit * jnp.sum(unit * grad, axis=-1, keepdims=True))
+            dy = grad * (sigmoid * (1.0 + y * (1.0 - sigmoid)))
+            for o in range(KW):
+                dconv_ref[kind, o : o + 1, cols] += jnp.sum(dy * shifted[o], axis=0, keepdims=True)
+            at = slice(kind * half + head * DK, kind * half + (head + 1) * DK)
+            longer = jnp.concatenate([dy, dy_next[:, at]], axis=0)
+            dy_next[:, at] = dy[:PAD]
+            dpre = dy * kernel[0:1]
+            for o in range(1, KW):
+                dpre = dpre + jnp.where(same_next[o - 1], longer[o : o + STRETCH], 0.0) * kernel[o : o + 1]
+            dpre_ref[rows, first_col : first_col + DK] = dpre.astype(BF)
+
+        for head in range(heads):
+            cols = slice(head * DK, (head + 1) * DK)
+            gate_cols = slice(half + head * DK, half + (head + 1) * DK)
+            beta, run_col, run_row, doc_col, doc_row, carried, to_last = head_terms(
+                aux, aux2, run2, aux_t, run_t, head, heads
+            )
+            decay = decay_matrix(run_col, run_row, doc_col, doc_row, p_row, p_col)
+            keys = jnp.concatenate([k_ref[0, rows, cols], k_ref[1, rows, cols]], axis=0)
+            queries = q_ref[rows, cols]
+            mixed = mixed_ref[rows, cols]
+            gate = pre_ref[pl.ds(top + PAD, STRETCH), gate_cols]
+            sigmoid = jax.nn.sigmoid(gate)
+            silu = gate * sigmoid
+            scale = lax.rsqrt(jnp.mean(mixed * mixed, axis=-1, keepdims=True) + 1e-05)
+            scaled = mixed * scale
+            dgated = dgated_ref[rows, cols]
+            part = dgated * scaled
+            dpre_ref[rows, gate_cols] = (
+                part * mix_ref[...] * (sigmoid * (1.0 + gate * (1.0 - sigmoid)))
+            ).astype(BF)
+            dgain_ref[...] += jnp.sum(part * silu, axis=0, keepdims=True)
+            dscaled = dgated * mix_ref[...] * silu
+            dout = scale * (dscaled - scaled * jnp.mean(dscaled * scaled, axis=-1, keepdims=True))
+
+            index = block * heads + head
+            state, pseudo = state_ref[index], pseudo_ref[index]
+            dnext = dstate[head]
+            dnext_parts, state_parts, pseudo_parts = split(dnext), split(state), split(pseudo)
+            dout_parts, q_parts = split(dout), split(queries)
+            gram = dot1(keys, keys, NT)
+            core = jnp.where(strict, decay * gram, 0.0)
+            amat = beta * core
+            qdecay = decay[STRETCH:]
+            attn = qdecay * dot3(q_parts, keys, NT)
+            dattn = dot3(dout_parts, pseudo_parts, NT)
+            dqk = split(qdecay * dattn)
+            dpseudo = dot3(attn, dout_parts, TN) + to_last * dot3(keys, dnext_parts)
+            dtarget = dot3(inv_ref[index], dpseudo, TN)
+            dtarget_parts = split(dtarget)
+            damat = jnp.where(strict, -dot3(dtarget_parts, pseudo_parts, NT), 0.0)
+            e_a, e_m = damat * amat, dattn * attn
+            dgram = split(beta * decay * damat)
+            dbeta = jnp.sum(dtarget * pseudo, axis=-1, keepdims=True) / jnp.maximum(beta, 1e-30)
+            dvalues = (beta * dtarget).astype(BF).astype(F32)
+            dread = -(beta * carried) * dtarget
+            dout_c = carried[STRETCH:] * dout
+            dread_parts, dout_c_parts = split(dread), split(dout_c)
+            last = carried[span - 1 : span]
+            dstate[head] = last * dnext + dot3(keys, dread_parts, TN) + dot3(q_parts, dout_c_parts, TN)
+            dq_state = dot3(dout_c_parts, state_parts, NT)
+            dk_state = dot3(dread_parts, state_parts, NT)
+            dk_last = dot3(to_last * pseudo, dnext_parts, NT)
+            conv_back(0, head, dq_state + dot3(dqk, keys))
+            dkeys = (
+                dk_state + dk_last + dot3(dgram, keys) + dot3(dgram, keys, TN) + dot3(dqk, q_parts, TN)
+            ).astype(BF).astype(F32)
+            conv_back(1, head, dkeys[:STRETCH])
+            conv_back(2, head, dkeys[STRETCH:])
+            conv_back(3, head, dvalues[:STRETCH])
+            conv_back(4, head, dvalues[STRETCH:])
+
+            wide = keys.astype(F32)
+            e_last = jnp.sum(wide * dk_last, axis=-1, keepdims=True)
+            drun = jnp.sum(e_a, axis=-1, keepdims=True) - e_last + jnp.sum(wide * dk_state, axis=-1, keepdims=True)
+            drun_q = jnp.sum(e_m, axis=-1, keepdims=True) + jnp.sum(queries * dq_state, axis=-1, keepdims=True)
+            at_last = jnp.sum(e_last, axis=0, keepdims=True) + last * jnp.sum(
+                jnp.sum(dnext * state, axis=-1, keepdims=True), axis=0, keepdims=True
+            )
+            drun = drun[:STRETCH] + drun[STRETCH:] + drun_q
+            drun = drun + jnp.where(iota((STRETCH, 1), 0) == STRETCH - 1, at_last, 0.0)
+            lane = 2 * heads + head
+            drun_all = jnp.where(lanes == lane, drun, drun_all)
+            dbeta_all = jnp.where(lanes == head, dbeta[:STRETCH], dbeta_all)
+            dbeta_all = jnp.where(lanes == heads + head, dbeta[STRETCH:], dbeta_all)
+            sums = jnp.sum(e_a, axis=0, keepdims=True) + jnp.sum(e_m, axis=0, keepdims=True)
+            column_sums = jnp.where(wide_rows == lane, sums, column_sums)
+        down = column_sums.T
+        ddecay = dot6(upper, drun_all - down[:STRETCH] - down[STRETCH:])
+        raw = dot6(pre_ref[pl.ds(top + PAD, STRETCH), scal_cols], select)
+        sigmoid = jax.nn.sigmoid(raw)
+        shifted = raw + rates_ref[1:2, :]
+        draw_decay = ddecay * rate * jax.nn.sigmoid(shifted)
+        is_decay = (lanes >= 2 * heads) & (lanes < 3 * heads)
+        draw_decay = jnp.where(is_decay, draw_decay, 0.0)
+        dscal_ref[0:1, :] += jnp.sum(
+            jnp.where(is_decay, ddecay * rate * softplus(shifted), 0.0), axis=0, keepdims=True
+        )
+        dscal_ref[1:2, :] += jnp.sum(draw_decay, axis=0, keepdims=True)
+        dbeta_low = dbeta_all.astype(BF).astype(F32)
+        draw = jnp.where(lanes < 2 * heads, dbeta_low * 2.0 * sigmoid * (1.0 - sigmoid), draw_decay)
+        dpre_ref[rows, scal_cols] = dot6(draw, select, NT).astype(BF)
+        run_slot(slots, step)
+        return carry
+
+    lax.fori_loop(0, blocks, back, 0)
+    swap.wait_recv()
+
+    def outputs(block, carry):
+        rows = pl.ds(pl.multiple_of(block * STRETCH, STRETCH), STRETCH)
+        total = part_ref[rows, :].astype(F32) + part_in[rows, :].astype(F32)
+        out_ref[rows, :] = (middle_ref[rows, :] + total).astype(BF)
+        return carry
+
+    lax.fori_loop(0, blocks, outputs, 0)
+    for step in left:
+        step()
+    swap.wait_send()
+    for part in parts:
+        scatter.drain(part)
+
+
+def back_call(line, q, k, v, aux, pre, docs, conv, rates, mix, mixed, inv, state, pseudo, dgated, middle, part, grad):
+    seq, half = q.shape
+    heads = half // DK
+    depth, tail = grad.shape[3:]
+    shape = jax.ShapeDtypeStruct
+    dma = pltpu.SemaphoreType.DMA
+    return pl.pallas_call(
+        functools.partial(back_kernel, line, heads),
+        out_shape=(
+            shape((seq, pre.shape[1]), BF),
+            shape(conv.shape, F32),
+            shape((2, DK), F32),
+            shape((1, DK), F32),
+            shape((depth, tail), F32),
+            shape(part.shape, BF),
+        ),
+        in_specs=[VMEM] * 16 + [pl.BlockSpec(memory_space=pl.ANY)],
+        out_specs=(VMEM,) * 6,
+        scratch_shapes=[
+            pltpu.VMEM((heads, DK, DK), F32),
+            pltpu.VMEM((seq + 2 * PAD, DK), F32),
+            pltpu.VMEM((PAD, 5 * half), F32),
+            pltpu.VMEM(part.shape, BF),
+        ]
+        + scatter_scratch(line, depth, tail, True)
+        + [dma, dma]
+        + scatter_sems(line, 4),
+        compiler_params=pltpu.CompilerParams(
+            collective_id=2, has_side_effects=True, vmem_limit_bytes=60 << 20
+        ),
+        name="mixer_backward",
+    )(q, k, v, aux, pre, docs, conv, rates, mix, mixed, inv, state, pseudo, dgated, middle, part, grad)
+
+
+def tail_kernel(
+    line, heads, x_ref, norm_ref, dpre_ref, w_ref, back_ref, dconv_ref, dscal_ref, dmix_ref, dffn_ref,
+    out_ref, gq_ref, gg_ref, gk_ref, gv_ref, gs_ref, gcq_ref, gck_ref, gcv_ref, gnorm_ref, gffn_ref, gtiny_ref,
+    normed, nb_own, nb_in, grad, total, mid, far, path, small, small_in, small_line, small_sum, mix_in, scal_in,
+    n_send, n_recv, h_send, h_recv, m_send, m_recv, l_send, l_recv, *sems,
+):
+    place = Place(line)
+    side, me = place.side, place.dp
+    place.enter(everyone=True)
+    seq, width = x_ref.shape
+    half = gq_ref.shape[1]
+    chunks = seq // CHUNK
+    scal_at = 6 * half
+    mix_swap = remote(dmix_ref, mix_in, m_send.at[2], m_recv.at[2], place.peer)
+    mix_swap.start()
+
+    def normalise(index, carry):
+        rows = chunk_rows(index)
+        x = x_ref[rows, :].astype(F32)
+        scale = lax.rsqrt(jnp.mean(x * x, axis=-1, keepdims=True) + 1e-06)
+        normed[rows, :] = (x * scale * norm_ref[...]).astype(BF)
+        return carry
+
+    lax.fori_loop(0, chunks, normalise, 0)
+
+    def weigh(index, carry):
+        cols = pl.ds(pl.multiple_of(index * DK, DK), DK)
+        put_blocks(grad, index, slice(0, scal_at + DK), product(normed[:, cols], dpre_ref[...], TN))
+        return carry
+
+    lax.fori_loop(0, width // DK, weigh, 0)
+    cuts = [(2 * half, 2 * half), (4 * half, 2 * half + DK), (0, 2 * half)]
+    scatter = Scatter(place, grad, total, cuts, (mid, far, path), sems)
+    parts = range(len(cuts))
+    for part in parts:
+        scatter.begin(part)
+
+    def nb_copy(index):
+        rows = chunk_rows(index)
+        return remote(nb_own.at[rows], nb_in.at[rows], n_send.at[index], n_recv.at[index], place.peer)
+
+    merges = [functools.partial(scatter.merge, part, which) for part in parts for which in (0, 1)]
+    merge_slots = deal(merges, chunks)
+
+    def project(index, carry):
+        rows = chunk_rows(index)
+        nb_own[rows, :] = product(dpre_ref[rows, :], flat(w_ref, 0, scal_at + DK), NT).astype(BF)
+        nb_copy(index).start()
+        run_slot(merge_slots, index)
+        return carry
+
+    lax.fori_loop(0, chunks, project, 0)
+    gnorm_ref[...] = jnp.zeros_like(gnorm_ref)
+
+    def finish(index, carry):
+        rows = chunk_rows(index)
+        nb_copy(index).wait_recv()
+        back = nb_own[rows, :].astype(F32) + nb_in[rows, :].astype(F32)
+        x = x_ref[rows, :].astype(F32)
+        scale = lax.rsqrt(jnp.mean(x * x, axis=-1, keepdims=True) + 1e-06)
+        unit = x * scale
+        gnorm_ref[...] += jnp.sum(back * unit, axis=0, keepdims=True)
+        back = back * norm_ref[...]
+        total_back = back_ref[rows, :] + scale * (back - unit * jnp.mean(unit * back, axis=-1, keepdims=True))
+        out_ref[rows, :] = total_back.astype(BF)
+        return carry
+
+    small_swaps = [
+        remote(small, small_in.at[0], m_send.at[0], m_recv.at[0], place.sibling),
+        remote(small_sum, small_in.at[1], m_send.at[1], m_recv.at[1], place.across),
+    ]
+
+    def line_copy(target):
+        device = (target * 4 + place.x * 2 + place.c, side)
+        return remote(small_line.at[place.z], small_line.at[place.z], l_send.at[target], l_recv.at[place.z], device)
+
+    def line_from(source):
+        device = (source * 4 + place.x * 2 + place.c, side)
+        return remote(small_line.at[source], small_line.at[source], l_send.at[source], l_recv.at[source], device)
+
+    def collect():
+        mix_swap.wait_recv()
+        small[0:5] = dconv_ref[...]
+        for i in range(2):
+            small[5, i : i + 1, :] = gnorm_ref[:, i * half : (i + 1) * half]
+            small[5, 2 + i : 3 + i, :] = dffn_ref[:, i * half : (i + 1) * half]
+        small[6] = jnp.zeros((KW, half), F32)
+        small[6, 0:1, 0:DK] = dmix_ref[...] + mix_in[...]
+        small[6, 0:1, DK : 2 * DK] = dscal_ref[0:1, :]
+        small[6, 0:1, 2 * DK : 3 * DK] = dscal_ref[1:2, :]
+        small_swaps[0].start()
+
+    def collect_across():
+        small_swaps[0].wait_recv()
+        small_sum[...] = small[...] + small_in[0]
+        small_swaps[1].start()
+
+    def collect_line():
+        small_swaps[1].wait_recv()
+        small_line[place.z] = small_sum[...] + small_in[1]
+        for target in range(line):
+            pl.when(target != place.z)(lambda target=target: line_copy(target).start())
+
+    home = [
+        remote(
+            total.at[:, pl.ds(pl.multiple_of((base + 1 - side) * half, half), half)],
+            ref.at[:, pl.ds(pl.multiple_of(side * half, half), half)],
+            h_send.at[i], h_recv.at[i], place.peer,
+        )
+        for i, (base, ref) in enumerate(((2, gk_ref), (4, gv_ref)))
+    ]
+    scal_home = remote(total.at[:, scal_at : scal_at + DK], scal_in, h_send.at[2], h_recv.at[2], place.peer)
+    own_half = pl.ds(pl.multiple_of(side * half, half), half)
+
+    def at_home(i):
+        base, ref = ((2, gk_ref), (4, gv_ref))[i]
+        home[i].start()
+        ref[:, own_half] = total[:, pl.ds(pl.multiple_of((base + side) * half, half), half)]
+
+    def at_home_value():
+        at_home(1)
+        scal_home.start()
+
+    chain = []
+    for part in parts:
+        chain += scatter.stages(part) + [functools.partial(scatter.end, part)]
+        if part == 0:
+            chain.append(functools.partial(at_home, 0))
+        if part == 1:
+            chain.append(at_home_value)
+    mid_way = len(scatter.stages(0)) + 2
+    slots = deal(chain[:mid_way], chunks)
+
+    def finish_and(index, carry):
+        finish(index, carry)
+        run_slot(slots, index)
+        return carry
+
+    lax.fori_loop(0, chunks, finish_and, 0)
+    rest = chain[mid_way:]
+    extra = [collect, collect_across, collect_line]
+    for i, step in enumerate(rest):
+        if i % 2 == 0 and extra:
+            extra.pop(0)()
+        step()
+    for step in extra:
+        step()
+    for source in range(line):
+        pl.when(source != place.z)(lambda source=source: line_from(source).wait_recv())
+    summed = small_line[0]
+    for source in range(1, line):
+        summed = summed + small_line[source]
+    small_sum_out = summed
+    gcq_ref[...] = small_sum_out[0]
+    small_swaps[0].wait_send()
+    small_swaps[1].wait_send()
+    small[...] = small_sum_out
+    conv_home = [
+        remote(
+            small.at[base + 1 - side], ref.at[:, own_half], h_send.at[i], h_recv.at[i], place.peer
+        )
+        for i, (base, ref) in ((3, (1, gck_ref)), (4, (3, gcv_ref)))
+    ]
+    for copy in conv_home:
+        copy.start()
+    gck_ref[:, own_half] = small[1 + side]
+    gcv_ref[:, own_half] = small[3 + side]
+    for i in range(2):
+        gnorm_ref[:, i * half : (i + 1) * half] = small_sum_out[5, i : i + 1]
+        gffn_ref[:, i * half : (i + 1) * half] = small_sum_out[5, 2 + i : 3 + i]
+    gtiny_ref[...] = small_sum_out[6, 0:1, 0 : 3 * DK]
+    gq_ref[...] = total[:, 0:half]
+    gg_ref[...] = total[:, half : 2 * half]
+    scal_home.wait_recv()
+    lanes = iota(scal_in.shape, 1)
+    ours = total[:, scal_at : scal_at + DK]
+    theirs = pltpu.roll(scal_in[...], DK - 2 * heads, 1)
+    gs_ref[...] = jnp.where(lanes < 2 * heads, ours + theirs, ours)
+    for copy in home + conv_home:
+        copy.wait_recv()
+    for copy in home + conv_home + [scal_home, mix_swap]:
+        copy.wait_send()
+    for target in range(line):
+        pl.when(target != place.z)(lambda target=target: line_copy(target).wait_send())
+
+    def sent(index, carry):
+        nb_copy(index).wait_send()
+        return carry
+
+    lax.fori_loop(0, chunks, sent, 0)
+    for part in parts:
+        scatter.drain(part)
+
+
+def tail_call(line, heads, x, norm, dpre, w, back, dconv, dscal, dmix, dffn):
+    seq, width = x.shape
+    devices, depth, columns = w.shape
+    half = dconv.shape[-1]
+    shape = jax.ShapeDtypeStruct
+    dma = pltpu.SemaphoreType.DMA
+    chunks = seq // CHUNK
+    tiny = (7, KW, half)
+    return pl.pallas_call(
+        functools.partial(tail_kernel, line, heads),
+        out_shape=(
+            shape((seq, width), BF),
+            shape((depth, half), F32),
+            shape((depth, half), F32),
+            shape((depth, 2 * half), F32),
+            shape((depth, 2 * half), F32),
+            shape((depth, DK), F32),
+            shape((KW, half), F32),
+            shape((KW, 2 * half), F32),
+            shape((KW, 2 * half), F32),
+            shape((1, width), F32),
+            shape((1, width), F32),
+            shape((1, 3 * DK), F32),
+        ),
+        in_specs=[VMEM] * 9,
+        out_specs=(VMEM,) * 12,
+        scratch_shapes=[
+            pltpu.VMEM((seq, width), BF),
+            pltpu.VMEM((seq, width), BF),
+            pltpu.VMEM((seq, width), BF),
+            pltpu.VMEM((line, 2, 2, depth, columns), BF),
+            pltpu.VMEM((depth, columns), F32),
+        ]
+        + scatter_scratch(line, depth, columns, False)
+        + [
+            pltpu.VMEM(tiny, F32),
+            pltpu.VMEM((2,) + tiny, F32),
+            pltpu.VMEM((line,) + tiny, F32),
+            pltpu.VMEM(tiny, F32),
+            pltpu.VMEM((1, DK), F32),
+            pltpu.VMEM((depth, DK), F32),
+        ]
+        + [dma((chunks,)), dma((chunks,)), dma((5,)), dma((5,)), dma((3,)), dma((3,)), dma((line,)), dma((line,))]
+        + scatter_sems(line, 3),
+        compiler_params=pltpu.CompilerParams(
+            collective_id=3, has_side_effects=True, vmem_limit_bytes=56 << 20
+        ),
+        name="tail",
+    )(x, norm, dpre, w, back, dconv, dscal, dmix, dffn)
+
+
 GROUPS = 8
-
-
-def product(first, second, dims=NN):
-    return lax.dot_general(first, second, (dims, ((), ())), preferred_element_type=F32)
-
-
-def rms_scale(values, scales):
-    return values * lax.rsqrt(jnp.mean(values * values, axis=-1, keepdims=True) + 1e-06) * scales
-
-
-def unit_rows(values):
-    return values * lax.rsqrt(jnp.sum(values * values, axis=-1, keepdims=True) + 1e-06)
-
-
-def silu_grad(values):
-    sigmoid = jax.nn.sigmoid(values)
-    return sigmoid * (1.0 + values * (1.0 - sigmoid))
-
-
-def short_conv(signal, kernel, doc_ids):
-    seq_len = signal.shape[0]
-    summed = signal * kernel[0]
-    for offset in range(1, kernel.shape[0]):
-        shifted = jnp.pad(signal, ((offset, 0), (0, 0)))[:seq_len]
-        shifted_docs = jnp.pad(doc_ids, (offset, 0), constant_values=-1)[:seq_len]
-        same_doc = (shifted_docs == doc_ids).astype(F32)[:, None]
-        summed = summed + shifted * same_doc * kernel[offset]
-    return summed
-
-
-def unit_heads(values):
-    seq_len = values.shape[0]
-    return unit_rows(values.reshape(seq_len, -1, DK)).reshape(seq_len, -1)
 
 
 def per_device(
@@ -773,10 +1398,6 @@
     depth = w_query.shape[0]
     half = w_query.shape[1]
     heads = w_alpha.shape[1]
-    side = lax.axis_index("step")
-
-    def swap(array):
-        return lax.ppermute(array, "step", [(0, 1), (1, 0)])
 
     rest = jnp.concatenate([w_out.T, w_gate, w_up, w_down.T], axis=1)
     scal = jnp.concatenate(
@@ -789,116 +1410,38 @@
         scal, rest, rates, conv_query, conv_key[0], conv_value[0], gain_row,
     )
     ff = w_gate.shape[1]
-    front_w = front_w.reshape(-1, front_w.shape[-1])
-    back_w = back_w.reshape(-1, back_w.shape[-1])
-    inputs = tokens[0].astype(F32)
-    docs = doc_ids[0]
-    seq_len = inputs.shape[0]
-    normed_f, pull_first = jax.vjp(rms_scale, inputs, norm_gain)
-    normed = normed_f.astype(BF)
-    pre = pre[PAD:]
-    gate_pre = pre[:, half : 2 * half]
-
-    def prepare(pre_in, query_kernel, key_0, key_1, value_0, value_1, log_rates, rate_bias):
-        queries = unit_heads(jax.nn.silu(short_conv(pre_in[:, :half], query_kernel, docs))) * DK ** (-0.5)
-        keys = [
-            unit_heads(jax.nn.silu(short_conv(pre_in[:, (2 + i) * half : (3 + i) * half], kernel, docs)))
-            for i, kernel in enumerate((key_0, key_1))
-        ]
-        values = [
-            jax.nn.silu(short_conv(pre_in[:, (4 + i) * half : (5 + i) * half], kernel, docs))
-            for i, kernel in enumerate((value_0, value_1))
-        ]
-        scalars = pre_in[:, 6 * half :] @ scalar_select(side, heads)
-        betas = 2.0 * jax.nn.sigmoid(scalars[:, : 2 * heads])
-        decays = -jnp.exp(log_rates) * jax.nn.softplus(scalars[:, 2 * heads : 3 * heads] + rate_bias)
-        return (queries, jnp.stack(keys), jnp.stack(values), betas, decays)
-
-    _, pull_prepare = jax.vjp(
-        prepare, pre, conv[0], conv[1], conv[2], conv[3], conv[4], decay_log, decay_bias
+    weight_row = jnp.full((1, tokens.shape[2]), weight_here, F32)
+    middle, middle_back, gated_back, ffn_part, grad_back, grad_ffn_gain = ffn_call(
+        lax.axis_size("dp") // 4, gated, tokens[0], cotangent[0], weight_row, ffn_gain[None], back_w
     )
-
-    attention = lax.psum(product(gated, back_w[:, :half], NT).astype(BF), "step").astype(F32)
-    middle = inputs + attention
-    normed_ffn_f, pull_second = jax.vjp(rms_scale, middle, ffn_gain)
-    normed_ffn = normed_ffn_f.astype(BF)
-    gate_w, up_w, down_w = (back_w[:, half + i * ff : half + (i + 1) * ff] for i in range(3))
-    gate_in = product(normed_ffn, gate_w)
-    up_in = product(normed_ffn, up_w)
-    hidden = (jax.nn.silu(gate_in) * up_in).astype(BF)
-    ffn_out = lax.psum(product(hidden, down_w, NT).astype(BF), "step").astype(F32)
-    output = (middle + ffn_out).astype(BF)[None]
-
-    seed = cotangent[0].astype(F32) * weight_here
-    seed_low = seed.astype(BF)
-    grad_down = product(seed_low, hidden, TN)
-    hidden_back = product(seed_low, down_w)
-    gate_back = (hidden_back * up_in * silu_grad(gate_in)).astype(BF)
-    up_back = (hidden_back * jax.nn.silu(gate_in)).astype(BF)
-    grad_gate = product(normed_ffn, gate_back, TN)
-    grad_up = product(normed_ffn, up_back, TN)
-    ffn_in_back = lax.psum(
-        (product(gate_back, gate_w, NT) + product(up_back, up_w, NT)).astype(BF), "step"
-    ).astype(F32)
-    middle_norm_back, grad_ffn_gain = pull_second(ffn_in_back)
-    middle_back = seed + middle_norm_back
-    attn_back = middle_back.astype(BF)
-    grad_out = product(attn_back, gated, TN)
-    sum_back = lax.psum_scatter(
-        jnp.concatenate([grad_out, grad_gate, grad_up, grad_down], axis=1).astype(BF),
-        "dp", scatter_dimension=0, tiled=True,
-    ).astype(F32)
-    gated_back = product(attn_back, back_w[:, :half])
-    dq, dk, dv, daux, dgate, dgain = mixer_bwd(
-        queries, keys, values, aux, gate_pre, gain_row, mixed, inv, state, pseudo, gated_back
+    dpre_low, dconv, dscal, dgain, sum_back, output = back_call(
+        lax.axis_size("dp") // 4, queries, keys, values, aux, pre, doc_ids, conv, rates, gain_row, mixed, inv, state,
+        pseudo, gated_back, middle, ffn_part, grad_back,
     )
-    dbetas = daux[:, : 2 * heads].astype(BF).astype(F32)
-    ddecays = daux[:, 2 * heads : 3 * heads]
-    dpre, d_cq, d_k0, d_k1, d_v0, d_v1, d_log, d_bias = pull_prepare(
-        (dq, dk.astype(F32), dv.astype(F32), dbetas, ddecays)
+    output = output[None]
+    input_grad, g_query, g_outgate, g_key, g_value, g_scal, g_cq, g_ck, g_cv, g_norm, g_ffn, tiny = tail_call(
+        lax.axis_size("dp") // 4, heads, tokens[0], norm_gain[None], dpre_low, front_w, middle_back, dconv, dscal,
+        dgain, grad_ffn_gain,
     )
-    dpre_low = jnp.concatenate([dpre[:, :half].astype(BF), dgate, dpre[:, 2 * half :].astype(BF)], axis=1)
-    grad_front = product(normed, dpre_low, TN)
-    normed_back = lax.psum(product(dpre_low, front_w, NT).astype(BF), "step").astype(F32)
-    input_back, grad_norm_gain = pull_first(normed_back)
-    input_grad = (middle_back + input_back).astype(BF)[None]
-    sum_front = lax.psum_scatter(grad_front.astype(BF), "dp", scatter_dimension=0, tiled=True)
-
-    def home(parts):
-        mine = jnp.where(side == 0, parts[0], parts[1])
-        other = swap(jnp.where(side == 0, parts[1], parts[0]))
-        return jnp.where(
-            side == 0, jnp.concatenate([mine, other], axis=1), jnp.concatenate([other, mine], axis=1)
-        )
-
-    col = lambda i: sum_front[:, i * half : (i + 1) * half]
-    sum_key, sum_value = home([col(2), col(3)]), home([col(4), col(5)])
-    tail = sum_front[:, 6 * half :]
-    sum_beta = tail[:, : 2 * heads] + swap(tail[:, 2 * heads : 4 * heads])
-    small = lax.psum(
-        (grad_norm_gain, d_log, d_bias, d_cq, d_k0, d_k1, d_v0, d_v1, grad_ffn_gain), "dp"
-    )
-    sum_norm_gain, sum_log, sum_bias, sum_cq, s_k0, s_k1, s_v0, s_v1, sum_ffn_gain = small
-    sum_mix_gain = lax.psum(dgain[0], ("dp", "step"))
-    f32 = lambda a: a.astype(F32)
+    here = slice(2 * heads, 3 * heads)
     return (
         output,
-        input_grad,
-        sum_norm_gain,
-        f32(col(0)),
-        f32(col(1)),
-        f32(sum_key)[None],
-        f32(sum_value)[None],
-        f32(sum_beta)[None],
-        f32(tail[:, 4 * heads : 5 * heads]),
-        sum_log,
-        sum_bias,
-        sum_cq,
-        home([s_k0, s_k1])[None],
-        home([s_v0, s_v1])[None],
-        sum_mix_gain,
+        input_grad[None],
+        g_norm[0],
+        g_query,
+        g_outgate,
+        g_key[None],
+        g_value[None],
+        g_scal[None, :, : 2 * heads],
+        g_scal[:, 4 * heads : 5 * heads],
+        tiny[0, DK : 2 * DK][here],
+        tiny[0, 2 * DK :][here],
+        g_cq,
+        g_ck[None],
+        g_cv[None],
+        tiny[0, :DK],
         sum_back[:, :half].T,
-        sum_ffn_gain,
+        g_ffn[0],
         sum_back[:, half : half + ff],
         sum_back[:, half + ff : half + 2 * ff],
         sum_back[:, half + 2 * ff :].T,

time: 651 us -> 417 us (0.64); the launches traced: 643 us -> 416 us
  Pallas kernels: 168 us -> 392 us
  waiting for transfers between devices: 165 us -> 0 us
  blocking collectives: 102 us -> 0 us
  other arithmetic: 75.2 us -> 6.08 us
  matrix products: 62.7 us -> 0 us
  local copies, waits for them, and re-layouts: 47.9 us -> 17.7 us
  between operations: 15.4 us -> 0.76 us
    pallas_call x1 -> x3, Pallas kernels: 50.5 us -> 274 us  [the longest x1 124 us: back_call(): pl.pallas_call(functools.partial(back_kernel, line, heads), out_shape=(sh...]
    reduce_scatter x2 -> x0, waiting for transfers between devices: 111 us -> none  [the longest x1 104 us: per_device(): lax.psum_scatter(jnp.concatenate([grad_out, grad_gate, grad_up, grad_down...]
    psum x2 -> x0, blocking collectives: 102 us -> none  [the longest x1 62.1 us: per_device(): lax.psum((grad_norm_gain, d_log, d_bias, d_cq, d_k0, d_k1, d_v0, d_v1, gr...]
    dot_general x16 -> x0, matrix products: 62.7 us -> none  [the longest x14 61.3 us: product(): lax.dot_general(first, second, (dims, ((), ())), preferred_element_type=F32)]
    psum x3 -> x0, waiting for transfers between devices: 52.5 us -> none  [the longest x1 27.1 us: per_device(): lax.psum(product(gated, back_w[:, :half], NT).astype(BF), 'step')]
    reduce_sum x10 -> x0, other arithmetic: 32.8 us -> none  [the longest x1 9.84 us: short_conv(): summed = summed + shifted * same_doc * kernel[offset]]
    concatenate x4 -> x0, other arithmetic: 10.9 us -> none  [the longest x1 9.17 us: per_device(): jnp.concatenate([grad_out, grad_gate, grad_up, grad_down], axis=1)]
    mul x8 -> x0, local copies, waits for them, and re-layouts: 10.4 us -> none  [the longest x4 5.31 us: unit_rows(): values * lax.rsqrt(jnp.sum(values * values, axis=-1, keepdims=True) + 1e-06)]
  transfers between devices with their start and end apart: 10 -> 0, of which waited for: 5 -> 0; matrix products, arithmetic and copies ran while one was open for 13% -> 0% of each run, Pallas kernels for 0% -> 0%
where the time goes in v3:
time: 417 us; the launch traced here: 416 us
  Pallas kernels  392 us (94%)
  local copies, waits for them, and re-layouts  17.7 us (4%)
  other arithmetic  6.08 us (1%)
    pallas_call x1, Pallas kernels, back_call(): pl.pallas_call(functools.partial(back_kernel, line, heads), out_shape=(sh...  124 us
    pallas_call x1, Pallas kernels, front_call(): pl.pallas_call(functools.partial(front_kernel, line, heads), out_shape=(s...  118 us
    pallas_call x1, Pallas kernels, tail_call(): pl.pallas_call(functools.partial(tail_kernel, line, heads), out_shape=(sh...  88.8 us
    pallas_call x1, Pallas kernels, ffn_call(): pl.pallas_call(functools.partial(ffn_kernel, line), out_shape=(shape((seq...  61.7 us
    unnamed x39, local copies, waits for them, and re-layouts  10.6 us

profile of v3, /device:TPU:0, one launch (start us, length us, event | category | flops | bytes accessed | tf_op | source)
XLA Modules:
  0.0 416.3 jit_solution(3905215088576031254)
XLA Ops:
  0.7 0.8 convert_reduce_fusion
  1.4 0.7 select_reduce_fusion
  2.2 0.6 fusion
  2.8 0.1 pad.14.clone
  2.9 0.1 pad.12.clone
  2.9 1.3 select_maximum_fusion.rates_ref
  4.3 1.2 broadcast_in_dim.46.weight_ref
  5.5 0.8 copy.46
  6.3 0.8 copy.47
  7.1 0.7 maximum_maximum_fusion.scal_ref
  7.7 2.0 pad_maximum_fusion.rest_ref
  9.7 117.7 %front.1 = (bf16[512,512]{1,0:T(8,128)(2,1)}, f32[512,512]{1,0:T(8,128)}, f32[32,128,128]{2,1,0:T(8,128)}, f32[36,128,128]{2,1,0:T(8,128)}, f32[32,128,128]{2,1,...) custom-call(bf16[512,1024]{1,0:T(8,128)(2,1)} %bitcast.34, ...), custom_call_target="tpu_custom_call" | custom-call | tf_op jit(solution)/shard_map/front/pallas_call | solution.py:548
  127.4 61.7 %feed_forward.1 = (f32[512,1024]{1,0:T(8,128)}, f32[512,1024]{1,0:T(8,128)}, f32[512,512]{1,0:T(8,128)}, bf16[512,1024]{1,0:T(8,128)(2,1)}, bf16[4,2,2,64,4736]{4,3,2,1,0:T(8,128)(2,1)}, /*index=5*/f32[1,1024]{1,0:T(1,128)}) custom-call(bf16[512,512]{1,0:T(8,128)(2,1)} %get-tuple-element.67.gated_ref, bf16[512,1024]{1,0:T(8,128)(2,1)} %bitcast.35, ...), custom_call_target="tpu_custom_call" | custom-call | tf_op jit(solution)/shard_map/feed_forward/pallas_call | solution.py:720
  189.1 123.5 %mixer_backward.1 = (bf16[512,3200]{1,0:T(8,128)(2,1)}, f32[5,4,512]{2,1,0:T(4,128)}, f32[2,128]{1,0:T(2,128)}, f32[1,128]{1,0:T(1,128)}, f32[64,4736]{1,0:T(8,128)}, /*index=5*/bf16[512,1024]{1,0:T(8,128)(2,1)}) custom-call(f32[512,512]{1,0:T(8,128)} %get-tuple-element.57.q_ref, bf16[2,512,512]{2,1,0:T(8,128)(2,1)} %get-tuple-element.58.k_ref, ...), custom_call_target="tpu_custom_call" | custom-call | tf_op jit(solution)/shard_map/mixer_backward/pallas_call | solution.py:1089
  312.7 0.0 copy-start
  312.7 88.8 %tail.1 = (bf16[512,1024]{1,0:T(8,128)(2,1)}, f32[64,512]{1,0:T(8,128)}, f32[64,512]{1,0:T(8,128)}, f32[64,1024]{1,0:T(8,128)}, f32[64,1024]{1,0:T(8,128)}, /*in...) custom-call(bf16[512,1024]{1,0:T(8,128)(2,1)} %bitcast.36, ...), custom_call_target="tpu_custom_call" | custom-call | tf_op jit(solution)/shard_map/tail/pallas_call | solution.py:1319
  401.5 0.0 copy-start.1
  401.5 1.2 slice_bitcast_fusion.3
  402.7 1.2 slice_bitcast_fusion.4
  403.9 0.8 slice.38
  404.8 0.7 copy.49
  405.4 0.8 slice_bitcast_fusion.2
  406.2 0.7 copy.48
  406.9 0.0 copy-done
  406.9 0.7 slice_bitcast_fusion.1
  407.5 0.0 copy-start.2
  407.5 1.0 slice_bitcast_fusion
  408.5 0.0 copy-done.1
  408.5 0.0 copy-start.11
  408.5 0.0 copy-start.6
  408.5 0.0 copy-start.5
  408.5 0.0 copy-start.4
  408.5 1.0 copy.61
  409.5 0.0 copy-done.2
  409.5 0.0 copy-start.3
  409.5 0.0 copy-start.9
  409.5 0.0 copy-start.8
  409.5 0.0 copy-start.7
  409.5 0.0 copy-start.10
  409.6 1.0 copy.62
  410.5 0.0 copy-done.11
  410.5 0.6 copy.63
  411.1 0.0 copy-done.6
  411.1 0.7 copy.64
  411.8 0.0 copy-done.5
  411.8 0.7 copy.65
  412.4 0.0 copy-done.4
  412.4 0.7 copy.66
  413.1 0.0 copy-done.3
  413.1 0.7 copy.67
  413.9 0.0 copy-done.9
  413.9 0.6 copy.68
  414.5 0.0 copy-done.8
  414.5 0.6 copy.69
  415.1 0.0 copy-done.7
  415.1 0.6 copy.70
  415.7 0.0 copy-done.10
  415.7 0.6 copy.71
  (2 shorter events, 0.0 us)
Async XLA Ops:
  312.7 94.2 %copy-start = (f32[64,4736]{1,0:T(8,128)S(1)}, f32[64,4736]{1,0:T(8,128)}, u32[]{:S(2)}) copy-start(f32[64,4736]{1,0:T(8,128)} %get-tuple-element.92) | copy-start | bytes 3637252
  401.5 7.0 %copy-start.1 = (bf16[512,1024]{1,0:T(8,128)(2,1)S(1)}, bf16[512,1024]{1,0:T(8,128)(2,1)}, u32[]{:S(2)}) copy-start(bf16[512,1024]{1,0:T(8,128)(2,1)} %get-tuple-element.73) | copy-start | bytes 3145732
  407.5 2.0 copy-start.2
  408.5 2.0 copy-start.11
  408.5 2.6 copy-start.6
  408.5 3.3 copy-start.5
  408.5 3.9 copy-start.4
  409.5 3.6 copy-start.3
  409.5 4.3 %copy-start.9 = (f32[4,512]{1,0:T(4,128)S(1)}, f32[4,512]{1,0:T(4,128)}, u32[]{:S(2)}) copy-start(f32[4,512]{1,0:T(4,128)} %get-tuple-element.170) | copy-start | bytes 24580
  409.5 4.9 %copy-start.8 = (f32[4,1024]{1,0:T(4,128)S(1)}, f32[4,1024]{1,0:T(4,128)}, u32[]{:S(2)}) copy-start(f32[4,1024]{1,0:T(4,128)} %get-tuple-element.90) | copy-start | bytes 49156
  409.5 5.5 %copy-start.7 = (f32[4,1024]{1,0:T(4,128)S(1)}, f32[4,1024]{1,0:T(4,128)}, u32[]{:S(2)}) copy-start(f32[4,1024]{1,0:T(4,128)} %get-tuple-element.91) | copy-start | bytes 49156
  409.5 6.1 %copy-start.10 = (f32[1,1024]{1,0:T(1,128)S(1)}, f32[1,1024]{1,0:T(1,128)}, u32[]{:S(2)}) copy-start(f32[1,1024]{1,0:T(1,128)} %get-tuple-element.93) | copy-start | bytes 12292

commit v4 on v2

v4 whole, which is shorter than its diff:
```python
import functools

import jax
import jax.numpy as jnp
from jax import lax
from jax.experimental import pallas as pl
from jax.experimental.pallas import tpu as pltpu
from jax.sharding import PartitionSpec as P

STRETCH = 64
DK = 128
F32 = jnp.float32
BF = jnp.bfloat16
NN = ((1,), (0,))
NT = ((1,), (1,))
TN = ((0,), (0,))


def split(a):
    if a.dtype == BF:
        return (a,)
    hi = a.astype(BF)
    return (hi, (a - hi.astype(F32)).astype(BF))


def dot1(a, b, dims=NN):
    return lax.dot_general(a.astype(BF), b.astype(BF), (dims, ((), ())), preferred_element_type=F32)


def dot3(a, b, dims=NN):
    a = a if isinstance(a, tuple) else split(a)
    b = b if isinstance(b, tuple) else split(b)
    one = lambda x, y: lax.dot_general(x, y, (dims, ((), ())), preferred_element_type=F32)
    out = one(a[0], b[0])
    if len(a) > 1:
        out = out + one(a[1], b[0])
    if len(b) > 1:
        out = out + one(a[0], b[1])
    return out


def dot6(a, b, dims=NN):
    return lax.dot_general(
        a, b, (dims, ((), ())), precision=lax.Precision.HIGHEST, preferred_element_type=F32
    )


def iota(shape, dim):
    return lax.broadcasted_iota(jnp.int32, shape, dim)


def product(first, second, dims=NN):
    return lax.dot_general(first, second, (dims, ((), ())), preferred_element_type=F32)


def block_masks():
    span = 2 * STRETCH
    row, col = iota((span, span), 0), iota((span, span), 1)
    t_row, t_col = row % STRETCH, col % STRETCH
    p_row, p_col = 2 * t_row + row // STRETCH, 2 * t_col + col // STRETCH
    return t_row, t_col, p_row, p_col


def twice(block):
    return jnp.concatenate([block, block], axis=0)


def block_scalars(aux):
    low = (iota((STRETCH, STRETCH), 0) >= iota((STRETCH, STRETCH), 1)).astype(F32)
    running = dot6(low, aux)
    aux2, run2 = twice(aux), twice(running)
    return aux2, run2, aux2.T, run2.T


def head_terms(aux, aux2, run2, aux_t, run_t, head, heads):
    beta = jnp.concatenate(
        [aux[:, head : head + 1], aux[:, heads + head : heads + head + 1]], axis=0
    )
    lane = 2 * heads + head
    run_col = run2[:, lane : lane + 1]
    run_row = run_t[lane : lane + 1, :]
    doc_lane = 3 * heads
    doc_col = aux2[:, doc_lane : doc_lane + 1]
    doc_row = aux_t[doc_lane : doc_lane + 1, :]
    fresh = aux2[:, doc_lane + 1 : doc_lane + 2]
    span = 2 * STRETCH
    carried = jnp.where(fresh > 0.5, jnp.exp(run_col), 0.0)
    last_run = run_col[span - 1 : span, :]
    to_last = jnp.where(doc_col == doc_col[span - 1 : span, :], jnp.exp(last_run - run_col), 0.0)
    return beta, run_col, run_row, doc_col, doc_row, carried, to_last


def decay_matrix(run_col, run_row, doc_col, doc_row, p_row, p_col):
    inside = (p_row >= p_col) & (doc_col == doc_row)
    return jnp.where(inside, jnp.exp(jnp.where(inside, run_col - run_row, 0.0)), 0.0)


def inverse(mats, masks):
    t_row, t_col, p_row, p_col = masks
    eye = (p_row == p_col).astype(F32)
    pair = (t_row == t_col) & (p_row > p_col)
    out = [eye - jnp.where(pair, a, 0.0) for a in mats]
    level = 1
    while (1 << level) <= STRETCH:
        merge = (
            ((t_row >> level) == (t_col >> level))
            & (((t_row >> (level - 1)) & 1) == 1)
            & (((t_col >> (level - 1)) & 1) == 0)
        )
        low = [x.astype(BF) for x in out]
        half = [dot1(x, jnp.where(merge, a, 0.0)) for x, a in zip(low, mats)]
        out = [o - dot1(h, x) for o, h, x in zip(out, half, low)]
        level += 1
    rest = [eye - x - dot3(a, x) for a, x in zip(mats, out)]
    return [x + dot1(x, r) for x, r in zip(out, rest)]


VMEM = pl.BlockSpec(memory_space=pltpu.VMEM)


MESH = pl.DeviceIdType.MESH


class Place:
    def __init__(self, line):
        self.line = line
        self.dp, self.side = lax.axis_index("dp"), lax.axis_index("step")
        self.z, self.x, self.c = self.dp // 4, (self.dp // 2) % 2, self.dp % 2
        self.sibling = (self.dp + 1 - 2 * self.c, self.side)
        self.across = (self.dp + 2 - 4 * self.x, self.side)
        self.ahead = (
            (lax.rem(self.dp + 4, 4 * line), self.side),
            (lax.rem(self.dp + 4 * line - 4, 4 * line), self.side),
        )
        self.peer = (self.dp, 1 - self.side)
        self.can_send = (self.z + 1 < line, self.z > 0)

    def reaches(self, way, far):
        return self.z - far >= 0 if way == 0 else self.z + far < self.line

    def behind(self, way, far):
        return self.dp - 4 * far if way == 0 else self.dp + 4 * far

    def enter(self, plane=True, peer=True, everyone=False):
        barrier = pltpu.get_barrier_semaphore()

        def greet(device):
            pl.semaphore_signal(barrier, inc=1, device_id=device, device_id_type=MESH)

        count = 0
        if peer:
            greet(self.peer)
            count = 1
        if plane:
            greet(self.sibling)
            greet(self.across)
            count = count + 2
        if everyone:
            for z in range(self.line):
                device = (z * 4 + self.x * 2 + self.c, self.side)
                pl.when(z != self.z)(functools.partial(greet, device))
            count = count + self.line - 1
        elif plane:
            for way in (0, 1):
                pl.when(self.can_send[way])(functools.partial(greet, self.ahead[way]))
            count = count + self.can_send[0].astype(jnp.int32) + self.can_send[1].astype(jnp.int32)
        pl.semaphore_wait(barrier, count)


def remote(src, dst, send_sem, recv_sem, device):
    return pltpu.make_async_remote_copy(
        src_ref=src, dst_ref=dst, send_sem=send_sem, recv_sem=recv_sem,
        device_id=device, device_id_type=MESH,
    )


def gather_sems(line, parts):
    dma = pltpu.SemaphoreType.DMA
    return [
        dma((2, line, parts)), dma((2, line, parts)),
        dma((2, line, parts)), dma((2, line, parts)),
        dma((2, 2, line, parts)), dma((2, 2, line, parts)),
    ]


class Gather:
    def __init__(self, place, buf, cuts, sems):
        self.place, self.buf, self.cuts = place, buf, cuts
        self.zs, self.zr, self.xs, self.xr, self.cs, self.cr = sems

    def block(self, index, part):
        start, width = self.cuts[part]
        return self.buf.at[index, :, pl.ds(start, width)]

    def line_copy(self, index, way, far, part):
        ref = self.block(index, part)
        return remote(ref, ref, self.zs.at[way, far, part], self.zr.at[way, far, part], self.place.ahead[way])

    def across_copy(self, index, way, far, part):
        ref = self.block(index, part)
        return remote(ref, ref, self.xs.at[way, far, part], self.xr.at[way, far, part], self.place.across)

    def sibling_copy(self, index, column, way, far, part):
        ref = self.block(index, part)
        return remote(
            ref, ref, self.cs.at[column, way, far, part], self.cr.at[column, way, far, part], self.place.sibling
        )

    def spread(self, index, way, far, part):
        place = self.place
        for to in (0, 1) if far == 0 else (way,):
            pl.when(place.can_send[to])(lambda to=to: self.line_copy(index, to, far + 1, part).start())
        self.across_copy(index, way, far, part).start()
        self.sibling_copy(index, 0, way, far, part).start()

    def ways(self, far):
        return (0,) if far == 0 else (0, 1)

    def each(self, far, act):
        if far == 0:
            act(0)
            return
        for way in (0, 1):
            pl.when(self.place.reaches(way, far))(functools.partial(act, way))

    def step(self, far, part):
        place = self.place
        if far == 0:
            self.spread(place.dp, 0, 0, part)
            return

        def from_line(way):
            index = place.behind(way, far)
            self.line_copy(index, way, far, part).wait_recv()
            self.spread(index, way, far, part)

        def from_across(way):
            index = place.behind(way, far - 1) + 2 - 4 * place.x
            self.across_copy(index, way, far - 1, part).wait_recv()
            self.sibling_copy(index, 1, way, far - 1, part).start()

        if far < place.line:
            self.each(far, from_line)
        self.each(far - 1, from_across)

    def steps(self):
        return [
            functools.partial(self.step, far, part)
            for far in range(self.place.line + 1)
            for part in range(len(self.cuts))
        ]

    def ready(self, part):
        place = self.place
        for far in range(place.line):
            for column in (0, 1):

                def from_sibling(way):
                    index = place.behind(way, far) + 1 - 2 * place.c + column * (2 - 4 * place.x)
                    self.sibling_copy(index, column, way, far, part).wait_recv()

                self.each(far, from_sibling)

    def drain(self, part):
        place = self.place
        for far in range(place.line):

            def sent(way):
                index = place.behind(way, far)
                for to in (0, 1) if far == 0 else (way,):
                    pl.when(place.can_send[to])(
                        lambda to=to: self.line_copy(index, to, far + 1, part).wait_send()
                    )
                self.across_copy(index, way, far, part).wait_send()
                self.sibling_copy(index, 0, way, far, part).wait_send()
                self.sibling_copy(index + 2 - 4 * place.x, 1, way, far, part).wait_send()

            self.each(far, sent)


def run_slot(slots, turn):
    for index, steps in enumerate(slots):
        if steps:

            def go(steps=steps):
                for step in steps:
                    step()

            pl.when(turn == index)(go)


def deal(steps, turns):
    return [steps[len(steps) * i // turns : len(steps) * (i + 1) // turns] for i in range(turns)]


def scatter_sems(line, parts):
    dma = pltpu.SemaphoreType.DMA
    return [dma((2, parts))] * 4 + [dma((parts,))] * 2 + [dma((2, line, parts))] * 2


def scatter_scratch(line, depth, width, own):
    slots = [pltpu.VMEM((2, line, depth, width), BF), pltpu.VMEM((line, depth, width), BF),
             pltpu.VMEM((2, line, depth, width), BF)]
    return slots + ([pltpu.VMEM((2, line, depth, width), BF)] if own else [])


class Scatter:
    def __init__(self, place, grad, out, cuts, slots, sems, own=None):
        self.place, self.grad, self.out, self.cuts, self.own = place, grad, out, cuts, own
        self.mid, self.far, self.path = slots
        self.cs, self.cr, self.ls, self.lr, self.xs, self.xr, self.zs, self.zr = sems

    def cols(self, part):
        start, width = self.cuts[part]
        return pl.ds(start, width)

    def column(self, which):
        return 1 - self.place.x if which == 0 else self.place.x

    def sibling_copy(self, part, which):
        place, cols, x = self.place, self.cols(part), self.column(which)
        return remote(
            self.grad.at[:, x, 1 - place.c, :, cols], self.mid.at[which, :, :, cols],
            self.cs.at[which, part], self.cr.at[which, part], place.sibling,
        )

    def own_copy(self, part, which):
        cols, x = self.cols(part), self.column(which)
        return pltpu.make_async_copy(
            self.grad.at[:, x, self.place.c, :, cols], self.own.at[which, :, :, cols], self.ls.at[which, part]
        )

    def across_copy(self, part):
        cols = self.cols(part)
        return remote(
            self.mid.at[0, :, :, cols], self.far.at[:, :, cols], self.xs.at[part], self.xr.at[part], self.place.across
        )

    def line_copy(self, part, way, target):
        cols = self.cols(part)
        ref = self.path.at[way, target, :, cols]
        return remote(
            self.mid.at[1, target, :, cols], ref,
            self.zs.at[way, target, part], self.zr.at[way, target, part], self.place.ahead[way],
        )

    def pass_copy(self, part, way, target):
        cols = self.cols(part)
        ref = self.path.at[way, target, :, cols]
        return remote(
            ref, ref, self.zs.at[way, target, part], self.zr.at[way, target, part], self.place.ahead[way]
        )

    def begin(self, part):
        for which in (0, 1):
            if self.own is not None:
                self.own_copy(part, which).start()
            self.sibling_copy(part, which).start()

    def merge(self, part, which):
        self.sibling_copy(part, which).wait_recv()
        if self.own is not None:
            self.own_copy(part, which).wait()
        cols = self.cols(part)
        for target in range(self.place.line):
            if self.own is not None:
                mine = self.own[which, target, :, cols]
            else:
                mine = self.grad[target, self.column(which), self.place.c, :, cols]
            both = self.mid[which, target, :, cols].astype(F32) + mine.astype(F32)
            self.mid[which, target, :, cols] = both.astype(BF)
        if which == 0:
            self.across_copy(part).start()

    def join(self, part):
        self.across_copy(part).wait_recv()
        cols = self.cols(part)
        for target in range(self.place.line):
            both = self.mid[1, target, :, cols].astype(F32) + self.far[target, :, cols].astype(F32)
            self.mid[1, target, :, cols] = both.astype(BF)

    def wave(self, part, turn):
        place, cols = self.place, self.cols(part)
        for way in (0, 1):
            hops = place.z if way == 0 else place.line - 1 - place.z
            target = place.line - 1 - turn + hops if way == 0 else turn - hops

            def start(way=way, target=target):
                self.line_copy(part, way, target).start()

            def go_on(way=way, target=target):
                self.pass_copy(part, way, target).wait_recv()
                both = self.path[way, target, :, cols].astype(F32) + self.mid[1, target, :, cols].astype(F32)
                self.path[way, target, :, cols] = both.astype(BF)
                self.pass_copy(part, way, target).start()

            pl.when(hops == 0)(start)
            pl.when((hops > 0) & (hops <= turn))(go_on)

    def end(self, part):
        place, cols = self.place, self.cols(part)
        start, width = self.cuts[part]
        z = place.z
        self.out[:, cols] = self.mid[1, z, :, cols].astype(F32)

        def take(way):
            self.pass_copy(part, way, z).wait_recv()
            self.out[:, cols] += self.path[way, z, :, cols].astype(F32)

        pl.when(z > 0)(functools.partial(take, 0))
        pl.when(z < place.line - 1)(functools.partial(take, 1))

    def drain_sibling(self, part):
        for which in (0, 1):
            self.sibling_copy(part, which).wait_send()

    def drain(self, part):
        place = self.place
        self.across_copy(part).wait_send()
        for target in range(place.line):
            for way in (0, 1):
                ahead = target > place.z if way == 0 else target < place.z
                pl.when(ahead)(lambda way=way, target=target: self.pass_copy(part, way, target).wait_send())

    def stages(self, part):
        waves = [functools.partial(self.wave, part, turn) for turn in range(self.place.line - 1)]
        return [functools.partial(self.join, part)] + waves + [functools.partial(self.end, part)]


KW = 4
PAD = 8


def conv_window(window, kernel, same):
    rows = window.shape[0] - PAD
    out = window[PAD:] * kernel[0:1]
    for offset in range(1, KW):
        out = out + jnp.where(same[offset - 1], window[PAD - offset : PAD - offset + rows], 0.0) * kernel[offset : offset + 1]
    return out


def same_documents(window):
    rows = window.shape[0] - PAD
    return [window[PAD:] == window[PAD - offset : PAD - offset + rows] for offset in range(1, KW)]


def rows_of(ref, block, count, extra=0):
    return ref[pl.ds(pl.multiple_of(block * STRETCH, STRETCH), count + extra), :]


def scalar_select(side, heads):
    src, dst = iota((DK, DK), 0), iota((DK, DK), 1)
    kind, head = dst // heads, dst % heads
    first = jnp.where(kind == side, 0, 2 * heads)
    source = jnp.where(kind < 2, first + side * heads + head, 4 * heads + head)
    return ((src == source) & (kind < 3)).astype(F32)


def softplus(values):
    return jnp.maximum(values, 0.0) + jnp.log1p(jnp.exp(-jnp.abs(values)))


def front_kernel(
    line, heads, x_ref, docs_ref, norm_ref, wq_ref, wg_ref, wk_ref, wv_ref, beta_ref, alpha_ref, wo_ref, gate_ref,
    up_ref, down_ref, log_ref, bias_ref, cq_ref, ck_ref, cv_ref, mix_ref,
    gated_ref, middle_ref, conv_ref, rates_ref,
    mixed_out, inv_out, state_out, pseudo_out, pre_out, q_out, k_out, v_out, aux_out, front_out, rest_out,
    mixed_ref, inv_ref, state_ref, pseudo_ref, pre_ref, q_ref, k_ref, v_ref, aux_ref,
    front, rest, wo, normed, doc_cols, attn, scal, scal_in, attn_own, attn_in,
    local_sem, y_send, y_recv, a_send, a_recv, *sems,
):
    place = Place(line)
    side = place.side
    seq = x_ref.shape[0]
    depth, half = wq_ref.shape
    span = 2 * STRETCH
    blocks = seq // STRETCH
    scal_at = 6 * half
    me = place.dp
    place.enter()

    own_cols = pl.ds(pl.multiple_of(side * half, half), half)
    other_cols = pl.ds(pl.multiple_of((1 - side) * half, half), half)

    def at(first):
        return pl.ds(pl.multiple_of((first + side) * half, half), half)

    swaps = [
        remote(wk_ref.at[:, other_cols], front.at[me, :, at(2)], y_send.at[0], y_recv.at[0], place.peer),
        remote(wv_ref.at[:, other_cols], front.at[me, :, at(4)], y_send.at[1], y_recv.at[1], place.peer),
        remote(scal, scal_in, y_send.at[2], y_recv.at[2], place.peer),
        remote(ck_ref.at[:, other_cols], conv_ref.at[1 + side], y_send.at[3], y_recv.at[3], place.peer),
        remote(cv_ref.at[:, other_cols], conv_ref.at[3 + side], y_send.at[4], y_recv.at[4], place.peer),
    ]
    scal[...] = jnp.zeros_like(scal)
    corner = (iota((depth, depth), 0) == iota((depth, depth), 1)).astype(BF)
    scal[:, 0 : 2 * heads] = product(corner, beta_ref[...], NT).astype(BF)
    scal[:, 4 * heads : 5 * heads] = product(corner, alpha_ref[...], NT).astype(BF)
    for swap in swaps:
        swap.start()
    ff = gate_ref.shape[1]
    rest[:, 0:half] = wo_ref[...]
    rest[:, half : half + ff] = gate_ref[...]
    rest[:, half + ff : half + 2 * ff] = up_ref[...]
    rest[:, half + 2 * ff : half + 3 * ff] = down_ref[...]
    own_rest = pltpu.make_async_copy(rest, rest_out.at[me], local_sem.at[0])
    own_rest.start()
    rates_ref[...] = jnp.zeros_like(rates_ref)
    rates_ref[0:1, 2 * heads : 3 * heads] = log_ref[...]
    rates_ref[1:2, 2 * heads : 3 * heads] = bias_ref[...]
    front[me, :, 0:half] = wq_ref[...]
    front[me, :, half : 2 * half] = wg_ref[...]
    front[me, :, at(2)] = wk_ref[:, own_cols]
    front[me, :, at(4)] = wv_ref[:, own_cols]
    conv_ref[0] = cq_ref[...]
    conv_ref[1 + side] = ck_ref[:, own_cols]
    conv_ref[3 + side] = cv_ref[:, own_cols]

    head_cuts = [(0, 2 * half), (2 * half, 2 * half), (4 * half, 2 * half + DK)]
    first = Gather(place, front, head_cuts, sems[:6])
    rest_cuts = [(0, half)] + [(half + i * ff, ff) for i in range(3)]
    second = Gather(place, rest_out, rest_cuts, sems[6:])

    first.step(0, 0)
    for swap in swaps:
        swap.wait_recv()
    lanes = iota((depth, DK), 1)
    theirs = pltpu.roll(scal_in[...].astype(F32), 2 * heads, 1)
    ours = scal[...].astype(F32)
    swapped = (lanes >= 2 * heads) & (lanes < 4 * heads)
    front[me, :, scal_at : scal_at + DK] = jnp.where(swapped, theirs, ours).astype(BF)
    for part in (1, 2):
        first.step(0, part)

    def normalise(block, carry):
        rows = pl.ds(pl.multiple_of(block * STRETCH, STRETCH), STRETCH)
        x = x_ref[rows, :].astype(F32)
        scale = lax.rsqrt(jnp.mean(x * x, axis=-1, keepdims=True) + 1e-06)
        normed[rows, :] = (x * scale * norm_ref[...]).astype(BF)
        return carry

    lax.fori_loop(0, blocks, normalise, 0)
    doc_cols[0:PAD, :] = jnp.full((PAD, DK), -1.0, F32)
    for i in range(seq // DK):
        lane_docs = docs_ref[:, i * DK : (i + 1) * DK].astype(F32)
        doc_cols[PAD + i * DK : PAD + (i + 1) * DK, :] = jnp.broadcast_to(lane_docs, (DK, DK)).T
    pre_ref[0:PAD, :] = jnp.zeros((PAD, pre_ref.shape[1]), F32)

    steps = first.steps()[3:]
    for step in steps:
        step()
    own_rest.wait()
    for part in range(4):
        second.step(0, part)
    tile = 2 * DK
    for part, (start, width) in enumerate(head_cuts):
        first.ready(part)

        def project(index, carry, start=start):
            cols = pl.ds(pl.multiple_of(start + index * tile, DK), tile)
            weights = front[:, :, cols].reshape(-1, tile)
            pre_ref[PAD:, cols] = jnp.dot(normed[...], weights, preferred_element_type=F32)
            return carry

        lax.fori_loop(0, 2 * half // tile, project, 0)
    scal_cols = slice(scal_at, scal_at + DK)
    pre_ref[PAD:, scal_cols] = jnp.dot(
        normed[...], front[:, :, scal_cols].reshape(-1, DK), preferred_element_type=F32
    )
    keep_front = pltpu.make_async_copy(front, front_out, local_sem.at[1])
    keep_front.start()

    def keep(index, src, dst):
        return pltpu.make_async_copy(src, dst, local_sem.at[index])

    keep_pre = keep(2, pre_ref, pre_out)
    keep_pre.start()
    early = [keep(3, inv_ref, inv_out), keep(4, q_ref, q_out), keep(5, k_ref, k_out), keep(6, v_ref, v_out)]
    early.append(keep(7, aux_ref, aux_out))
    late = [keep(8, mixed_ref, mixed_out), keep(9, state_ref, state_out), keep(10, pseudo_ref, pseudo_out)]
    keep_wo = keep(11, rest_out.at[:, :, pl.ds(0, half)], wo)

    select = scalar_select(side, heads)
    rate = -jnp.exp(rates_ref[0:1, :])
    masks = block_masks()
    t_row, t_col, p_row, p_col = masks
    together = 2
    turns = blocks // together
    slots = deal(second.steps()[4:], turns + blocks // 2) + [[]] * (blocks - blocks // 2)

    def keys_of(rows, cols):
        return jnp.concatenate([k_ref[0, rows, cols], k_ref[1, rows, cols]], axis=0)

    def prepare_block(block):
        rows = pl.ds(pl.multiple_of(block * STRETCH, STRETCH), STRETCH)
        doc_window = rows_of(doc_cols, block, STRETCH, PAD)
        same = same_documents(doc_window)
        raw = dot6(pre_ref[pl.ds(pl.multiple_of(block * STRETCH, STRETCH) + PAD, STRETCH), scal_cols], select)
        lane = iota((STRETCH, DK), 1)
        beta = (2.0 * jax.nn.sigmoid(raw)).astype(BF).astype(F32)
        decay = rate * softplus(raw + rates_ref[1:2, :])
        docs = doc_window[PAD:]
        fresh = (docs == doc_window[PAD - 1 : PAD]).astype(F32)
        aux = jnp.where(lane < 2 * heads, beta, jnp.where(lane < 3 * heads, decay, 0.0))
        aux = jnp.where(lane == 3 * heads, docs, jnp.where(lane == 3 * heads + 1, fresh, aux))
        aux_ref[rows, :] = aux
        for head in range(heads):
            cols = slice(head * DK, (head + 1) * DK)
            for kind in (1, 2, 0, 3, 4):
                first_col = (0, 2, 3, 4, 5)[kind] * half + head * DK
                window = pre_ref[
                    pl.ds(pl.multiple_of(block * STRETCH, STRETCH), STRETCH + PAD), first_col : first_col + DK
                ]
                value = conv_window(window, conv_ref[kind, :, cols], same)
                value = value * jax.nn.sigmoid(value)
                if kind < 3:
                    value = value * lax.rsqrt(jnp.sum(value * value, axis=-1, keepdims=True) + 1e-06)
                if kind == 0:
                    q_ref[rows, cols] = value * DK ** (-0.5)
                elif kind < 3:
                    k_ref[kind - 1, rows, cols] = value.astype(BF)
                else:
                    v_ref[kind - 3, rows, cols] = value.astype(BF)
        aux2, run2, aux_t, run_t = block_scalars(aux)
        mats = []
        for head in range(heads):
            cols = slice(head * DK, (head + 1) * DK)
            beta, run_col, run_row, doc_col, doc_row, carried, to_last = head_terms(
                aux, aux2, run2, aux_t, run_t, head, heads
            )
            decay = decay_matrix(run_col, run_row, doc_col, doc_row, p_row, p_col)
            keys = keys_of(rows, cols)
            gram = dot1(keys, keys, NT)
            mats.append(beta * jnp.where(p_row > p_col, decay * gram, 0.0))
            attn[block * heads + head] = decay[STRETCH:] * dot3(q_ref[rows, cols], keys, NT)
        return mats

    def prepare(turn, carry):
        mats = []
        for i in range(together):
            mats += prepare_block(turn * together + i)
        for i, inv in enumerate(inverse(mats, masks)):
            inv_ref[turn * together * heads + i] = inv
        run_slot(slots[:turns], turn)
        return carry

    lax.fori_loop(0, blocks // together, prepare, 0)
    for copy in early:
        copy.start()
    for head in range(heads):
        state_ref[head] = jnp.zeros((DK, DK), F32)

    def attn_copy(index):
        rows = chunk_rows(index)
        return remote(attn_own.at[rows], attn_in.at[rows], a_send.at[index], a_recv.at[index], place.peer)


    def advance(block, carry):
        rows = pl.ds(pl.multiple_of(block * STRETCH, STRETCH), STRETCH)
        aux = aux_ref[rows, :]
        aux2, run2, aux_t, run_t = block_scalars(aux)
        for head in range(heads):
            cols = slice(head * DK, (head + 1) * DK)
            beta, run_col, run_row, doc_col, doc_row, carried, to_last = head_terms(
                aux, aux2, run2, aux_t, run_t, head, heads
            )
            keys = keys_of(rows, cols)
            values = jnp.concatenate([v_ref[0, rows, cols], v_ref[1, rows, cols]], axis=0).astype(F32)
            state = state_ref[block * heads + head]
            state_parts = split(state)
            target = beta * (values - carried * dot3(keys, state_parts))
            pseudo = dot3(inv_ref[block * heads + head], target)
            pseudo_ref[block * heads + head] = pseudo
            mixed = carried[STRETCH:] * dot3(q_ref[rows, cols], state_parts) + dot3(
                attn[block * heads + head], pseudo
            )
            state_ref[(block + 1) * heads + head] = carried[span - 1 : span] * state + dot3(
                keys, to_last * pseudo, TN
            )
            mixed_ref[rows, cols] = mixed
            scale = lax.rsqrt(jnp.mean(mixed * mixed, axis=-1, keepdims=True) + 1e-05)
            gate = pre_ref[
                pl.ds(pl.multiple_of(block * STRETCH, STRETCH) + PAD, STRETCH),
                half + head * DK : half + (head + 1) * DK,
            ]
            gated_ref[rows, cols] = (mixed * scale * mix_ref[...] * (gate * jax.nn.sigmoid(gate))).astype(BF)
        run_slot(slots[turns:], block)
        per_pair = 2 * CHUNK // STRETCH

        def hand_over():
            pair = block // per_pair

            def complete():
                second.ready(0)
                keep_wo.start()
                keep_wo.wait()

            pl.when(pair == 0)(complete)
            rows = pair_rows(pair)
            attn_own[rows, :] = product(gated_ref[rows, :], wo[...].reshape(-1, half), NT).astype(BF)
            attn_copy(2 * pair).start()
            attn_copy(2 * pair + 1).start()

        pl.when(lax.rem(block, per_pair) == per_pair - 1)(hand_over)
        return carry

    lax.fori_loop(0, blocks, advance, 0)
    for copy in late:
        copy.start()

    def middle(index, carry):
        rows = chunk_rows(index)
        attn_copy(index).wait_recv()
        both = attn_own[rows, :].astype(F32) + attn_in[rows, :].astype(F32)
        middle_ref[rows, :] = x_ref[rows, :].astype(F32) + both
        return carry

    lax.fori_loop(0, seq // CHUNK, middle, 0)
    for part in (1, 2, 3):
        second.ready(part)

    def handed(index, carry):
        attn_copy(index).wait_send()
        return carry

    lax.fori_loop(0, seq // CHUNK, handed, 0)
    for swap in swaps:
        swap.wait_send()
    for part in range(3):
        first.drain(part)
    for part in range(4):
        second.drain(part)
    for copy in [keep_front, keep_pre] + early + late:
        copy.wait()


def front_call(line, x, docs, norm, wq, wg, wk, wv, beta, alpha, wo, gate, up, down, log, bias, cq, ck, cv, mix):
    seq, half = x.shape[0], wq.shape[1]
    depth, ff = gate.shape
    tail = half + 3 * ff
    heads, blocks = half // DK, seq // STRETCH
    units, span = heads * blocks, 2 * STRETCH
    width = 6 * half + DK
    shape = jax.ShapeDtypeStruct
    anywhere = pl.BlockSpec(memory_space=pl.ANY)
    dma = pltpu.SemaphoreType.DMA
    kept = (
        shape((seq, half), F32),
        shape((units, span, span), F32),
        shape((units + heads, DK, DK), F32),
        shape((units, span, DK), F32),
        shape((seq + PAD, width), F32),
        shape((seq, half), F32),
        shape((2, seq, half), BF),
        shape((2, seq, half), BF),
        shape((seq, DK), F32),
    )
    low = pltpu.VMEM(x.shape, BF)
    chunks = seq // CHUNK
    return pl.pallas_call(
        functools.partial(front_kernel, line, heads),
        out_shape=(
            shape((seq, half), BF),
            shape(x.shape, F32),
            shape((5, KW, half), F32),
            shape((2, DK), F32),
        )
        + kept
        + (
            shape((4 * line, depth, width), BF),
            shape((4 * line, depth, tail), BF),
        ),
        in_specs=[VMEM] * 19,
        out_specs=(VMEM,) * 4 + (anywhere,) * 11,
        scratch_shapes=[pltpu.VMEM(array.shape, array.dtype) for array in kept]
        + [
            pltpu.VMEM((4 * line, depth, width), BF),
            pltpu.VMEM((depth, tail), BF),
            pltpu.VMEM((4 * line, depth, half), BF),
            low,
            pltpu.VMEM((seq + PAD, DK), F32),
            pltpu.VMEM((units, STRETCH, span), F32),
            pltpu.VMEM((depth, DK), BF),
            pltpu.VMEM((depth, DK), BF),
            low,
            low,
            dma((12,)),
            dma((5,)),
            dma((5,)),
            dma((chunks,)),
            dma((chunks,)),
        ]
        + gather_sems(line, 3)
        + gather_sems(line, 4),
        compiler_params=pltpu.CompilerParams(
            collective_id=0, has_side_effects=True, vmem_limit_bytes=60 << 20
        ),
        name="front",
    )(x, docs, norm, wq, wg, wk, wv, beta, alpha, wo, gate, up, down, log, bias, cq, ck, cv, mix)


CHUNK = 128


def chunk_rows(index):
    return pl.ds(pl.multiple_of(index * CHUNK, CHUNK), CHUNK)


def pair_rows(index):
    return pl.ds(pl.multiple_of(index * 2 * CHUNK, 2 * CHUNK), 2 * CHUNK)


def flat(ref, start, width):
    return ref[:, :, :, :, start : start + width].reshape(-1, width)


def put_blocks(ref, index, cols, value):
    depth = ref.shape[3]
    count = DK // depth
    value = value.astype(BF)
    if count == 2:
        ref[index // 2, index % 2, :, :, cols] = value.reshape(2, depth, value.shape[-1])
    else:
        ref[pl.ds(index * (count // 4), count // 4), :, :, :, cols] = value.reshape(
            count // 4, 2, 2, depth, value.shape[-1]
        )


def rest_kernel(
    line, heads, gated_ref, x_ref, cot_ref, middle_ref, domains_ref, gain_ref, norm_ref, docs_ref, conv_ref, rates_ref, mix_ref,
    w_hbm, fw_hbm, pre_hbm, q_hbm, k_hbm, v_hbm, aux_hbm, mixed_hbm, inv_hbm, state_hbm, pseudo_hbm,
    out_ref, igrad_ref, sum_ref, gq_ref, gg_ref, gk_ref, gv_ref, gs_ref, gcq_ref, gck_ref, gcv_ref, gnorm_ref,
    gffn_ref, gtiny_ref,
    w_ref, fw_ref, attn_own, attn_in, in_own, in_in, normed, seed_low, work, back_ref, dgated_ref,
    dstate, doc_cols, dy_next, dconv_ref, dscal_ref, dgain_ref, total, mid, far, path,
    pre_s, q_s, k_s, v_s, aux_s, mixed_s, inv_s, state_s, pseudo_s,
    small, small_in, small_line, small_sum, mix_in, scal_in,
    load_sem, stream_sem, f_send, f_recv, o_send, o_recv, n_send, n_recv, h_send, h_recv,
    m_send, m_recv, l_send, l_recv, free_sem, *sems,
):
    place = Place(line)
    side, me = place.side, place.dp
    seq, width = x_ref.shape
    half = gated_ref.shape[1]
    tail = sum_ref.shape[-1]
    ff = (tail - half) // 3
    chunks = seq // CHUNK
    blocks = seq // STRETCH
    span = 2 * STRETCH
    gate_up = (half, 2 * ff)
    down = (half + 2 * ff, ff)
    scal_at = 6 * half
    front_width = scal_at + DK

    def load(index, start, count):
        cols = pl.ds(start, count)
        return pltpu.make_async_copy(w_hbm.at[:, :, :, :, cols], w_ref.at[:, :, :, :, cols], load_sem.at[index])

    loads = [load(0, 0, half), load(1, *gate_up), load(2, *down)]
    load_front = pltpu.make_async_copy(fw_hbm, fw_ref, load_sem.at[3])
    for copy in loads:
        copy.start()
    place.enter(everyone=True)

    def streams(block, slot):
        units = pl.ds(block * heads, heads)
        rows = pl.ds(pl.multiple_of(block * STRETCH, STRETCH), STRETCH)
        pairs = [
            (pre_hbm.at[pl.ds(pl.multiple_of(block * STRETCH, STRETCH), STRETCH + PAD)], pre_s),
            (q_hbm.at[rows], q_s),
            (k_hbm.at[:, rows], k_s),
            (v_hbm.at[:, rows], v_s),
            (aux_hbm.at[rows], aux_s),
            (mixed_hbm.at[rows], mixed_s),
            (inv_hbm.at[units], inv_s),
            (state_hbm.at[units], state_s),
            (pseudo_hbm.at[units], pseudo_s),
        ]
        return [
            pltpu.make_async_copy(src, dst.at[slot], stream_sem.at[slot, i]) for i, (src, dst) in enumerate(pairs)
        ]

    domains = domains_ref[...]
    rows_all = domains.shape[1]
    places = iota(domains.shape, 1)
    mine = jnp.sum(jnp.where(places == me, domains, 0), axis=1, keepdims=True)
    count = jnp.sum((domains == mine).astype(F32), axis=1, keepdims=True)
    row_weight = 2.0 / (1.0 + count * (GROUPS / rows_all))

    def in_copy(index):
        rows = chunk_rows(index)
        return remote(in_own.at[rows], in_in.at[rows], f_send.at[index], f_recv.at[index], place.peer)

    gffn_ref[...] = jnp.zeros_like(gffn_ref)
    for copy in loads:
        copy.wait()

    def feed(index, carry):
        rows = chunk_rows(index)
        middle = middle_ref[rows, :]
        scale = lax.rsqrt(jnp.mean(middle * middle, axis=-1, keepdims=True) + 1e-06)
        low = (middle * scale * gain_ref[...]).astype(BF)
        normed[rows, :] = low
        both = product(low, flat(w_ref, *gate_up))
        gate_in, up_in = both[:, :ff], both[:, ff:]
        sigmoid = jax.nn.sigmoid(gate_in)
        silu = gate_in * sigmoid
        seed = (cot_ref[rows, :].astype(F32) * row_weight).astype(BF)
        seed_low[rows, :] = seed
        hidden_back = product(seed, flat(w_ref, *down))
        gate_back = (hidden_back * up_in * (sigmoid * (1.0 + gate_in * (1.0 - sigmoid)))).astype(BF)
        up_back = (hidden_back * silu).astype(BF)
        work[rows, 0:ff] = gate_back
        work[rows, ff : 2 * ff] = up_back
        low_hidden = (silu * up_in).astype(BF)
        work[rows, 2 * ff : 3 * ff] = low_hidden
        return carry

    def feed_pair(index, carry):
        lax.fori_loop(2 * index, 2 * index + 2, feed, 0)
        rows = pair_rows(index)
        in_own[rows, :] = product(work[rows, 0 : 2 * ff], flat(w_ref, *gate_up), NT).astype(BF)
        in_copy(2 * index).start()
        in_copy(2 * index + 1).start()
        attn_own[rows, :] = product(work[rows, 2 * ff : 3 * ff], flat(w_ref, *down), NT).astype(BF)
        return carry

    lax.fori_loop(0, chunks // 2, feed_pair, 0)

    def weigh(index, carry):
        cols = pl.ds(pl.multiple_of(index * DK, DK), DK)
        put_blocks(w_ref, index, slice(half + 2 * ff, half + 3 * ff), product(seed_low[:, cols], work[:, 2 * ff : 3 * ff], TN))
        put_blocks(w_ref, index, slice(half, half + 2 * ff), product(normed[:, cols], work[:, 0 : 2 * ff], TN))
        return carry

    lax.fori_loop(0, width // DK, weigh, 0)
    cuts = [(half, ff), (half + ff, ff), (half + 2 * ff, ff), (0, half)]
    scatter = Scatter(place, w_ref, sum_ref, cuts, (mid, far, path), sems[:8])
    parts = range(len(cuts))
    for part in parts[:-1]:
        scatter.begin(part)
    scatter.merge(0, 0)
    scatter.merge(0, 1)
    merges = [functools.partial(scatter.merge, part, which) for part in (1, 2) for which in (0, 1)]
    merge_slots = deal(merges, chunks - 1)


    def finish(index, carry):
        rows = chunk_rows(index)
        in_copy(index).wait_recv()
        grad = in_own[rows, :].astype(F32) + in_in[rows, :].astype(F32)
        middle = middle_ref[rows, :]
        scale = lax.rsqrt(jnp.mean(middle * middle, axis=-1, keepdims=True) + 1e-06)
        unit = middle * scale
        gffn_ref[...] += jnp.sum(grad * unit, axis=0, keepdims=True)
        grad = grad * gain_ref[...]
        seed = cot_ref[rows, :].astype(F32) * row_weight
        total = seed + scale * (grad - unit * jnp.mean(unit * grad, axis=-1, keepdims=True))
        back_ref[rows, :] = total
        low = total.astype(BF)
        seed_low[rows, :] = low
        dgated_ref[rows, :] = product(low, flat(w_ref, 0, half))
        run_slot(merge_slots, index)
        return carry

    lax.fori_loop(0, chunks, finish, 0)

    def weigh_out(index, carry):
        cols = pl.ds(pl.multiple_of(index * DK, DK), DK)
        put_blocks(w_ref, index, slice(0, half), product(seed_low[:, cols], gated_ref[...], TN))
        return carry

    lax.fori_loop(0, width // DK, weigh_out, 0)
    scatter.begin(parts[-1])
    swap = remote(attn_own, attn_in, o_send, o_recv, place.peer)
    swap.start()
    for copy in streams(blocks - 1, (blocks - 1) % 2):
        copy.start()
    load_front.start()

    masks = block_masks()
    t_row, t_col, p_row, p_col = masks
    strict = p_row > p_col
    for head in range(heads):
        dstate[head] = jnp.zeros((DK, DK), F32)
    dgain_ref[...] = jnp.zeros_like(dgain_ref)
    dconv_ref[...] = jnp.zeros_like(dconv_ref)
    dscal_ref[...] = jnp.zeros_like(dscal_ref)
    dy_next[...] = jnp.zeros_like(dy_next)
    doc_cols[0:PAD, :] = jnp.full((PAD, DK), -1.0, F32)
    doc_cols[PAD + seq :, :] = jnp.full((PAD, DK), -1.0, F32)
    for i in range(seq // DK):
        lane_docs = docs_ref[:, i * DK : (i + 1) * DK].astype(F32)
        doc_cols[PAD + i * DK : PAD + (i + 1) * DK, :] = jnp.broadcast_to(lane_docs, (DK, DK)).T
    upper = (iota((STRETCH, STRETCH), 0) <= iota((STRETCH, STRETCH), 1)).astype(F32)
    lanes = iota((STRETCH, DK), 1)
    wide_rows = iota((span, DK), 0)
    select = scalar_select(side, heads)
    rate = -jnp.exp(rates_ref[0:1, :])
    scal_at = 6 * half
    scal_cols = slice(scal_at, scal_at + DK)

    chains = [scatter.stages(part) for part in parts]
    slots = [[] for _ in range(blocks)]
    left = []
    slots[0] += [functools.partial(scatter.merge, parts[-1], which) for which in (0, 1)]
    for part, turn in ((0, 2), (1, 5)):
        for step in chains[part]:
            (slots[turn] if turn < blocks else left).append(step)
            turn += step is not chains[part][0]

    def back(step, carry):
        block = blocks - 1 - step
        top = pl.multiple_of(block * STRETCH, STRETCH)
        rows = pl.ds(top, STRETCH)
        slot = lax.rem(block, 2)
        for copy in streams(block, slot):
            copy.wait()

        def fetch():
            for copy in streams(block - 1, 1 - slot):
                copy.start()

        pl.when(block > 0)(fetch)
        aux = aux_s[slot]
        aux2, run2, aux_t, run_t = block_scalars(aux)
        doc_window = doc_cols[pl.ds(top, STRETCH + 2 * PAD), :]
        same = same_documents(doc_window[: STRETCH + PAD])
        here = doc_window[PAD : PAD + STRETCH]
        same_next = [doc_window[PAD + o : PAD + o + STRETCH] == here for o in range(1, KW)]
        dbeta_all = jnp.zeros((STRETCH, DK), F32)
        drun_all = jnp.zeros((STRETCH, DK), F32)
        column_sums = jnp.zeros((span, DK), F32)

        def conv_back(kind, head, grad):
            first_col = (0, 2, 3, 4, 5)[kind] * half + head * DK
            cols = slice(head * DK, (head + 1) * DK)
            window = pre_s[slot, :, first_col : first_col + DK]
            kernel = conv_ref[kind, :, cols]
            shifted = [window[PAD:]] + [
                jnp.where(same[o - 1], window[PAD - o : PAD - o + STRETCH], 0.0) for o in range(1, KW)
            ]
            y = shifted[0] * kernel[0:1]
            for o in range(1, KW):
                y = y + shifted[o] * kernel[o : o + 1]
            sigmoid = jax.nn.sigmoid(y)
            act = y * sigmoid
            if kind < 3:
                scale = lax.rsqrt(jnp.sum(act * act, axis=-1, keepdims=True) + 1e-06)
                unit = act * scale
                if kind == 0:
                    grad = grad * DK ** (-0.5)
                grad = scale * (grad - unit * jnp.sum(unit * grad, axis=-1, keepdims=True))
            dy = grad * (sigmoid * (1.0 + y * (1.0 - sigmoid)))
            for o in range(KW):
                dconv_ref[kind, o : o + 1, cols] += jnp.sum(dy * shifted[o], axis=0, keepdims=True)
            at = slice(kind * half + head * DK, kind * half + (head + 1) * DK)
            longer = jnp.concatenate([dy, dy_next[:, at]], axis=0)
            dy_next[:, at] = dy[:PAD]
            dpre = dy * kernel[0:1]
            for o in range(1, KW):
                dpre = dpre + jnp.where(same_next[o - 1], longer[o : o + STRETCH], 0.0) * kernel[o : o + 1]
            work[rows, first_col : first_col + DK] = dpre.astype(BF)

        for head in range(heads):
            cols = slice(head * DK, (head + 1) * DK)
            gate_cols = slice(half + head * DK, half + (head + 1) * DK)
            beta, run_col, run_row, doc_col, doc_row, carried, to_last = head_terms(
                aux, aux2, run2, aux_t, run_t, head, heads
            )
            decay = decay_matrix(run_col, run_row, doc_col, doc_row, p_row, p_col)
            keys = jnp.concatenate([k_s[slot, 0, :, cols], k_s[slot, 1, :, cols]], axis=0)
            queries = q_s[slot, :, cols]
            mixed = mixed_s[slot, :, cols]
            gate = pre_s[slot, PAD:, gate_cols]
            sigmoid = jax.nn.sigmoid(gate)
            silu = gate * sigmoid
            scale = lax.rsqrt(jnp.mean(mixed * mixed, axis=-1, keepdims=True) + 1e-05)
            scaled = mixed * scale
            dgated = dgated_ref[rows, cols]
            part = dgated * scaled
            work[rows, gate_cols] = (
                part * mix_ref[...] * (sigmoid * (1.0 + gate * (1.0 - sigmoid)))
            ).astype(BF)
            dgain_ref[...] += jnp.sum(part * silu, axis=0, keepdims=True)
            dscaled = dgated * mix_ref[...] * silu
            dout = scale * (dscaled - scaled * jnp.mean(dscaled * scaled, axis=-1, keepdims=True))

            state, pseudo = state_s[slot, head], pseudo_s[slot, head]
            dnext = dstate[head]
            dnext_parts, state_parts, pseudo_parts = split(dnext), split(state), split(pseudo)
            dout_parts, q_parts = split(dout), split(queries)
            gram = dot1(keys, keys, NT)
            core = jnp.where(strict, decay * gram, 0.0)
            amat = beta * core
            qdecay = decay[STRETCH:]
            attn = qdecay * dot3(q_parts, keys, NT)
            dattn = dot3(dout_parts, pseudo_parts, NT)
            dqk = split(qdecay * dattn)
            dpseudo = dot3(attn, dout_parts, TN) + to_last * dot3(keys, dnext_parts)
            dtarget = dot3(inv_s[slot, head], dpseudo, TN)
            dtarget_parts = split(dtarget)
            damat = jnp.where(strict, -dot3(dtarget_parts, pseudo_parts, NT), 0.0)
            e_a, e_m = damat * amat, dattn * attn
            dgram = split(beta * decay * damat)
            dbeta = jnp.sum(dtarget * pseudo, axis=-1, keepdims=True) / jnp.maximum(beta, 1e-30)
            dvalues = (beta * dtarget).astype(BF).astype(F32)
            dread = -(beta * carried) * dtarget
            dout_c = carried[STRETCH:] * dout
            dread_parts, dout_c_parts = split(dread), split(dout_c)
            last = carried[span - 1 : span]
            dstate[head] = last * dnext + dot3(keys, dread_parts, TN) + dot3(q_parts, dout_c_parts, TN)
            dq_state = dot3(dout_c_parts, state_parts, NT)
            dk_state = dot3(dread_parts, state_parts, NT)
            dk_last = dot3(to_last * pseudo, dnext_parts, NT)
            conv_back(0, head, dq_state + dot3(dqk, keys))
            dkeys = (
                dk_state + dk_last + dot3(dgram, keys) + dot3(dgram, keys, TN) + dot3(dqk, q_parts, TN)
            ).astype(BF).astype(F32)
            conv_back(1, head, dkeys[:STRETCH])
            conv_back(2, head, dkeys[STRETCH:])
            conv_back(3, head, dvalues[:STRETCH])
            conv_back(4, head, dvalues[STRETCH:])

            wide = keys.astype(F32)
            e_last = jnp.sum(wide * dk_last, axis=-1, keepdims=True)
            drun = jnp.sum(e_a, axis=-1, keepdims=True) - e_last + jnp.sum(wide * dk_state, axis=-1, keepdims=True)
            drun_q = jnp.sum(e_m, axis=-1, keepdims=True) + jnp.sum(queries * dq_state, axis=-1, keepdims=True)
            at_last = jnp.sum(e_last, axis=0, keepdims=True) + last * jnp.sum(
                jnp.sum(dnext * state, axis=-1, keepdims=True), axis=0, keepdims=True
            )
            drun = drun[:STRETCH] + drun[STRETCH:] + drun_q
            drun = drun + jnp.where(iota((STRETCH, 1), 0) == STRETCH - 1, at_last, 0.0)
            lane = 2 * heads + head
            drun_all = jnp.where(lanes == lane, drun, drun_all)
            dbeta_all = jnp.where(lanes == head, dbeta[:STRETCH], dbeta_all)
            dbeta_all = jnp.where(lanes == heads + head, dbeta[STRETCH:], dbeta_all)
            sums = jnp.sum(e_a, axis=0, keepdims=True) + jnp.sum(e_m, axis=0, keepdims=True)
            column_sums = jnp.where(wide_rows == lane, sums, column_sums)
        down = column_sums.T
        ddecay = dot6(upper, drun_all - down[:STRETCH] - down[STRETCH:])
        raw = dot6(pre_s[slot, PAD:, scal_cols], select)
        sigmoid = jax.nn.sigmoid(raw)
        shifted = raw + rates_ref[1:2, :]
        draw_decay = ddecay * rate * jax.nn.sigmoid(shifted)
        is_decay = (lanes >= 2 * heads) & (lanes < 3 * heads)
        draw_decay = jnp.where(is_decay, draw_decay, 0.0)
        dscal_ref[0:1, :] += jnp.sum(
            jnp.where(is_decay, ddecay * rate * softplus(shifted), 0.0), axis=0, keepdims=True
        )
        dscal_ref[1:2, :] += jnp.sum(draw_decay, axis=0, keepdims=True)
        dbeta_low = dbeta_all.astype(BF).astype(F32)
        draw = jnp.where(lanes < 2 * heads, dbeta_low * 2.0 * sigmoid * (1.0 - sigmoid), draw_decay)
        work[rows, scal_cols] = dot6(draw, select, NT).astype(BF)
        run_slot(slots, step)
        return carry

    lax.fori_loop(0, blocks, back, 0)
    mix_swap = remote(dgain_ref, mix_in, m_send.at[2], m_recv.at[2], place.peer)
    mix_swap.start()

    def normalise(index, carry):
        rows = chunk_rows(index)
        x = x_ref[rows, :].astype(F32)
        scale = lax.rsqrt(jnp.mean(x * x, axis=-1, keepdims=True) + 1e-06)
        normed[rows, :] = (x * scale * norm_ref[...]).astype(BF)
        return carry

    lax.fori_loop(0, chunks, normalise, 0)

    def in_sent(index, carry):
        in_copy(index).wait_send()
        return carry

    lax.fori_loop(0, chunks, in_sent, 0)

    def weigh_front(index, carry):
        cols = pl.ds(pl.multiple_of(index * DK, DK), DK)
        put_blocks(w_ref, index, slice(0, front_width), product(normed[:, cols], work[:, 0:front_width], TN))
        return carry

    for part in parts:
        scatter.drain_sibling(part)
    for step in left:
        step()
    lax.fori_loop(0, width // DK, weigh_front, 0)

    def release(stage):
        for part in ((0, 1), (2, 3))[stage]:
            scatter.drain(part)
        sem = free_sem.at[stage]
        for device in (place.sibling, place.across):
            pl.semaphore_signal(sem, inc=1, device_id=device, device_id_type=MESH)
        for way in (0, 1):
            pl.when(place.can_send[way])(
                lambda way=way: pl.semaphore_signal(sem, inc=1, device_id=place.ahead[way], device_id_type=MESH)
            )

    def await_release(stage):
        senders = 2 + place.can_send[0].astype(jnp.int32) + place.can_send[1].astype(jnp.int32)
        pl.semaphore_wait(free_sem.at[stage], senders)

    cuts = [(2 * half, 2 * half), (4 * half, 2 * half + DK), (0, half), (half, half)]
    later = Scatter(place, w_ref, total, cuts, (mid, far, path), sems[8:])
    chains[2][0]()
    chains[2][1]()
    release(0)
    await_release(0)
    later.begin(0)
    later.begin(1)
    load_front.wait()

    def outputs(index, carry):
        rows = chunk_rows(index)
        both = attn_own[rows, :].astype(F32) + attn_in[rows, :].astype(F32)
        out_ref[rows, :] = (middle_ref[rows, :] + both).astype(BF)
        return carry

    def nb_copy(index):
        rows = chunk_rows(index)
        return remote(in_own.at[rows], in_in.at[rows], n_send.at[index], n_recv.at[index], place.peer)

    def project_back(index):
        rows = pair_rows(index)
        in_own[rows, :] = product(work[rows, 0:front_width], flat(fw_ref, 0, front_width), NT).astype(BF)
        nb_copy(2 * index).start()
        nb_copy(2 * index + 1).start()

    swap.wait_recv()
    project_back(0)
    later.merge(0, 0)
    later.merge(0, 1)
    for step in chains[2][2:3]:
        step()
    for index in range(1, chunks // 2):
        project_back(index)
    later.merge(1, 0)
    later.merge(1, 1)
    for step in chains[2][3:-1] + chains[3][:2]:
        step()
    lax.fori_loop(0, chunks, outputs, 0)
    chains[2][-1]()
    for step in chains[3][2:]:
        step()
    release(1)
    await_release(1)
    later.begin(2)
    later.begin(3)
    gnorm_ref[...] = jnp.zeros_like(gnorm_ref)

    def finish_back(index, carry):
        rows = chunk_rows(index)
        nb_copy(index).wait_recv()
        back = in_own[rows, :].astype(F32) + in_in[rows, :].astype(F32)
        x = x_ref[rows, :].astype(F32)
        scale = lax.rsqrt(jnp.mean(x * x, axis=-1, keepdims=True) + 1e-06)
        unit = x * scale
        gnorm_ref[...] += jnp.sum(back * unit, axis=0, keepdims=True)
        back = back * norm_ref[...]
        total_back = back_ref[rows, :] + scale * (back - unit * jnp.mean(unit * back, axis=-1, keepdims=True))
        igrad_ref[rows, :] = total_back.astype(BF)
        return carry

    small_swaps = [
        remote(small, small_in.at[0], m_send.at[0], m_recv.at[0], place.sibling),
        remote(small_sum, small_in.at[1], m_send.at[1], m_recv.at[1], place.across),
    ]

    def line_copy(target):
        device = (target * 4 + place.x * 2 + place.c, side)
        return remote(small_line.at[place.z], small_line.at[place.z], l_send.at[target], l_recv.at[place.z], device)

    def line_from(source):
        device = (source * 4 + place.x * 2 + place.c, side)
        return remote(small_line.at[source], small_line.at[source], l_send.at[source], l_recv.at[source], device)

    def collect():
        mix_swap.wait_recv()
        small[0:5] = dconv_ref[...]
        for i in range(2):
            small[5, i : i + 1, :] = gnorm_ref[:, i * half : (i + 1) * half]
            small[5, 2 + i : 3 + i, :] = gffn_ref[:, i * half : (i + 1) * half]
        small[6] = jnp.zeros((KW, half), F32)
        small[6, 0:1, 0:DK] = dgain_ref[...] + mix_in[...]
        small[6, 0:1, DK : 2 * DK] = dscal_ref[0:1, :]
        small[6, 0:1, 2 * DK : 3 * DK] = dscal_ref[1:2, :]
        small_swaps[0].start()

    def collect_across():
        small_swaps[0].wait_recv()
        small_sum[...] = small[...] + small_in[0]
        small_swaps[1].start()

    def collect_line():
        small_swaps[1].wait_recv()
        small_line[place.z] = small_sum[...] + small_in[1]
        for target in range(line):
            pl.when(target != place.z)(lambda target=target: line_copy(target).start())

    home = [
        remote(
            total.at[:, pl.ds(pl.multiple_of((base + 1 - side) * half, half), half)],
            ref.at[:, pl.ds(pl.multiple_of(side * half, half), half)],
            h_send.at[i], h_recv.at[i], place.peer,
        )
        for i, (base, ref) in enumerate(((2, gk_ref), (4, gv_ref)))
    ]
    scal_home = remote(total.at[:, scal_at : scal_at + DK], scal_in, h_send.at[2], h_recv.at[2], place.peer)
    own_half = pl.ds(pl.multiple_of(side * half, half), half)

    def at_home(i):
        base, ref = ((2, gk_ref), (4, gv_ref))[i]
        home[i].start()
        ref[:, own_half] = total[:, pl.ds(pl.multiple_of((base + side) * half, half), half)]

    def at_home_value():
        at_home(1)
        scal_home.start()

    after = [later.stages(part) for part in range(4)]
    homes = [functools.partial(at_home, 0), at_home_value]
    merge = functools.partial
    slots = [
        [merge(later.merge, 2, 0), merge(later.merge, 2, 1)],
        [merge(later.merge, 3, 0), merge(later.merge, 3, 1)],
        after[0][:2],
        after[0][2:3],
    ]

    def finish_and(index, carry):
        finish_back(index, carry)
        run_slot(slots, index)
        return carry

    lax.fori_loop(0, chunks, finish_and, 0)
    rest = after[0][3:-1] + after[1][:2] + after[0][-1:] + homes[:1] + after[1][2:-1] + after[2][:2] + after[1][-1:]
    rest += homes[1:] + after[3][:2]
    for pair in zip(after[2][2:], after[3][2:]):
        rest += pair
    extra = [collect, collect_across, collect_line]
    for i, step in enumerate(rest):
        if i % 2 == 0 and extra:
            extra.pop(0)()
        step()
    for step in extra:
        step()
    for source in range(line):
        pl.when(source != place.z)(lambda source=source: line_from(source).wait_recv())
    summed = small_line[0]
    for source in range(1, line):
        summed = summed + small_line[source]
    small_sum_out = summed
    gcq_ref[...] = small_sum_out[0]
    small_swaps[0].wait_send()
    small_swaps[1].wait_send()
    small[...] = small_sum_out
    conv_home = [
        remote(
            small.at[base + 1 - side], ref.at[:, own_half], h_send.at[i], h_recv.at[i], place.peer
        )
        for i, (base, ref) in ((3, (1, gck_ref)), (4, (3, gcv_ref)))
    ]
    for copy in conv_home:
        copy.start()
    gck_ref[:, own_half] = small[1 + side]
    gcv_ref[:, own_half] = small[3 + side]
    for i in range(2):
        gnorm_ref[:, i * half : (i + 1) * half] = small_sum_out[5, i : i + 1]
        gffn_ref[:, i * half : (i + 1) * half] = small_sum_out[5, 2 + i : 3 + i]
    gtiny_ref[...] = small_sum_out[6, 0:1, 0 : 3 * DK]
    gq_ref[...] = total[:, 0:half]
    gg_ref[...] = total[:, half : 2 * half]
    scal_home.wait_recv()
    lanes = iota(scal_in.shape, 1)
    ours = total[:, scal_at : scal_at + DK]
    theirs = pltpu.roll(scal_in[...], DK - 2 * heads, 1)
    gs_ref[...] = jnp.where(lanes < 2 * heads, ours + theirs, ours)
    for copy in home + conv_home:
        copy.wait_recv()
    for copy in home + conv_home + [scal_home, mix_swap]:
        copy.wait_send()
    for target in range(line):
        pl.when(target != place.z)(lambda target=target: line_copy(target).wait_send())

    def sent(index, carry):
        nb_copy(index).wait_send()
        return carry

    lax.fori_loop(0, chunks, sent, 0)
    for part in range(4):
        later.drain_sibling(part)
        later.drain(part)
    swap.wait_send()


def rest_call(line, gated, x, cot, middle, domains, gain, norm, docs, conv, rates, mix, w, fw, pre, q, k, v, aux, mixed, inv, state, pseudo):
    seq, width = x.shape
    half = gated.shape[1]
    heads = half // DK
    depth, tail = w.shape[3:]
    columns = fw.shape[-1]
    ff = (tail - half) // 3
    shape = jax.ShapeDtypeStruct
    dma = pltpu.SemaphoreType.DMA
    chunks = seq // CHUNK
    span = 2 * STRETCH
    tiny = (7, KW, half)
    low = pltpu.VMEM((seq, width), BF)
    wide = pltpu.VMEM((seq, width), F32)
    return pl.pallas_call(
        functools.partial(rest_kernel, line, heads),
        out_shape=(
            shape((seq, width), BF),
            shape((seq, width), BF),
            shape((depth, tail), F32),
            shape((depth, half), F32),
            shape((depth, half), F32),
            shape((depth, 2 * half), F32),
            shape((depth, 2 * half), F32),
            shape((depth, DK), F32),
            shape((KW, half), F32),
            shape((KW, 2 * half), F32),
            shape((KW, 2 * half), F32),
            shape((1, width), F32),
            shape((1, width), F32),
            shape((1, 3 * DK), F32),
        ),
        in_specs=[VMEM] * 11 + [pl.BlockSpec(memory_space=pl.ANY)] * 11,
        out_specs=(VMEM,) * 14,
        scratch_shapes=[
            pltpu.VMEM(w.shape, BF),
            pltpu.VMEM(fw.shape, BF),
        ]
        + [low] * 6
        + [pltpu.VMEM((seq, 3 * ff), BF), wide, pltpu.VMEM((seq, half), F32)]
        + [
            pltpu.VMEM((heads, DK, DK), F32),
            pltpu.VMEM((seq + 2 * PAD, DK), F32),
            pltpu.VMEM((PAD, 5 * half), F32),
            pltpu.VMEM((5, KW, half), F32),
            pltpu.VMEM((2, DK), F32),
            pltpu.VMEM((1, DK), F32),
            pltpu.VMEM((depth, columns), F32),
        ]
        + scatter_scratch(line, depth, tail, False)
        + [
            pltpu.VMEM((2, STRETCH + PAD, columns), F32),
            pltpu.VMEM((2, STRETCH, half), F32),
            pltpu.VMEM((2, 2, STRETCH, half), BF),
            pltpu.VMEM((2, 2, STRETCH, half), BF),
            pltpu.VMEM((2, STRETCH, DK), F32),
            pltpu.VMEM((2, STRETCH, half), F32),
            pltpu.VMEM((2, heads, span, span), F32),
            pltpu.VMEM((2, heads, DK, DK), F32),
            pltpu.VMEM((2, heads, span, DK), F32),
        ]
        + [
            pltpu.VMEM(tiny, F32),
            pltpu.VMEM((2,) + tiny, F32),
            pltpu.VMEM((line,) + tiny, F32),
            pltpu.VMEM(tiny, F32),
            pltpu.VMEM((1, DK), F32),
            pltpu.VMEM((depth, DK), F32),
        ]
        + [dma((4,)), dma((2, 9))]
        + [dma((chunks,))] * 2
        + [dma, dma]
        + [dma((chunks,)), dma((chunks,)), dma((5,)), dma((5,)), dma((3,)), dma((3,)), dma((line,)), dma((line,))]
        + [pltpu.SemaphoreType.REGULAR((2,))]
        + scatter_sems(line, 4)
        + scatter_sems(line, 4),
        compiler_params=pltpu.CompilerParams(
            collective_id=1, has_side_effects=True, vmem_limit_bytes=63 << 20
        ),
        name="rest",
    )(gated, x, cot, middle, domains, gain, norm, docs, conv, rates, mix, w, fw, pre, q, k, v, aux, mixed, inv, state, pseudo)


def deliver_kernel(heads, *refs):
    count = (len(refs) - 21) // 2
    sources, outs, held, sems = refs[:count], refs[count : count + 20], refs[count + 20 : -1], refs[-1]
    copies = [pltpu.make_async_copy(src, dst, sems.at[i]) for i, (src, dst) in enumerate(zip(sources, held))]
    for copy in copies:
        copy.start()
    (
        out_ref, igrad_ref, sum_ref, gq_ref, gg_ref, gk_ref, gv_ref, gs_ref, gcq_ref, gck_ref, gcv_ref, gnorm_ref,
        gffn_ref, gtiny_ref,
    ) = held
    (
        output, input_grad, norm, query, outgate, key, value, beta, alpha, log, bias, c_query, c_key, c_value, mix,
        w_out, ffn, gate, up, down,
    ) = outs
    for copy in copies:
        copy.wait()
    output[0] = out_ref[...]
    input_grad[0] = igrad_ref[...]
    norm[...] = gnorm_ref[...]
    ffn[...] = gffn_ref[...]
    query[...] = gq_ref[...]
    outgate[...] = gg_ref[...]
    key[0] = gk_ref[...]
    value[0] = gv_ref[...]
    depth, half = query.shape
    ff = gate.shape[1]
    corner = (iota((depth, depth), 0) == iota((depth, depth), 1)).astype(F32)
    turned = dot6(gs_ref[...], corner, TN)
    beta[...] = turned[0 : 2 * heads]
    alpha[...] = turned[4 * heads : 5 * heads]
    here = slice(2 * heads, 3 * heads)
    log[...] = gtiny_ref[:, DK : 2 * DK][:, here]
    bias[...] = gtiny_ref[:, 2 * DK :][:, here]
    mix[...] = gtiny_ref[:, 0:DK]
    c_query[...] = gcq_ref[...]
    c_key[0] = gck_ref[...]
    c_value[0] = gcv_ref[...]
    w_out[...] = sum_ref[:, 0:half]
    gate[...] = sum_ref[:, half : half + ff]
    up[...] = sum_ref[:, half + ff : half + 2 * ff]
    down[...] = sum_ref[:, half + 2 * ff :]


def deliver_call(heads, *parts):
    seq, width = parts[0].shape
    depth, tail = parts[2].shape
    half = parts[3].shape[1]
    ff = (tail - half) // 3
    shape = lambda *dims: jax.ShapeDtypeStruct(dims, F32)
    low = jax.ShapeDtypeStruct((1, seq, width), BF)
    return pl.pallas_call(
        functools.partial(deliver_kernel, heads),
        out_shape=(
            low, low, shape(1, width), shape(depth, half), shape(depth, half), shape(1, depth, 2 * half),
            shape(1, depth, 2 * half), shape(2 * heads, depth), shape(heads, depth), shape(1, heads),
            shape(1, heads), shape(KW, half), shape(1, KW, 2 * half), shape(1, KW, 2 * half), shape(1, DK),
            shape(depth, half), shape(1, width), shape(depth, ff), shape(depth, ff), shape(depth, ff),
        ),
        in_specs=[pl.BlockSpec(memory_space=pl.ANY)] * 14,
        out_specs=(VMEM,) * 20,
        scratch_shapes=[pltpu.VMEM(part.shape, part.dtype) for part in parts]
        + [pltpu.SemaphoreType.DMA((len(parts),))],
        compiler_params=pltpu.CompilerParams(vmem_limit_bytes=63 << 20),
        name="deliver",
    )(*parts)


GROUPS = 8


def per_device(
    tokens,
    cotangent,
    domains,
    doc_ids,
    norm_gain,
    w_query,
    w_outgate,
    w_key,
    w_value,
    w_beta,
    w_alpha,
    decay_log,
    decay_bias,
    conv_query,
    conv_key,
    conv_value,
    mix_gain,
    w_out,
    ffn_gain,
    w_gate,
    w_up,
    w_down,
):
    line = lax.axis_size("dp") // 4
    by_place = lambda array: array.reshape((line, 2, 2) + array.shape[1:])
    gain_row = mix_gain[None]
    (
        gated, middle, conv, rates, mixed, inv, state, pseudo, pre, queries, keys, values, aux, front_w, back_w
    ) = front_call(
        line, tokens[0], doc_ids, norm_gain[None], w_query, w_outgate, w_key[0], w_value[0], w_beta[0].T, w_alpha.T,
        w_out.T, w_gate, w_up, w_down.T, decay_log[None], decay_bias[None], conv_query, conv_key[0], conv_value[0],
        gain_row,
    )
    parts = rest_call(
        line, gated, tokens[0], cotangent[0], middle, domains[None], ffn_gain[None], norm_gain[None], doc_ids, conv,
        rates, gain_row, by_place(back_w), by_place(front_w), pre, queries, keys, values, aux, mixed, inv, state,
        pseudo,
    )
    results = list(deliver_call(w_alpha.shape[1], *parts))
    for index in (2, 9, 10, 14, 16):
        results[index] = results[index][0]
    for index in (8, 15, 19):
        results[index] = results[index].T
    results[7] = results[7].T[None]
    return tuple(results)


def solution(mesh):
    return jax.shard_map(
        per_device,
        mesh=mesh,
        in_specs=(
            P("dp", None, None),
            P("dp", None, None),
            P(),
            P("dp", None),
            P(),
            P("dp", "step"),
            P("dp", "step"),
            P("step", "dp", None),
            P("step", "dp", None),
            P("step", "dp", None),
            P("dp", "step"),
            P("step"),
            P("step"),
            P(None, "step"),
            P("step", None, None),
            P("step", None, None),
            P(),
            P("step", "dp"),
            P(),
            P("dp", "step"),
            P("dp", "step"),
            P("step", "dp"),
        ),
        out_specs=(
            P("dp", None, None),
            P("dp", None, None),
            P(),
            P("dp", "step"),
            P("dp", "step"),
            P("step", "dp", None),
            P("step", "dp", None),
            P("step", "dp", None),
            P("dp", "step"),
            P("step"),
            P("step"),
            P(None, "step"),
            P("step", None, None),
            P("step", None, None),
            P(),
            P("step", "dp"),
            P(),
            P("dp", "step"),
            P("dp", "step"),
            P("step", "dp"),
        ),
        check_vma=False,
    )
```

time: 651 us -> 307 us (0.47); the launches traced: 643 us -> 307 us
  waiting for transfers between devices: 165 us -> 0 us
  Pallas kernels: 168 us -> 306 us
  blocking collectives: 102 us -> 0 us
  other arithmetic: 75.2 us -> 0 us
  matrix products: 62.7 us -> 0 us
  local copies, waits for them, and re-layouts: 47.9 us -> 0 us
  between operations: 15.4 us -> 0.86 us
    pallas_call x1 -> x2, Pallas kernels: 50.5 us -> 180 us  [the longest x1 176 us: rest_call(): pl.pallas_call(functools.partial(rest_kernel, line, heads), out_shape=(sh...]
    reduce_scatter x2 -> x0, waiting for transfers between devices: 111 us -> none  [the longest x1 104 us: per_device(): lax.psum_scatter(jnp.concatenate([grad_out, grad_gate, grad_up, grad_down...]
    psum x2 -> x0, blocking collectives: 102 us -> none  [the longest x1 62.1 us: per_device(): lax.psum((grad_norm_gain, d_log, d_bias, d_cq, d_k0, d_k1, d_v0, d_v1, gr...]
    dot_general x16 -> x0, matrix products: 62.7 us -> none  [the longest x14 61.3 us: product(): lax.dot_general(first, second, (dims, ((), ())), preferred_element_type=F32)]
    psum x3 -> x0, waiting for transfers between devices: 52.5 us -> none  [the longest x1 27.1 us: per_device(): lax.psum(product(gated, back_w[:, :half], NT).astype(BF), 'step')]
    reduce_sum x13 -> x0, other arithmetic: 33.6 us -> none  [the longest x1 9.84 us: short_conv(): summed = summed + shifted * same_doc * kernel[offset]]
    concatenate x6 -> x0, other arithmetic: 13.6 us -> none  [the longest x1 9.17 us: per_device(): jnp.concatenate([grad_out, grad_gate, grad_up, grad_down], axis=1)]
    mul x8 -> x0, local copies, waits for them, and re-layouts: 10.4 us -> none  [the longest x4 5.31 us: unit_rows(): values * lax.rsqrt(jnp.sum(values * values, axis=-1, keepdims=True) + 1e-06)]
  transfers between devices with their start and end apart: 10 -> 0, of which waited for: 5 -> 0; matrix products, arithmetic and copies ran while one was open for 13% -> 0% of each run, Pallas kernels for 0% -> 0%
where the time goes in v4:
time: 307 us
  Pallas kernels  306 us (100%)
    pallas_call x1, Pallas kernels, rest_call(): pl.pallas_call(functools.partial(rest_kernel, line, heads), out_shape=(sh...  176 us
    pallas_call x1, Pallas kernels, front_call(): pl.pallas_call(functools.partial(front_kernel, line, heads), out_shape=(s...  126 us

profile of v4, /device:TPU:0, one launch (start us, length us, event | category | flops | bytes accessed | tf_op | source)
XLA Modules:
  0.0 306.6 jit_solution(16217528614752598369)
XLA Ops:
  0.7 125.6 %front.1 = (bf16[512,512]{1,0:T(8,128)(2,1)}, f32[512,1024]{1,0:T(8,128)}, f32[5,4,512]{2,1,0:T(4,128)}, f32[2,128]{1,0:T(2,128)}, f32[512,512]{1,0:T(8,128)}, /...) custom-call(bf16[512,1024]{1,0:T(8,128)(2,1)} %bitcast.33, ...), custom_call_target="tpu_custom_call" | custom-call | tf_op jit(solution)/shard_map/front/pallas_call | solution.py:760
  126.2 175.7 %rest.1 = (bf16[512,1024]{1,0:T(8,128)(2,1)}, bf16[512,1024]{1,0:T(8,128)(2,1)}, f32[64,4736]{1,0:T(8,128)}, f32[64,512]{1,0:T(8,128)}, f32[64,512]{1,0:T(8,128)...) custom-call(bf16[512,512]{1,0:T(8,128)(2,1)} %get-tuple-element.69.g, ...), custom_call_target="tpu_custom_call" | custom-call | tf_op jit(solution)/shard_map/rest/pallas_call | solution.py:1410
  301.9 4.5 %deliver.1 = (bf16[1,512,1024]{2,1,0:T(8,128)(2,1)}, bf16[1,512,1024]{2,1,0:T(8,128)(2,1)}, f32[1,1024]{1,0:T(1,128)}, f32[64,512]{1,0:T(8,128)}, f32[64,512]{1,...) custom-call(bf16[512,1024]{1,0:T(8,128)(2,1)} %get-tuple-element.84., ...), custom_call_target="tpu_custom_call" | custom-call | tf_op jit(solution)/shard_map/deliver/pallas_call | solution.py:1529
